TPU v7x, 768 devices: a whole 4x8x12 slice. The times are simulated.
768 devices in a mesh: col: 96 (over x, z, core), node: 8 (over y).
Axes of the slice: x: 4, y: 8, z: 12, core: 2. Of those that a mesh axis runs over, the one named last changes fastest.
Arguments:
- features: bfloat16 [768, 98304], P('col', 'node'), may hold values from -6 to 6
- w_one: bfloat16 [2, 768, 1024], P(None, 'col'), may hold values from -0.15625 to 0.15625
- adj_one: bfloat16 [96, 8, 128, 128], P('node'), may hold values from -0.1875 to 0.1875
- list_one: int32 [96, 8], P('node'), may hold values from 0 to 95
- adj_two: bfloat16 [12288, 4, 128], P(('node', 'col')), may hold values from -0.25 to 0.25
- list_two: int32 [96, 4], P('node'), may hold values from 0 to 11, as said below
- w_two: bfloat16 [2, 1024, 153], replicated, may hold values from -0.1875 to 0.1875
- cotangent: bfloat16 [12288, 153], P(('node', 'col')), may hold values from -6 to 6
Outputs:
- hidden: bfloat16 [12288, 1024], P(('node', 'col'))
- logits: float32 [12288, 153], P(('node', 'col'))
- neighbor_grad: float32 [1024, 153], replicated
Inputs may be any that keep to these rules, and one draw needn't show every extreme that they name: `list_two`: each row names 4 different blocks.
All inputs are finite; a program needn't handle non-finite values.
Results may differ from a plain program's by a relative error of at most 0.0054.
Values may be sent and summed in bfloat16 or wider, within the bound.
No kernel may reach another device: no remote copies, remote signals or barrier semaphores. Data moves between devices by JAX's collectives and lax.ppermute only.
A program may use at most 32 MiB of HBM per device.

v0:
```python
import jax
import jax.numpy as jnp
from jax import lax
from jax.sharding import PartitionSpec as P


def per_device(features, w_one, adj_one, list_one, adj_two, list_two, w_two, cotangent):
    cols, sources = features.shape
    blocks_here, fanout = list_one.shape
    block = adj_one.shape[-1]
    frontier = blocks_here * block
    mine = adj_two.shape[0]
    tiles = features.reshape(cols, sources // block, block)
    chosen_nodes = jnp.take(tiles, list_one, axis=1)
    first_aggregate = jnp.einsum(
        "fhks,hkts->fht", chosen_nodes, adj_one, preferred_element_type=jnp.float32
    )
    first_aggregate = first_aggregate.astype(jnp.bfloat16).reshape(cols, frontier)
    inputs = jnp.stack([first_aggregate, features[:, :frontier]])
    part = inputs
    pre = lax.psum_scatter(
        jnp.einsum("ifr,ifh->rh", part, w_one, preferred_element_type=jnp.float32),
        "col",
        scatter_dimension=0,
        tiled=True,
    )
    hidden = jnp.maximum(pre, 0.0).astype(jnp.bfloat16)
    row_ids = lax.axis_index("col") * mine + jnp.arange(mine, dtype=jnp.int32)
    row_block = row_ids // block
    block_ids = jnp.arange(blocks_here, dtype=jnp.int32)
    select = (row_block[:, None] == block_ids[None, :]).astype(jnp.int32)
    row_lists = jnp.sum(select[:, :, None] * list_two[None, :, :], axis=1)
    match = (row_lists[:, :, None] == block_ids[None, None, :]).astype(jnp.float32)
    dense = jnp.einsum("rkj,rks->rjs", match, adj_two.astype(jnp.float32))
    dense = dense.astype(jnp.bfloat16).reshape(mine, frontier)
    part = dense
    second_aggregate = jnp.dot(
        part, lax.all_gather(hidden, "col", axis=0, tiled=True), preferred_element_type=jnp.float32
    )
    second_aggregate = second_aggregate.astype(jnp.bfloat16)
    logits = jnp.dot(second_aggregate, w_two[0], preferred_element_type=jnp.float32) + jnp.dot(
        hidden, w_two[1], preferred_element_type=jnp.float32
    )
    grad_term = jnp.dot(second_aggregate.T, cotangent, preferred_element_type=jnp.float32)
    neighbor_grad = lax.psum(grad_term, ("col", "node"))
    return (hidden, logits, neighbor_grad)


def solution(mesh):
    in_specs = (
        P("col", "node"),
        P(None, "col", None),
        P("node", None, None, None),
        P("node", None),
        P(("node", "col"), None, None),
        P("node", None),
        P(),
        P(("node", "col"), None),
    )
    out_specs = (P(("node", "col"), None), P(("node", "col"), None), P())
    return jax.shard_map(
        per_device, mesh=mesh, in_specs=in_specs, out_specs=out_specs, check_vma=False
    )
```

profile of v0, /device:TPU:1, one launch (start us, length us, event | category | flops | bytes accessed | tf_op | source)
XLA Modules:
  0.0 839.0 jit_solution(4699109725897517934)
XLA Ops:
  7.2 0.0 copy-start
  7.2 0.0 copy-start.2
  7.2 0.0 reduce-scatter.2.cloned.1.call-start
  7.2 0.8 compare_select_fusion
  8.1 0.8 compare_and_fusion
  8.8 0.1 copy.20
  8.9 0.1 reshape.63
  9.0 0.1 copy.19
  9.1 0.7 slice_bitcast_fusion
  9.9 1.6 gather_fusion
  11.4 0.0 copy-done
  11.5 1.0 fusion.1
  12.4 0.0 copy-done.2
  12.4 3.7 convolution_bitcast_fusion
  16.1 0.0 copy-start.4
  16.1 0.0 copy-start.5
  16.1 0.0 reduce-scatter.2.cloned.1.call-update
  16.1 0.0 copy-start.3
  16.2 0.0 all-gather.2.cloned.1.call-start
  16.2 216.5 %reduce-scatter.2.cloned.1.call-done = f32[16,1024]{1,0:T(8,128)} async-done(((f32[1536,1024]{1,0:T(8,128)}), f32[16,1024]{1,0:T(8,128)}) %reduce-scatter.2.cloned.1.call-update) | async-done | bytes 65552 | tf_op jit(solution)/shard_map/reduce_scatter | solution.py:21
  232.7 1.5 maximum_convert_fusion
  234.1 0.0 all-gather.2.cloned.1.call-update
  234.2 0.0 all-reduce.2.cloned.1.call-start
  234.2 0.0 copy-done.4
  234.2 0.1 copy.21
  234.3 0.1 multiply_reduce_fusion
  234.4 0.1 copy.22
  234.5 0.0 copy-done.5
  234.5 0.3 convolution_convert_fusion
  234.8 0.0 copy-start.1
  234.8 3.4 fusion.16
  238.3 122.4 %all-gather.2.cloned.1.call-done = bf16[1536,1024]{1,0:T(8,128)(2,1)} async-done(((bf16[16,1024]{1,0:T(8,128)(2,1)}), bf16[1536,1024]{1,0:T(8,128)(2,1)}) %all-gather.2.cloned.1.call-update) | async-done | bytes 3145744 | tf_op jit(solution)/shard_map/all_gather | solution.py:38
  360.7 2.4 convolution_convert_fusion.1
  363.1 0.0 copy-done.3
  363.1 1.1 fusion.17
  364.2 0.0 all-reduce.2.cloned.1.call-update
  364.2 1.3 fusion.2
  365.5 0.0 copy-done.1
  365.5 1.9 convolution_add_fusion
  367.4 463.1 %all-reduce.2.cloned.1.call-done = f32[1024,153]{0,1:T(8,128)} async-done(((f32[1024,153]{0,1:T(8,128)}), f32[1024,153]{0,1:T(8,128)}) %all-reduce.2.cloned.1.call-update) | async-done | bytes 626704 | tf_op jit(solution)/shard_map/psum | solution.py:45
  830.5 2.0 copy.38
  (3 shorter events, 0.0 us)
Async XLA Ops:
  7.2 4.3 copy-start
  7.2 5.2 copy-start.2
  7.2 225.5 %reduce-scatter.2.cloned.1.call-start = ((), (), s32[]{:S(2)}) async-start(), calls=%async_computation.1 | async-start | bytes 6356992 | tf_op jit(solution)/shard_map/reduce_scatter | solution.py:21
  16.1 218.1 %copy-start.4 = (s32[12,4]{0,1:T(4,128)S(1)}, s32[12,4]{0,1:T(4,128)}, u32[]{:S(2)}) copy-start(s32[12,4]{0,1:T(4,128)} %param.13) | copy-start | bytes 580
  16.1 218.4 %copy-start.5 = (bf16[16,4,128]{2,1,0:T(4,128)(2,1)S(1)}, bf16[16,4,128]{2,1,0:T(4,128)(2,1)}, u32[]{:S(2)}) copy-start(bf16[16,4,128]{2,1,0:T(4,128)(2,1)} %param.12) | copy-start | bytes 49156
  16.1 346.9 %copy-start.3 = (bf16[16,153]{1,0:T(8,128)(2,1)S(1)}, bf16[16,153]{1,0:T(8,128)(2,1)}, u32[]{:S(2)}) copy-start(bf16[16,153]{1,0:T(8,128)(2,1)} %param.15) | copy-start | bytes 14692
  16.2 344.5 %all-gather.2.cloned.1.call-start = ((), (), s32[]{:S(2)}) async-start(), calls=%async_computation.2 | async-start | bytes 3178496 | tf_op jit(solution)/shard_map/all_gather | solution.py:38
  234.2 596.4 %all-reduce.2.cloned.1.call-start = ((), (), s32[]{:S(2)}) async-start(), calls=%async_computation.3 | async-start | bytes 1310720 | tf_op jit(solution)/shard_map/psum | solution.py:45
  234.8 130.7 %copy-start.1 = (bf16[16,1024]{1,0:T(8,128)(2,1)S(1)}, bf16[16,1024]{1,0:T(8,128)(2,1)}, u32[]{:S(2)}) copy-start(bf16[16,1024]{1,0:T(8,128)(2,1)} %maximum_convert_fusion) | copy-start | bytes 98308
Sparse Core Ops, SparseCore 0:
  16.3 216.3 reduce-scatter.1
  237.5 123.1 all-gather.1
  367.5 462.9 all-reduce.1
where the time goes:
time: 839 us
  waiting for transfers between devices  802 us (96%)
  between operations  13.8 us (2%)
  matrix products  11.7 us (1%)
    psum x1, waiting for transfers between devices, per_device(): neighbor_grad = lax.psum(grad_term, ('col', 'node'))  463 us
    reduce_scatter x1, waiting for transfers between devices, per_device(): lax.psum_scatter(jnp.einsum('ifr,ifh->rh', part, w_one, preferred_element...  216 us
    all_gather x1, waiting for transfers between devices, per_device(): lax.all_gather(hidden, 'col', axis=0, tiled=True)  122 us
  transfers between devices with their start and end apart: 3, of which 3 were waited for; matrix products, arithmetic and copies ran while one was open for 1% of the time, Pallas kernels for 0%

commit v1 on v0

v1 whole, which is shorter than its diff:
```python
import jax
import jax.numpy as jnp
from jax import lax
from jax.sharding import Mesh, PartitionSpec as P

F32, BF16 = jnp.float32, jnp.bfloat16


def exchange(parts, axis):
    return lax.all_to_all(parts, axis, 0, 0, tiled=True)


def to_all(part, axis, size):
    return exchange(jnp.broadcast_to(part[None], (size, *part.shape)), axis)


def per_device(features, w_one, adj_one, list_one, adj_two, list_two, w_two, cotangent):
    cols, sources = features.shape
    blocks, fanout = list_one.shape
    block = adj_one.shape[-1]
    mine = adj_two.shape[0]
    lanes = block // mine
    hid = w_one.shape[-1]
    nodes = lax.axis_size("node")
    wide = hid // lanes
    cls = cotangent.shape[-1]
    share = -(-cls // blocks)

    tiles = features.reshape(cols, sources // block, block)
    chosen = jnp.take(tiles, list_one, axis=1)
    agg = jnp.einsum("fhks,hkts->hft", chosen, adj_one, preferred_element_type=F32)
    own = tiles[:, :blocks].transpose(1, 0, 2)
    inputs = jnp.concatenate([agg.astype(BF16), own], axis=1)
    weights = jnp.broadcast_to(w_one.reshape(1, 2 * cols, hid), (blocks, 2 * cols, hid))
    got = exchange(jnp.concatenate([inputs, weights], axis=2), "block")
    got = got.reshape(blocks * 2 * cols, block + hid)
    part = jnp.einsum(
        "kr,kjh->jrh",
        got[:, :block],
        got[:, block:].reshape(-1, lanes, wide),
        preferred_element_type=F32,
    ).astype(BF16)
    edges = adj_two.reshape(mine * adj_two.shape[1], block)
    cot = jnp.pad(cotangent, ((0, 0), (0, 2 * block - cls))).reshape(2 * mine, block)
    extra = jnp.concatenate([edges, cot], axis=0)
    extra = jnp.broadcast_to(extra[None], (lanes, *extra.shape))
    got = exchange(jnp.concatenate([part, extra], axis=1), "lane")
    pre = jnp.sum(got[:, :block].astype(F32), axis=0)
    hidden = jnp.maximum(pre, 0.0).astype(BF16)
    edges = got[:, block : block + edges.shape[0]].reshape(block, -1, block)
    cot = got[:, block + edges.shape[1] * mine :].reshape(block, 2 * block)

    every = to_all(hidden, "block", blocks)
    listed = lax.dynamic_index_in_dim(list_two, lax.axis_index("block"), 0, keepdims=False)
    near = jnp.take(every, listed, axis=0)
    second = jnp.einsum("rks,ksh->rh", edges, near, preferred_element_type=F32).astype(BF16)
    grad = jnp.einsum("rc,rh->ch", cot, second, preferred_element_type=F32)
    grad = grad[: blocks * share].reshape(blocks, share, wide).astype(BF16)
    grad = jnp.sum(exchange(grad, "block").astype(F32), axis=0)
    grad = jnp.sum(to_all(grad, "node", nodes), axis=0).astype(BF16)
    grad = to_all(grad, "block", blocks).reshape(blocks * share, wide)

    rows = jnp.stack([second, hidden]).reshape(2, lanes, mine, wide)
    rows = rows.transpose(1, 0, 2, 3).reshape(lanes, 2 * mine, wide)
    grad = jnp.broadcast_to(grad[None], (lanes, *grad.shape))
    got = exchange(jnp.concatenate([rows, grad], axis=1), "lane")
    both = got[:, : 2 * mine].reshape(lanes, 2, mine, wide).transpose(2, 1, 0, 3)
    both = both.reshape(mine, 2, hid)
    logits = jnp.einsum("rih,ihc->rc", both, w_two, preferred_element_type=F32)
    grad = got[:, 2 * mine : 2 * mine + cls].transpose(0, 2, 1).reshape(hid, cls).astype(F32)
    return both[:, 1], logits, grad


def solution(mesh):
    cols, nodes = mesh.devices.shape
    lanes = 8
    fine = Mesh(mesh.devices.reshape(cols // lanes, lanes, nodes), ("block", "lane", "node"))
    col = ("block", "lane")
    rows = ("node", "block", "lane")
    in_specs = (
        P(col, "node"),
        P(None, col, None),
        P("node", None, None, None),
        P("node", None),
        P(rows, None, None),
        P("node", None),
        P(),
        P(rows, None),
    )
    out_specs = (P(rows, None), P(rows, None), P())
    return jax.shard_map(
        per_device, mesh=fine, in_specs=in_specs, out_specs=out_specs, check_vma=False
    )
```

time: 839 us -> 163 us (0.19)
  waiting for transfers between devices: 802 us -> 40.5 us
  blocking collectives: 0 us -> 69.4 us
  starting transfers between devices: 0.12 us -> 24.8 us
  between operations: 13.8 us -> 0.91 us
    psum x1 -> x0, waiting for transfers between devices: 463 us -> none  [per_device(): neighbor_grad = lax.psum(grad_term, ('col', 'node'))]
    reduce_scatter x1 -> x0, waiting for transfers between devices: 216 us -> none  [per_device(): lax.psum_scatter(jnp.einsum('ifr,ifh->rh', part, w_one, preferred_element...]
    all_gather x1 -> x0, waiting for transfers between devices: 122 us -> none  [per_device(): lax.all_gather(hidden, 'col', axis=0, tiled=True)]
    all_to_all x0 -> x4, blocking collectives: none -> 69.4 us  [exchange(): return lax.all_to_all(parts, axis, 0, 0, tiled=True)]
    all_to_all x0 -> x3, waiting for transfers between devices: none -> 40.5 us  [exchange(): return lax.all_to_all(parts, axis, 0, 0, tiled=True)]
    all_to_all x0 -> x3, starting transfers between devices: none -> 24.8 us  [exchange(): return lax.all_to_all(parts, axis, 0, 0, tiled=True)]
  transfers between devices with their start and end apart: 3 -> 3, of which waited for: 3 -> 3; matrix products, arithmetic and copies ran while one was open for 1% -> 3% of each run, Pallas kernels for 0% -> 0%
where the time goes in v1:
time: 163 us; the launch traced here: 162 us
  blocking collectives  69.4 us (43%)
  waiting for transfers between devices  40.5 us (25%)
  starting transfers between devices  24.8 us (15%)
  local copies, waits for them, and re-layouts  16.4 us (10%)
  matrix products  6.47 us (4%)
  other arithmetic  3.46 us (2%)
    all_to_all x4, blocking collectives, exchange(): return lax.all_to_all(parts, axis, 0, 0, tiled=True)  69.4 us
    all_to_all x3, waiting for transfers between devices, exchange(): return lax.all_to_all(parts, axis, 0, 0, tiled=True)  40.5 us
    all_to_all x3, starting transfers between devices, exchange(): return lax.all_to_all(parts, axis, 0, 0, tiled=True)  24.8 us
  transfers between devices with their start and end apart: 3, of which 3 were waited for; matrix products, arithmetic and copies ran while one was open for 3% of the time, Pallas kernels for 0%

profile of v1, /device:TPU:1, one launch (start us, length us, event | category | flops | bytes accessed | tf_op | source)
XLA Modules:
  0.0 162.0 jit_solution(14556066298112639953)
XLA Ops:
  0.6 0.0 copy-start
  0.6 0.0 copy-start.3
  0.7 0.0 copy-start.5
  0.7 0.0 copy-start.4
  0.7 0.8 compare_and_fusion
  1.5 0.8 compare_select_fusion
  2.3 0.1 copy.46
  2.4 0.1 copy.47
  2.5 0.1 reshape.125
  2.6 0.7 slice_bitcast_fusion.4
  3.4 1.6 gather_fusion
  4.9 0.0 copy-done
  5.0 1.0 fusion.2
  5.9 0.0 copy-done.3
  6.0 0.0 copy-start.6
  6.0 0.8 pad_maximum_fusion.1
  6.8 17.0 %all-to-all-start = ((bf16[12,16,1152]{2,1,0:T(8,128)(2,1)}), bf16[12,16,1152]{2,1,0:T(8,128)(2,1)}, u32[]{:S(2)}, u32[]{:S(2)}) async-start(bf16[12,16,1152]{2,1,0:T(8,128)(2,1)} %pad_maximum_fusion.1), calls=%async_computation | async-start | bytes 884736 | tf_op jit(solution)/shard_map/all_to_all | solution.py:10
  23.8 0.0 copy-done.5
  23.8 0.0 copy-done.4
  23.8 16.9 %all-to-all-done = bf16[12,16,1152]{2,1,0:T(8,128)(2,1)} async-done(((bf16[12,16,1152]{2,1,0:T(8,128)(2,1)}), bf16[12,16,1152]{2,1,0:T(8,128)(2,1)}, u32[]{:S(2)}, u32[]{:S(2)}) %all-to-all-start) | async-done | bytes 442400 | tf_op jit(solution)/shard_map/all_to_all | solution.py:10
  40.7 1.3 fusion
  42.0 23.4 %all_to_all.35 = bf16[8,224,128]{2,1,0:T(8,128)(2,1)S(1)} all-to-all(bf16[8,224,128]{2,1,0:T(8,128)(2,1)S(1)} %pad_maximum_fusion), channel_id=1, replica_groups=mesh['block'=12,'lane'=8,'node'=8] {'lane'}, dimensions={0} | all-to-all | bytes 917504 | tf_op jit(solution)/shard_map/all_to_all | solution.py:10
  65.4 0.0 copy-start.1
  65.4 0.8 copy-done.1
  66.2 0.0 copy-start.2
  66.3 0.6 copy-done.2
  66.9 0.8 broadcast_in_dim.67
  67.7 3.6 %all-to-all-start.2 = ((bf16[12,128,128]{2,1,0:T(8,128)(2,1)}), bf16[12,128,128]{2,1,0:T(8,128)(2,1)S(1)}, u32[]{:S(2)}, u32[]{:S(2)}) async-start(bf16[12,128,128]{2,1,0:T(8,128)(2,1)} %broadcast_in_dim.67), calls=%async_computation.2 | async-start | bytes 786432 | tf_op jit(solution)/shard_map/all_to_all | solution.py:10
  71.3 0.0 copy-done.6
  71.3 0.2 dynamic-slice_reduce_fusion
  71.5 1.5 slice.50
  72.9 1.5 reshape.119
  74.4 1.6 slice.48
  76.0 15.2 %all-to-all-done.2 = bf16[12,128,128]{2,1,0:T(8,128)(2,1)S(1)} async-done(((bf16[12,128,128]{2,1,0:T(8,128)(2,1)}), bf16[12,128,128]{2,1,0:T(8,128)(2,1)S(1)}, u32[]{:S(2)}, u32[]{:S(2)}) %all-to-all-start.2) | async-done | bytes 393248 | tf_op jit(solution)/shard_map/all_to_all | solution.py:10
  91.2 1.2 gather_fusion.1
  92.4 1.2 fusion.1
  93.6 1.0 fusion.17
  94.7 13.4 %all_to_all.36 = bf16[12,13,128]{2,1,0:T(8,128)(2,1)S(1)} all-to-all(bf16[12,13,128]{2,1,0:T(8,128)(2,1)S(1)} %convert_element_type.64), channel_id=1, replica_groups=mesh['block'=12,'lane'=8,'node'=8] {'block'}, dimensions={0} | all-to-all | bytes 79872 | tf_op jit(solution)/shard_map/all_to_all | solution.py:10
  108.2 13.8 %all_to_all.37 = f32[8,13,128]{2,1,0:T(8,128)S(1)} all-to-all(f32[8,13,128]{2,1,0:T(8,128)S(1)} %broadcast_in_dim.69), channel_id=1, replica_groups=mesh['block'=12,'lane'=8,'node'=8] {'node'}, dimensions={0} | all-to-all | bytes 106496 | tf_op jit(solution)/shard_map/all_to_all | solution.py:10
  122.0 0.6 broadcast_in_dim.70
  122.7 4.3 %all-to-all-start.5 = ((bf16[12,13,128]{2,1,0:T(8,128)(2,1)}), bf16[12,13,128]{2,1,0:T(8,128)(2,1)S(1)}, u32[]{:S(2)}, u32[]{:S(2)}) async-start(bf16[12,13,128]{2,1,0:T(8,128)(2,1)} %broadcast_in_dim.70), calls=%async_computation.5 | async-start | bytes 98304 | tf_op jit(solution)/shard_map/all_to_all | solution.py:10
  126.9 0.8 pad_maximum_fusion.3
  127.7 8.5 %all-to-all-done.5 = bf16[12,13,128]{2,1,0:T(8,128)(2,1)S(1)} async-done(((bf16[12,13,128]{2,1,0:T(8,128)(2,1)}), bf16[12,13,128]{2,1,0:T(8,128)(2,1)S(1)}, u32[]{:S(2)}, u32[]{:S(2)}) %all-to-all-start.5) | async-done | bytes 39968 | tf_op jit(solution)/shard_map/all_to_all | solution.py:10
  136.3 18.8 %all_to_all.38 = bf16[8,188,128]{2,1,0:T(8,128)(2,1)S(1)} all-to-all(bf16[8,188,128]{2,1,0:T(8,128)(2,1)S(1)} %pad_maximum_fusion.2), channel_id=1, replica_groups=mesh['block'=12,'lane'=8,'node'=8] {'lane'}, dimensions={0} | all-to-all | bytes 770048 | tf_op jit(solution)/shard_map/all_to_all | solution.py:10
  155.1 0.7 copy.70
  155.7 1.5 reshape.121
  157.2 1.4 slice_bitcast_fusion.3
  158.6 2.0 %convolution_bitcast_fusion.2 = f32[16,153]{1,0:T(8,128)} fusion(bf16[16,2,1024]{2,0,1:T(8,128)(2,1)} %reshape.121, bf16[2,1024,153]{1,0,2:T(2,128)(2,1)} %param.14), kind=kOutput, calls=%fused_computation.8 | convolution fusion | flops 10027008 | bytes 702016 | tf_op jit(solution)/shard_map/rih,ihc->rc/dot_general | solution.py:69
  160.6 0.4 copy.69
  161.1 1.0 copy.58
  (23 shorter events, 0.5 us)
Async XLA Ops:
  0.6 4.3 %copy-start = (bf16[12,8,128,128]{3,2,1,0:T(8,128)(2,1)S(1)}, bf16[12,8,128,128]{3,2,1,0:T(8,128)(2,1)}, u32[]{:S(2)}) copy-start(bf16[12,8,128,128]{3,2,1,0:T(8,128)(2,1)} %param.10) | copy-start | bytes 9437188
  0.6 5.3 %copy-start.3 = (bf16[2,8,1024]{2,1,0:T(8,128)(2,1)S(1)}, bf16[2,8,1024]{2,1,0:T(8,128)(2,1)}, u32[]{:S(2)}) copy-start(bf16[2,8,1024]{2,1,0:T(8,128)(2,1)} %param.9) | copy-start | bytes 98308
  0.7 23.1 %copy-start.5 = (bf16[16,153]{1,0:T(8,128)(2,1)S(1)}, bf16[16,153]{1,0:T(8,128)(2,1)}, u32[]{:S(2)}) copy-start(bf16[16,153]{1,0:T(8,128)(2,1)} %param.15) | copy-start | bytes 14692
  0.7 23.2 %copy-start.4 = (bf16[16,4,128]{2,1,0:T(4,128)(2,1)S(1)}, bf16[16,4,128]{2,1,0:T(4,128)(2,1)}, u32[]{:S(2)}) copy-start(bf16[16,4,128]{2,1,0:T(4,128)(2,1)} %param.12) | copy-start | bytes 49156
  6.0 65.3 %copy-start.6 = (s32[12,4]{0,1:T(4,128)S(1)}, s32[12,4]{0,1:T(4,128)}, u32[]{:S(2)}) copy-start(s32[12,4]{0,1:T(4,128)} %param.13) | copy-start | bytes 580
  6.8 33.9 %all-to-all-start = ((bf16[12,16,1152]{2,1,0:T(8,128)(2,1)}), bf16[12,16,1152]{2,1,0:T(8,128)(2,1)}, u32[]{:S(2)}, u32[]{:S(2)}) async-start(bf16[12,16,1152]{2,1,0:T(8,128)(2,1)} %pad_maximum_fusion.1), calls=%async_computation | async-start | bytes 884736 | tf_op jit(solution)/shard_map/all_to_all | solution.py:10
  65.4 0.8 copy-start.1
  66.2 0.6 copy-start.2
  67.7 23.5 %all-to-all-start.2 = ((bf16[12,128,128]{2,1,0:T(8,128)(2,1)}), bf16[12,128,128]{2,1,0:T(8,128)(2,1)S(1)}, u32[]{:S(2)}, u32[]{:S(2)}) async-start(bf16[12,128,128]{2,1,0:T(8,128)(2,1)} %broadcast_in_dim.67), calls=%async_computation.2 | async-start | bytes 786432 | tf_op jit(solution)/shard_map/all_to_all | solution.py:10
  122.7 13.5 %all-to-all-start.5 = ((bf16[12,13,128]{2,1,0:T(8,128)(2,1)}), bf16[12,13,128]{2,1,0:T(8,128)(2,1)S(1)}, u32[]{:S(2)}, u32[]{:S(2)}) async-start(bf16[12,13,128]{2,1,0:T(8,128)(2,1)} %broadcast_in_dim.70), calls=%async_computation.5 | async-start | bytes 98304 | tf_op jit(solution)/shard_map/all_to_all | solution.py:10

commit v2 on v1

v2 whole, which is shorter than its diff:
```python
import jax
import jax.numpy as jnp
from jax import lax
from jax.sharding import Mesh, PartitionSpec as P

F32, BF16 = jnp.float32, jnp.bfloat16
LANE = ("x", "c")


def exchange(parts, axis):
    return lax.all_to_all(parts, axis, 0, 0, tiled=True)


def to_all(part, axis, size):
    return exchange(jnp.broadcast_to(part[None], (size, *part.shape)), axis)


def per_device(features, w_one, adj_one, list_one, adj_two, list_two, w_two, cotangent):
    cols, sources = features.shape
    blocks, fanout = list_one.shape
    block = adj_one.shape[-1]
    mine = adj_two.shape[0]
    lanes = block // mine
    hid = w_one.shape[-1]
    nodes = lax.axis_size("node")
    wide = hid // lanes
    cls = cotangent.shape[-1]
    share = -(-cls // blocks)
    xs = lax.axis_size("x")
    strips = block // (mine * lax.axis_size("c"))
    mid, low = lax.axis_index("z") // strips, lax.axis_index("z") % strips

    tiles = features.reshape(cols, sources // block, block)
    chosen = tiles.at[:, list_one].get(mode="promise_in_bounds")
    agg = jnp.einsum("fhks,hkts->hft", chosen, adj_one, preferred_element_type=F32)
    own = tiles[:, :blocks].transpose(1, 0, 2)
    inputs = jnp.concatenate([agg.astype(BF16), own], axis=1)
    weights = jnp.broadcast_to(w_one.reshape(1, 2 * cols, hid), (blocks, 2 * cols, hid))
    got = exchange(jnp.concatenate([inputs, weights], axis=2), "z")
    got = got.reshape(blocks * 2 * cols, block + hid)
    part = jnp.einsum(
        "kr,kjh->jrh",
        got[:, :block],
        got[:, block:].reshape(-1, lanes, wide),
        preferred_element_type=F32,
    ).astype(BF16)
    edges = adj_two.reshape(mine * adj_two.shape[1], block)
    cot = jnp.pad(cotangent, ((0, 0), (0, 2 * block - cls))).reshape(2 * mine, block)
    extra = jnp.concatenate([edges, cot], axis=0)
    extra = jnp.broadcast_to(extra[None], (lanes, *extra.shape))
    got = exchange(jnp.concatenate([part, extra], axis=1), LANE)
    pre = jnp.sum(got[:, :block].astype(F32), axis=0)
    hidden = jnp.maximum(pre, 0.0).astype(BF16)
    edges = got[:, block : block + edges.shape[0]].reshape(xs, block // xs, -1, block)
    cot = got[:, block + mine * edges.shape[2] :].reshape(block, 2 * block)

    every = to_all(hidden, "z", blocks)
    lists = list_two.reshape(xs, blocks // xs, -1)
    lists = lax.dynamic_index_in_dim(lists, mid, 1, keepdims=False)
    near = every.at[lists].get(mode="promise_in_bounds")
    second = jnp.einsum("xrks,xksh->xrh", edges, near, preferred_element_type=F32)
    second = second.astype(BF16).reshape(block, wide)
    held = every.reshape(xs, blocks // xs, strips, block // xs, wide)
    held = lax.dynamic_slice(held, (0, mid, low, 0, 0), (xs, 1, 1, block // xs, wide))
    grad = jnp.einsum("rc,rh->ch", cot, second, preferred_element_type=F32)
    grad = grad[: blocks * share].reshape(blocks, share, wide).astype(BF16)
    grad = jnp.sum(exchange(grad, "z").astype(F32), axis=0)
    grad = jnp.sum(to_all(grad, "node", nodes), axis=0).astype(BF16)
    grad = to_all(grad, "z", blocks).reshape(blocks * share, wide)

    rows = [second.reshape(lanes, mine, wide), held.reshape(lanes, mine, wide)]
    grad = jnp.broadcast_to(grad[None], (lanes, *grad.shape))
    got = exchange(jnp.concatenate([*rows, grad], axis=1), LANE)
    both = got[:, : 2 * mine].reshape(lanes, 2, mine, wide).transpose(2, 1, 0, 3)
    both = both.reshape(mine, 2, hid)
    logits = jnp.einsum("rih,ihc->rc", both, w_two, preferred_element_type=F32)
    grad = got[:, 2 * mine : 2 * mine + cls].transpose(0, 2, 1).reshape(hid, cls).astype(F32)
    return both[:, 1], logits, grad


def solution(mesh):
    nodes = mesh.devices.shape[1]
    fine = Mesh(mesh.devices.reshape(4, 12, 2, nodes), ("x", "z", "c", "node"))
    col = ("x", "z", "c")
    rows = ("node", *col)
    in_specs = (
        P(col, "node"),
        P(None, col, None),
        P("node", None, None, None),
        P("node", None),
        P(rows, None, None),
        P("node", None),
        P(),
        P(rows, None),
    )
    out_specs = (P(rows, None), P(rows, None), P())
    return jax.shard_map(
        per_device, mesh=fine, in_specs=in_specs, out_specs=out_specs, check_vma=False
    )
```

time: 163 us -> 159 us (0.975)
  blocking collectives: 69.4 us -> 45.7 us
  waiting for transfers between devices: 40.5 us -> 50.1 us
  starting transfers between devices: 24.8 us -> 30.2 us
  local copies, waits for them, and re-layouts: 16.4 us -> 20.8 us
    all_to_all x4 -> x3, blocking collectives: 69.4 us -> 45.7 us  [exchange(): return lax.all_to_all(parts, axis, 0, 0, tiled=True)]
    all_to_all x3 -> x4, waiting for transfers between devices: 40.5 us -> 50.1 us  [exchange(): return lax.all_to_all(parts, axis, 0, 0, tiled=True)]
    all_to_all x3 -> x4, starting transfers between devices: 24.8 us -> 30.2 us  [exchange(): return lax.all_to_all(parts, axis, 0, 0, tiled=True)]
  transfers between devices with their start and end apart: 3 -> 4, of which waited for: 3 -> 4; matrix products, arithmetic and copies ran while one was open for 3% -> 4% of each run, Pallas kernels for 0% -> 0%
where the time goes in v2:
time: 159 us; the launch traced here: 158 us
  waiting for transfers between devices  50.1 us (32%)
  blocking collectives  45.7 us (29%)
  starting transfers between devices  30.2 us (19%)
  local copies, waits for them, and re-layouts  20.8 us (13%)
  matrix products  6.52 us (4%)
  other arithmetic  3.48 us (2%)
    all_to_all x4, waiting for transfers between devices, exchange(): return lax.all_to_all(parts, axis, 0, 0, tiled=True)  50.1 us
    all_to_all x3, blocking collectives, exchange(): return lax.all_to_all(parts, axis, 0, 0, tiled=True)  45.7 us
    all_to_all x4, starting transfers between devices, exchange(): return lax.all_to_all(parts, axis, 0, 0, tiled=True)  30.2 us
  transfers between devices with their start and end apart: 4, of which 4 were waited for; matrix products, arithmetic and copies ran while one was open for 4% of the time, Pallas kernels for 0%

profile of v2, /device:TPU:1, one launch (start us, length us, event | category | flops | bytes accessed | tf_op | source)
XLA Modules:
  0.0 157.7 jit_solution(15168986404072192935)
XLA Ops:
  0.6 0.0 copy-start
  0.6 0.0 copy-start.3
  0.7 0.0 copy-start.5
  0.7 0.0 copy-start.4
  0.7 0.8 compare_select_fusion
  1.5 0.1 copy.51
  1.6 0.1 reshape.106
  1.7 0.7 slice_bitcast_fusion.4
  2.4 1.6 %gather_fusion = bf16[96,8,128]{2,1,0:T(8,128)(2,1)S(1)} fusion(bf16[8,96,128]{2,0,1:T(8,128)(2,1)} %bitcast.82, s32[1024]{0:T(1024)S(1)} %pad_clamp_fusion.1), kind=kCustom, calls=%fused_computation | custom fusion | bytes 393600 | tf_op jit(solution)/shard_map/gather | solution.py:34
  4.0 0.0 copy-done
  4.0 0.9 fusion.2
  5.0 0.0 copy-done.3
  5.0 0.1 broadcast_in_dim.20
  5.0 0.0 copy-start.6
  5.0 0.8 pad_maximum_fusion.1
  5.8 15.7 %all-to-all-start = ((bf16[12,16,1152]{2,1,0:T(8,128)(2,1)}), bf16[12,16,1152]{2,1,0:T(8,128)(2,1)}, u32[]{:S(2)}, u32[]{:S(2)}) async-start(bf16[12,16,1152]{2,1,0:T(8,128)(2,1)} %pad_maximum_fusion.1), calls=%async_computation | async-start | bytes 884736 | tf_op jit(solution)/shard_map/all_to_all | solution.py:11
  21.6 0.0 copy-done.5
  21.6 0.0 copy-done.4
  21.6 19.8 %all-to-all-done = bf16[12,16,1152]{2,1,0:T(8,128)(2,1)} async-done(((bf16[12,16,1152]{2,1,0:T(8,128)(2,1)}), bf16[12,16,1152]{2,1,0:T(8,128)(2,1)}, u32[]{:S(2)}, u32[]{:S(2)}) %all-to-all-start) | async-done | bytes 442400 | tf_op jit(solution)/shard_map/all_to_all | solution.py:11
  41.4 1.3 fusion
  42.8 15.1 %all_to_all.35 = bf16[8,224,128]{2,1,0:T(8,128)(2,1)S(1)} all-to-all(bf16[8,224,128]{2,1,0:T(8,128)(2,1)S(1)} %pad_maximum_fusion), channel_id=1, replica_groups=mesh['x'=4,'z'=12,'c'=2,'node'=8] {'x','c'}, dimensions={0} | all-to-all | bytes 917504 | tf_op jit(solution)/shard_map/all_to_all | solution.py:11
  57.9 0.0 copy-start.1
  57.9 0.8 copy-done.1
  58.8 0.8 broadcast_in_dim.22
  59.6 3.6 %all-to-all-start.2 = ((bf16[12,128,128]{2,1,0:T(8,128)(2,1)}), bf16[12,128,128]{2,1,0:T(8,128)(2,1)S(1)}, u32[]{:S(2)}, u32[]{:S(2)}) async-start(bf16[12,128,128]{2,1,0:T(8,128)(2,1)} %broadcast_in_dim.22), calls=%async_computation.2 | async-start | bytes 786432 | tf_op jit(solution)/shard_map/all_to_all | solution.py:11
  63.2 0.0 copy-done.6
  63.2 0.1 reshape.96
  63.3 0.1 constant_dynamic-slice_fusion.1
  63.3 0.1 copy.53
  63.5 0.1 reshape.114
  63.6 1.5 slice.50
  65.0 1.5 reshape.99
  66.5 1.6 slice.48
  68.1 13.9 %all-to-all-done.2 = bf16[12,128,128]{2,1,0:T(8,128)(2,1)S(1)} async-done(((bf16[12,128,128]{2,1,0:T(8,128)(2,1)}), bf16[12,128,128]{2,1,0:T(8,128)(2,1)S(1)}, u32[]{:S(2)}, u32[]{:S(2)}) %all-to-all-start.2) | async-done | bytes 393248 | tf_op jit(solution)/shard_map/all_to_all | solution.py:11
  82.0 1.4 gather_fusion.1
  83.4 1.3 fusion.1
  84.7 0.0 copy-start.2
  84.7 0.6 copy-done.2
  85.3 1.0 fusion.7
  86.3 0.6 slice.63
  87.0 1.4 convert_element_type.53
  88.4 14.0 %all_to_all.36 = bf16[12,13,128]{2,1,0:T(8,128)(2,1)S(1)} all-to-all(bf16[12,13,128]{2,1,0:T(8,128)(2,1)} %convert_element_type.53), channel_id=1, replica_groups=mesh['x'=4,'z'=12,'c'=2,'node'=8] {'z'}, dimensions={0} | all-to-all | bytes 79872 | tf_op jit(solution)/shard_map/all_to_all | solution.py:11
  102.4 0.6 broadcast_in_dim.23
  103.0 6.8 %all-to-all-start.4 = ((f32[8,13,128]{2,1,0:T(8,128)}), f32[8,13,128]{2,1,0:T(8,128)}, u32[]{:S(2)}, u32[]{:S(2)}) async-start(f32[8,13,128]{2,1,0:T(8,128)} %broadcast_in_dim.23), calls=%async_computation.4 | async-start | bytes 131072 | tf_op jit(solution)/shard_map/all_to_all | solution.py:11
  109.8 7.3 %all-to-all-done.4 = f32[8,13,128]{2,1,0:T(8,128)} async-done(((f32[8,13,128]{2,1,0:T(8,128)}), f32[8,13,128]{2,1,0:T(8,128)}, u32[]{:S(2)}, u32[]{:S(2)}) %all-to-all-start.4) | async-done | bytes 53280 | tf_op jit(solution)/shard_map/all_to_all | solution.py:11
  117.2 0.9 reduce_sum.29
  118.0 0.6 broadcast_in_dim.48
  118.6 4.1 %all-to-all-start.5 = ((bf16[12,13,128]{2,1,0:T(8,128)(2,1)}), bf16[12,13,128]{2,1,0:T(8,128)(2,1)}, u32[]{:S(2)}, u32[]{:S(2)}) async-start(bf16[12,13,128]{2,1,0:T(8,128)(2,1)} %broadcast_in_dim.48), calls=%async_computation.5 | async-start | bytes 98304 | tf_op jit(solution)/shard_map/all_to_all | solution.py:11
  122.8 0.6 constant_dynamic-slice_fusion
  123.4 9.0 %all-to-all-done.5 = bf16[12,13,128]{2,1,0:T(8,128)(2,1)} async-done(((bf16[12,13,128]{2,1,0:T(8,128)(2,1)}), bf16[12,13,128]{2,1,0:T(8,128)(2,1)}, u32[]{:S(2)}, u32[]{:S(2)}) %all-to-all-start.5) | async-done | bytes 39968 | tf_op jit(solution)/shard_map/all_to_all | solution.py:11
  132.4 0.8 broadcast_in_dim.49
  133.3 0.8 pad_maximum_fusion.2
  134.1 16.6 %all_to_all.37 = bf16[8,188,128]{2,1,0:T(8,128)(2,1)S(1)} all-to-all(bf16[8,188,128]{2,1,0:T(8,128)(2,1)S(1)} %pad_maximum_fusion.2), channel_id=1, replica_groups=mesh['x'=4,'z'=12,'c'=2,'node'=8] {'x','c'}, dimensions={0} | all-to-all | bytes 770048 | tf_op jit(solution)/shard_map/all_to_all | solution.py:11
  150.7 0.7 copy.75
  151.4 1.5 reshape.102
  152.9 1.4 slice_bitcast_fusion.3
  154.3 2.0 %convolution_bitcast_fusion.2 = f32[16,153]{1,0:T(8,128)} fusion(bf16[16,2,1024]{2,0,1:T(8,128)(2,1)} %reshape.102, bf16[2,1024,153]{1,0,2:T(2,128)(2,1)} %param.14), kind=kOutput, calls=%fused_computation.8 | convolution fusion | flops 10027008 | bytes 702016 | tf_op jit(solution)/shard_map/rih,ihc->rc/dot_general | solution.py:76
  156.3 0.4 copy.74
  156.8 1.0 copy.63
  (15 shorter events, 0.3 us)
Async XLA Ops:
  0.6 3.4 %copy-start = (bf16[12,8,128,128]{3,2,1,0:T(8,128)(2,1)S(1)}, bf16[12,8,128,128]{3,2,1,0:T(8,128)(2,1)}, u32[]{:S(2)}) copy-start(bf16[12,8,128,128]{3,2,1,0:T(8,128)(2,1)} %param.10) | copy-start | bytes 9437188
  0.6 4.3 %copy-start.3 = (bf16[2,8,1024]{2,1,0:T(8,128)(2,1)S(1)}, bf16[2,8,1024]{2,1,0:T(8,128)(2,1)}, u32[]{:S(2)}) copy-start(bf16[2,8,1024]{2,1,0:T(8,128)(2,1)} %param.9) | copy-start | bytes 98308
  0.7 20.9 %copy-start.5 = (bf16[16,153]{1,0:T(8,128)(2,1)S(1)}, bf16[16,153]{1,0:T(8,128)(2,1)}, u32[]{:S(2)}) copy-start(bf16[16,153]{1,0:T(8,128)(2,1)} %param.15) | copy-start | bytes 14692
  0.7 20.9 %copy-start.4 = (bf16[16,4,128]{2,1,0:T(4,128)(2,1)S(1)}, bf16[16,4,128]{2,1,0:T(4,128)(2,1)}, u32[]{:S(2)}) copy-start(bf16[16,4,128]{2,1,0:T(4,128)(2,1)} %param.12) | copy-start | bytes 49156
  5.0 58.2 %copy-start.6 = (s32[12,4]{0,1:T(4,128)S(1)}, s32[12,4]{0,1:T(4,128)}, u32[]{:S(2)}) copy-start(s32[12,4]{0,1:T(4,128)} %param.13) | copy-start | bytes 580
  5.8 35.6 %all-to-all-start = ((bf16[12,16,1152]{2,1,0:T(8,128)(2,1)}), bf16[12,16,1152]{2,1,0:T(8,128)(2,1)}, u32[]{:S(2)}, u32[]{:S(2)}) async-start(bf16[12,16,1152]{2,1,0:T(8,128)(2,1)} %pad_maximum_fusion.1), calls=%async_computation | async-start | bytes 884736 | tf_op jit(solution)/shard_map/all_to_all | solution.py:11
  57.9 0.8 copy-start.1
  59.6 22.4 %all-to-all-start.2 = ((bf16[12,128,128]{2,1,0:T(8,128)(2,1)}), bf16[12,128,128]{2,1,0:T(8,128)(2,1)S(1)}, u32[]{:S(2)}, u32[]{:S(2)}) async-start(bf16[12,128,128]{2,1,0:T(8,128)(2,1)} %broadcast_in_dim.22), calls=%async_computation.2 | async-start | bytes 786432 | tf_op jit(solution)/shard_map/all_to_all | solution.py:11
  84.7 0.6 copy-start.2
  103.0 14.2 %all-to-all-start.4 = ((f32[8,13,128]{2,1,0:T(8,128)}), f32[8,13,128]{2,1,0:T(8,128)}, u32[]{:S(2)}, u32[]{:S(2)}) async-start(f32[8,13,128]{2,1,0:T(8,128)} %broadcast_in_dim.23), calls=%async_computation.4 | async-start | bytes 131072 | tf_op jit(solution)/shard_map/all_to_all | solution.py:11
  118.6 13.8 %all-to-all-start.5 = ((bf16[12,13,128]{2,1,0:T(8,128)(2,1)}), bf16[12,13,128]{2,1,0:T(8,128)(2,1)}, u32[]{:S(2)}, u32[]{:S(2)}) async-start(bf16[12,13,128]{2,1,0:T(8,128)(2,1)} %broadcast_in_dim.48), calls=%async_computation.5 | async-start | bytes 98304 | tf_op jit(solution)/shard_map/all_to_all | solution.py:11

commit v3 on v2

v3 whole, which is shorter than its diff:
```python
import jax
import jax.numpy as jnp
from jax import lax
from jax.sharding import Mesh, PartitionSpec as P

F32, BF16 = jnp.float32, jnp.bfloat16
LANE = ("x", "c")


def exchange(parts, axis):
    return lax.all_to_all(parts, axis, 0, 0, tiled=True)


def to_all(part, size):
    return jnp.broadcast_to(part[None], (size, *part.shape))


def dot(spec, a, b):
    return jnp.einsum(spec, a, b, preferred_element_type=F32)


def two(a):
    high = a.astype(BF16)
    return high, (a - high.astype(F32)).astype(BF16)


def per_device(features, w_one, adj_one, list_one, adj_two, list_two, w_two, cotangent):
    cols, sources = features.shape
    blocks, fanout = list_one.shape
    block = adj_one.shape[-1]
    mine, listed = adj_two.shape[:2]
    hid, cls = w_two.shape[1:]
    xs, cores = lax.axis_size("x"), lax.axis_size("c")
    lanes = xs * cores
    wide = hid // lanes
    by_lane = -(-cls // (8 * lanes)) * 8
    every = by_lane * lanes
    by_z = every // blocks
    kept = -(-cls // 8) * 8
    strip = mine * cores
    strips = block // strip
    mids = blocks // xs
    place = lax.axis_index("z")
    lane = lax.axis_index("x") * cores + lax.axis_index("c")
    lists = list_two.reshape(xs, mids, listed)
    lists = lax.dynamic_index_in_dim(lists, place // strips, 1, keepdims=False)

    shape = (xs, block, strips, block)
    x_of, row, low_of, to = (lax.broadcasted_iota(jnp.int32, shape, i) for i in range(4))
    move = (row // strip == low_of) & (to // strip == x_of) & (row % strip == to % strip)
    move = move.astype(BF16)

    def to_z(a):
        a = a.reshape(xs, mids, -1, block)
        return dot("xmkl,xlzr->mzkr", a, move).astype(BF16).reshape(blocks, -1, block)

    def to_blocks(a):
        a = a.reshape(mids, strips, -1, block)
        return dot("mzkr,xlzr->xmkl", a, move).astype(BF16).reshape(blocks, -1, block)

    edges = to_all(adj_two.reshape(mine * listed, block), lanes)
    cot = jnp.pad(cotangent, ((0, 0), (0, every - cls))).reshape(mine, lanes, by_lane)
    cot = jnp.pad(cot.transpose(1, 0, 2), ((0, 0), (0, 0), (0, block - by_lane)))
    got = exchange(jnp.concatenate([edges, cot], axis=1), LANE)
    edges = got[:, : mine * listed].reshape(xs, strip, listed, block)
    cot = got[:, mine * listed :, :by_lane].reshape(xs, strip, by_lane)

    tiles = features.reshape(cols, sources // block, block)
    chosen = tiles.at[:, list_one].get(mode="promise_in_bounds")
    agg = dot("fhks,hkts->hft", chosen, adj_one).astype(BF16)
    own = tiles[:, :blocks].transpose(1, 0, 2)
    inputs = to_z(jnp.concatenate([agg, own], axis=1))
    weights = w_one.reshape(2 * cols, lanes, wide).transpose(1, 0, 2).reshape(-1, wide)
    back = dot("xrc,xrks->xkcs", cot, edges)
    hits = lists[:, :, None] == jnp.arange(blocks, dtype=jnp.int32)
    back = jnp.where(hits[..., None, None], back[:, :, None], 0.0).sum((0, 1)).astype(BF16)
    got = [inputs, to_z(back), to_all(weights, blocks)]
    got = exchange(jnp.concatenate(got, axis=1), "z")
    inputs, back, weights = jnp.split(got, (2 * cols, 2 * cols + by_lane), axis=1)
    weights = weights.reshape(blocks, lanes, 2 * cols, wide)
    part = dot("zkr,zjkh->jrh", inputs, weights).astype(BF16)
    back = jnp.concatenate(two(jnp.sum(back.astype(F32), axis=0)), axis=0)

    got = exchange(jnp.concatenate([part, to_all(back, lanes)], axis=1), LANE)
    pre = jnp.sum(got[:, :block].astype(F32), axis=0)
    hidden = jnp.maximum(pre, 0.0).astype(BF16)
    high = got[:, block : block + by_lane].reshape(every, block)
    low = got[:, block + by_lane :].reshape(every, block)
    grad = dot("cr,rh->ch", high, hidden) + dot("cr,rh->ch", low, hidden)
    grad = jnp.sum(exchange(grad.reshape(blocks, by_z, wide), "z"), axis=0)
    grad = lax.psum(grad, "node").astype(BF16)

    near_w = lax.dynamic_slice(w_two, (0, lane * wide, 0), (1, wide, cls))[0]
    near_w = jnp.pad(near_w, ((0, 0), (0, every - cls)))
    product = dot("hc,rh->cr", near_w, hidden).astype(BF16).reshape(lanes, by_lane, block)
    rows = hidden.reshape(lanes, mine, wide)
    got = exchange(jnp.concatenate([product, rows], axis=1), LANE)
    product = jnp.sum(got[:, :by_lane].astype(F32), axis=0).astype(BF16)
    hidden = got[:, by_lane:].transpose(1, 0, 2).reshape(mine, hid)
    own_logits = dot("rh,hc->rc", hidden, w_two[1])

    got = exchange(to_all(jnp.concatenate([grad, product], axis=0), blocks), "z")
    grad = got[:, :by_z].reshape(every, wide)[:kept]
    near = to_blocks(got[:, by_z:]).at[lists].get(mode="promise_in_bounds")
    logits = dot("xrks,xkcs->xrc", edges, near).reshape(lanes, mine, by_lane)
    logits = jnp.concatenate(two(logits), axis=2)
    logits = jnp.pad(logits, ((0, 0), (0, 0), (0, wide - 2 * by_lane)))
    got = exchange(jnp.concatenate([to_all(grad, lanes), logits], axis=1), LANE)
    logits = got[:, kept:].astype(F32)
    logits = logits[..., :by_lane] + logits[..., by_lane : 2 * by_lane]
    logits = logits.transpose(1, 0, 2).reshape(mine, every)[:, :cls] + own_logits
    grad = got[:, :cls].transpose(0, 2, 1).reshape(hid, cls).astype(F32)
    return hidden, logits, grad


def solution(mesh):
    nodes = mesh.devices.shape[1]
    fine = Mesh(mesh.devices.reshape(4, 12, 2, nodes), ("x", "z", "c", "node"))
    col = ("x", "z", "c")
    rows = ("node", *col)
    in_specs = (
        P(col, "node"),
        P(None, col, None),
        P("node", None, None, None),
        P("node", None),
        P(rows, None, None),
        P("node", None),
        P(),
        P(rows, None),
    )
    out_specs = (P(rows, None), P(rows, None), P())
    return jax.shard_map(
        per_device, mesh=fine, in_specs=in_specs, out_specs=out_specs, check_vma=False
    )
```

time: 159 us -> 155 us (0.975)
  waiting for transfers between devices: 50.1 us -> 34.5 us
  starting transfers between devices: 30.2 us -> 43.2 us
  other arithmetic: 3.48 us -> 6.54 us
  local copies, waits for them, and re-layouts: 20.8 us -> 17.9 us
  blocking collectives: 45.7 us -> 43.4 us
    all_to_all x3 -> x1, blocking collectives: 45.7 us -> 29 us  [exchange(): return lax.all_to_all(parts, axis, 0, 0, tiled=True)]
    all_to_all x4 -> x6, waiting for transfers between devices: 50.1 us -> 34.5 us  [exchange(): return lax.all_to_all(parts, axis, 0, 0, tiled=True)]
    psum x0 -> x1, blocking collectives: none -> 14.4 us  [per_device(): grad = lax.psum(grad, 'node').astype(BF16)]
    all_to_all x4 -> x6, starting transfers between devices: 30.2 us -> 43.2 us  [exchange(): return lax.all_to_all(parts, axis, 0, 0, tiled=True)]
    reshape x5 -> x4, local copies, waits for them, and re-layouts: 3.74 us -> 2.53 us  [the longest x1 0.91 us: per_device(): logits.transpose(1, 0, 2).reshape(mine, every)[:, :cls] + own_logits]
    unnamed x16 -> x29, local copies, waits for them, and re-layouts: 2.41 us -> 3.5 us
    slice x4 -> x6, local copies, waits for them, and re-layouts: 3.67 us -> 2.62 us  [the longest x1 2.58 us: per_device(): own_logits = dot('rh,hc->rc', hidden, w_two[1])]
    dot_general x5 -> x11, matrix products: 6.52 us -> 7.5 us  [dot(): return jnp.einsum(spec, a, b, preferred_element_type=F32)]
  transfers between devices with their start and end apart: 4 -> 6, of which waited for: 4 -> 5; matrix products, arithmetic and copies ran while one was open for 4% -> 10% of each run, Pallas kernels for 0% -> 0%
where the time goes in v3:
time: 155 us; the launch traced here: 154 us
  blocking collectives  43.4 us (28%)
  starting transfers between devices  43.2 us (28%)
  waiting for transfers between devices  34.5 us (22%)
  local copies, waits for them, and re-layouts  17.9 us (12%)
  matrix products  7.5 us (5%)
  other arithmetic  6.54 us (4%)
    all_to_all x6, starting transfers between devices, exchange(): return lax.all_to_all(parts, axis, 0, 0, tiled=True)  43.2 us
    all_to_all x6, waiting for transfers between devices, exchange(): return lax.all_to_all(parts, axis, 0, 0, tiled=True)  34.5 us
    all_to_all x1, blocking collectives, exchange(): return lax.all_to_all(parts, axis, 0, 0, tiled=True)  29 us
    psum x1, blocking collectives, per_device(): grad = lax.psum(grad, 'node').astype(BF16)  14.4 us
    dot_general x11, matrix products, dot(): return jnp.einsum(spec, a, b, preferred_element_type=F32)  7.5 us
    unnamed x29, local copies, waits for them, and re-layouts  3.5 us
  transfers between devices with their start and end apart: 6, of which 5 were waited for; matrix products, arithmetic and copies ran while one was open for 10% of the time, Pallas kernels for 0%

profile of v3, /device:TPU:1, one launch (start us, length us, event | category | flops | bytes accessed | tf_op | source)
XLA Modules:
  0.0 154.1 jit_solution(17269221051080002332)
XLA Ops:
  0.6 0.0 copy-start
  0.6 0.9 pad.17
  1.5 0.1 reshape.120
  1.6 0.7 broadcast_in_dim.65
  2.3 0.7 fusion.14
  3.0 13.8 %all-to-all-start = ((bf16[8,80,128]{2,1,0:T(8,128)(2,1)}), bf16[8,80,128]{2,1,0:T(8,128)(2,1)S(1)}, u32[]{:S(2)}, u32[]{:S(2)}) async-start(bf16[8,80,128]{2,1,0:T(8,128)(2,1)} %fusion.14), calls=%async_computation | async-start | bytes 327680 | tf_op jit(solution)/shard_map/all_to_all | solution.py:11
  16.8 0.6 broadcast_add_fusion
  17.4 0.6 compare_and_fusion
  18.0 0.8 copy.139
  18.8 0.8 reshape.119
  19.6 0.1 constant_dynamic-slice_fusion
  19.6 0.1 copy.103
  19.7 1.3 slice_bitcast_fusion.3
  21.1 0.7 compare_select_fusion
  21.8 0.1 copy.99
  21.9 0.1 reshape.138
  22.0 1.6 %gather_fusion = bf16[96,8,128]{2,1,0:T(8,128)(2,1)S(1)} fusion(bf16[8,96,128]{2,0,1:T(8,128)(2,1)} %bitcast.148, s32[1024]{0:T(1024)S(1)} %pad_clamp_fusion.1), kind=kCustom, calls=%fused_computation | custom fusion | bytes 393600 | tf_op jit(solution)/shard_map/gather | solution.py:69
  23.6 0.0 copy-start.7
  23.6 0.9 fusion.7
  24.6 0.2 fusion.29
  24.9 0.3 fusion.6
  25.1 0.4 copy-done.4
  25.6 0.1 iota_compare_fusion.4
  25.7 0.6 copy-done.2
  26.3 0.2 convolution_bitcast_fusion.1
  26.5 0.3 select_reduce_fusion
  26.8 1.2 fusion.5
  28.0 0.1 broadcast_in_dim.69
  28.1 29.0 %all_to_all.35 = bf16[12,168,128]{2,1,0:T(8,128)(2,1)S(1)} all-to-all(bf16[12,168,128]{2,1,0:T(8,128)(2,1)S(1)} %pad_maximum_fusion), channel_id=1, replica_groups=mesh['x'=4,'z'=12,'c'=2,'node'=8] {'z'}, dimensions={0} | all-to-all | bytes 1032192 | tf_op jit(solution)/shard_map/all_to_all | solution.py:11
  57.2 0.3 fusion.1
  57.5 0.8 pad_maximum_fusion.1
  58.3 7.5 %all-to-all-start.2 = ((bf16[8,176,128]{2,1,0:T(8,128)(2,1)}), bf16[8,176,128]{2,1,0:T(8,128)(2,1)S(1)}, u32[]{:S(2)}, u32[]{:S(2)}) async-start(bf16[8,176,128]{2,1,0:T(8,128)(2,1)} %pad_maximum_fusion.1), calls=%async_computation.2 | async-start | bytes 720896 | tf_op jit(solution)/shard_map/all_to_all | solution.py:11
  65.8 0.9 constant_dynamic-slice_fusion.1
  66.7 0.6 copy.163
  67.3 6.2 %all-to-all-done.2 = bf16[8,176,128]{2,1,0:T(8,128)(2,1)S(1)} async-done(((bf16[8,176,128]{2,1,0:T(8,128)(2,1)}), bf16[8,176,128]{2,1,0:T(8,128)(2,1)S(1)}, u32[]{:S(2)}, u32[]{:S(2)}) %all-to-all-start.2) | async-done | bytes 360480 | tf_op jit(solution)/shard_map/all_to_all | solution.py:11
  73.6 0.9 convolution_convert_fusion
  74.5 0.6 pad_maximum_fusion.3
  75.2 4.7 %all-to-all-start.3 = ((bf16[8,40,128]{2,1,0:T(8,128)(2,1)}), bf16[8,40,128]{2,1,0:T(8,128)(2,1)}, u32[]{:S(2)}, u32[]{:S(2)}) async-start(bf16[8,40,128]{2,1,0:T(8,128)(2,1)} %pad_maximum_fusion.3), calls=%async_computation.3 | async-start | bytes 163840 | tf_op jit(solution)/shard_map/all_to_all | solution.py:11
  79.9 0.1 fusion.31
  80.0 0.8 convolution_add_fusion
  80.8 4.1 %all-to-all-done.3 = bf16[8,40,128]{2,1,0:T(8,128)(2,1)} async-done(((bf16[8,40,128]{2,1,0:T(8,128)(2,1)}), bf16[8,40,128]{2,1,0:T(8,128)(2,1)}, u32[]{:S(2)}, u32[]{:S(2)}) %all-to-all-start.3) | async-done | bytes 81952 | tf_op jit(solution)/shard_map/all_to_all | solution.py:11
  84.9 3.5 %all-to-all-start.4 = ((f32[12,16,128]{2,1,0:T(8,128)}), f32[12,16,128]{2,1,0:T(8,128)S(1)}, u32[]{:S(2)}, u32[]{:S(2)}) async-start(f32[12,16,128]{2,1,0:T(8,128)} %bitcast.40), calls=%async_computation.4 | async-start | bytes 196608 | tf_op jit(solution)/shard_map/all_to_all | solution.py:11
  88.4 0.8 slice_reduce_fusion
  89.3 9.2 %all-to-all-done.4 = f32[12,16,128]{2,1,0:T(8,128)S(1)} async-done(((f32[12,16,128]{2,1,0:T(8,128)}), f32[12,16,128]{2,1,0:T(8,128)S(1)}, u32[]{:S(2)}, u32[]{:S(2)}) %all-to-all-start.4) | async-done | bytes 98336 | tf_op jit(solution)/shard_map/all_to_all | solution.py:11
  98.5 14.4 %psum.7 = bf16[16,128]{1,0:T(8,128)(2,1)S(1)} all-reduce(f32[16,128]{1,0:T(8,128)S(1)} %reduce_sum.51), channel_id=1, replica_groups=mesh['x'=4,'z'=12,'c'=2,'node'=8] {'node'}, use_global_device_ids=true, to_apply=%region_4.5 | all-reduce | flops 2048 | bytes 12288 | tf_op jit(solution)/shard_map/psum | solution.py:91
  112.9 0.7 broadcast_in_dim.71
  113.6 3.5 %all-to-all-start.5 = ((bf16[12,40,128]{2,1,0:T(8,128)(2,1)}), bf16[12,40,128]{2,1,0:T(8,128)(2,1)S(1)}, u32[]{:S(2)}, u32[]{:S(2)}) async-start(bf16[12,40,128]{2,1,0:T(8,128)(2,1)} %broadcast_in_dim.71), calls=%async_computation.5 | async-start | bytes 245760 | tf_op jit(solution)/shard_map/all_to_all | solution.py:11
  117.1 0.1 reshape.146
  117.2 10.7 %all-to-all-done.5 = bf16[12,40,128]{2,1,0:T(8,128)(2,1)S(1)} async-done(((bf16[12,40,128]{2,1,0:T(8,128)(2,1)}), bf16[12,40,128]{2,1,0:T(8,128)(2,1)S(1)}, u32[]{:S(2)}, u32[]{:S(2)}) %all-to-all-start.5) | async-done | bytes 122912 | tf_op jit(solution)/shard_map/all_to_all | solution.py:11
  127.9 1.8 %fusion.3 = bf16[4,128,3,24]{1,3,2,0:T(8,128)(2,1)} fusion(bf16[3,4,24,128,1]{3,2,1,0,4:T(8,128)(2,1)S(1)} %bitcast.161, s32[128]{0:T(128)S(1)} %get-tuple-element.12, s32[128]{0:T(128)S(1)} %copy-done.8, s32[128]{0:T(128)S(1)} %get-tuple-element.11, s32[128]{0:T(128)} %get-tuple-element.14, pred[128]{0:T(512)(128)(4,1)} %get-tuple-element.9, ...), kind=kOutput, calls=%fused_computation.10 | convolution fusion | flops 40144896 | bytes 149760 | tf_op jit(solution)/shard_map/mzkr,xlzr->xmkl/dot_general | solution.py:19
  129.7 1.5 gather_fusion.1
  131.2 0.1 fusion.15
  131.4 0.1 fusion.26
  131.5 0.8 pad_maximum_fusion.2
  132.3 10.1 %all-to-all-start.6 = ((bf16[8,176,128]{2,1,0:T(8,128)(2,1)}), bf16[8,176,128]{2,1,0:T(8,128)(2,1)S(1)}, u32[]{:S(2)}, u32[]{:S(2)}) async-start(bf16[8,176,128]{2,1,0:T(8,128)(2,1)} %pad_maximum_fusion.2), calls=%async_computation.6 | async-start | bytes 720896 | tf_op jit(solution)/shard_map/all_to_all | solution.py:11
  142.4 2.6 %slice.65 = bf16[1,1024,153]{1,0,2:T(2,128)(2,1)} slice(bf16[2,1024,153]{1,0,2:T(2,128)(2,1)} %param.14), slice={[1:2], [0:1024], [0:153]} | slice | bytes 626688 | tf_op jit(solution)/shard_map/slice | solution.py:100
  145.0 0.8 copy_bitcast_fusion.4
  145.7 4.4 %all-to-all-done.6 = bf16[8,176,128]{2,1,0:T(8,128)(2,1)S(1)} async-done(((bf16[8,176,128]{2,1,0:T(8,128)(2,1)}), bf16[8,176,128]{2,1,0:T(8,128)(2,1)S(1)}, u32[]{:S(2)}, u32[]{:S(2)}) %all-to-all-start.6) | async-done | bytes 360480 | tf_op jit(solution)/shard_map/all_to_all | solution.py:11
  150.1 0.1 fusion.20
  150.2 0.7 copy.115
  150.9 0.9 reshape.134
  151.9 0.4 copy.162
  152.3 1.0 copy.140
  153.3 0.8 convolution_add_fusion.1
  (50 shorter events, 0.5 us)
Async XLA Ops:
  0.6 23.0 %copy-start = (bf16[12,8,128,128]{3,2,1,0:T(8,128)(2,1)S(1)}, bf16[12,8,128,128]{3,2,1,0:T(8,128)(2,1)}, u32[]{:S(2)}) copy-start(bf16[12,8,128,128]{3,2,1,0:T(8,128)(2,1)} %param.10) | copy-start | bytes 9437188
  3.0 22.6 %all-to-all-start = ((bf16[8,80,128]{2,1,0:T(8,128)(2,1)}), bf16[8,80,128]{2,1,0:T(8,128)(2,1)S(1)}, u32[]{:S(2)}, u32[]{:S(2)}) async-start(bf16[8,80,128]{2,1,0:T(8,128)(2,1)} %fusion.14), calls=%async_computation | async-start | bytes 327680 | tf_op jit(solution)/shard_map/all_to_all | solution.py:11
  23.6 1.0 copy-start.6
  23.6 1.0 copy-start.7
  23.6 1.0 copy-start.9
  23.6 1.0 copy-start.10
  23.6 1.0 copy-start.11
  24.8 0.7 copy-start.4
  25.7 0.7 copy-start.2
  57.1 70.8 %copy-start.8 = (s32[128]{0:T(128)S(1)}, s32[128]{0:T(128)}, u32[]{:S(2)}) copy-start(s32[128]{0:T(128)} %get-tuple-element.13) | copy-start | bytes 1540
  58.3 15.3 %all-to-all-start.2 = ((bf16[8,176,128]{2,1,0:T(8,128)(2,1)}), bf16[8,176,128]{2,1,0:T(8,128)(2,1)S(1)}, u32[]{:S(2)}, u32[]{:S(2)}) async-start(bf16[8,176,128]{2,1,0:T(8,128)(2,1)} %pad_maximum_fusion.1), calls=%async_computation.2 | async-start | bytes 720896 | tf_op jit(solution)/shard_map/all_to_all | solution.py:11
  75.2 9.8 %all-to-all-start.3 = ((bf16[8,40,128]{2,1,0:T(8,128)(2,1)}), bf16[8,40,128]{2,1,0:T(8,128)(2,1)}, u32[]{:S(2)}, u32[]{:S(2)}) async-start(bf16[8,40,128]{2,1,0:T(8,128)(2,1)} %pad_maximum_fusion.3), calls=%async_computation.3 | async-start | bytes 163840 | tf_op jit(solution)/shard_map/all_to_all | solution.py:11
  79.9 51.3 %copy-start.3 = (bf16[8,64,128]{2,1,0:T(8,128)(2,1)S(1)}, bf16[8,64,128]{2,1,0:T(8,128)(2,1)}, u32[]{:S(2)}) copy-start(bf16[8,64,128]{2,1,0:T(8,128)(2,1)} %copy-done.2) | copy-start | bytes 393220
  84.9 13.5 %all-to-all-start.4 = ((f32[12,16,128]{2,1,0:T(8,128)}), f32[12,16,128]{2,1,0:T(8,128)S(1)}, u32[]{:S(2)}, u32[]{:S(2)}) async-start(f32[12,16,128]{2,1,0:T(8,128)} %bitcast.40), calls=%async_computation.4 | async-start | bytes 196608 | tf_op jit(solution)/shard_map/all_to_all | solution.py:11
  113.6 14.3 %all-to-all-start.5 = ((bf16[12,40,128]{2,1,0:T(8,128)(2,1)}), bf16[12,40,128]{2,1,0:T(8,128)(2,1)S(1)}, u32[]{:S(2)}, u32[]{:S(2)}) async-start(bf16[12,40,128]{2,1,0:T(8,128)(2,1)} %broadcast_in_dim.71), calls=%async_computation.5 | async-start | bytes 245760 | tf_op jit(solution)/shard_map/all_to_all | solution.py:11
  132.3 17.9 %all-to-all-start.6 = ((bf16[8,176,128]{2,1,0:T(8,128)(2,1)}), bf16[8,176,128]{2,1,0:T(8,128)(2,1)S(1)}, u32[]{:S(2)}, u32[]{:S(2)}) async-start(bf16[8,176,128]{2,1,0:T(8,128)(2,1)} %pad_maximum_fusion.2), calls=%async_computation.6 | async-start | bytes 720896 | tf_op jit(solution)/shard_map/all_to_all | solution.py:11
  145.7 8.3 %copy-start.5 = (bf16[16,1024]{1,0:T(8,128)(2,1)}, bf16[16,1024]{1,0:T(8,128)(2,1)S(1)}, u32[]{:S(2)}) copy-start(bf16[16,1024]{1,0:T(8,128)(2,1)S(1)} %copy_bitcast_fusion.4) | copy-start | bytes 98308
  151.8 1.4 copy-start.1

commit v4 on v3

v4 whole, which is shorter than its diff:
```python
import jax
import jax.numpy as jnp
import numpy as np
from jax import lax
from jax.sharding import Mesh, PartitionSpec as P

F32, BF16 = jnp.float32, jnp.bfloat16
LANE = ("x", "c")


def exchange(parts, axis):
    return lax.all_to_all(parts, axis, 0, 0, tiled=True)


def to_all(part, size):
    return jnp.broadcast_to(part[None], (size, *part.shape))


def dot(spec, a, b):
    return jnp.einsum(spec, a, b, preferred_element_type=F32)


def two(a):
    high = a.astype(BF16)
    return jnp.concatenate([high, (a - high.astype(F32)).astype(BF16)], axis=-2)


def per_device(features, w_one, adj_one, list_one, adj_two, list_two, w_two, cotangent):
    cols, sources = features.shape
    blocks, fanout = list_one.shape
    block = adj_one.shape[-1]
    mine, listed = adj_two.shape[:2]
    hid, cls = w_two.shape[1:]
    nodes = lax.axis_size("node")
    xs, cores = lax.axis_size("x"), lax.axis_size("c")
    lanes = xs * cores
    wide = hid // lanes
    by_lane = -(-cls // (8 * lanes)) * 8
    every = by_lane * lanes
    by_z = every // blocks
    kept = -(-cls // 8) * 8
    strip = mine * cores
    strips = block // strip
    mids = blocks // xs
    place, my_x, my_c = (lax.axis_index(axis) for axis in ("z", "x", "c"))
    lists = list_two.reshape(xs, mids, listed)
    lists = lax.dynamic_index_in_dim(lists, place // strips, 1, keepdims=False)

    edges = adj_two.reshape(mine * listed, block)
    cot = jnp.pad(cotangent, ((0, 0), (0, every - by_lane + block - cls)))
    cot = [lax.slice_in_dim(cot, j * by_lane, j * by_lane + block, axis=1) for j in range(lanes)]
    got = exchange(jnp.stack([jnp.concatenate([edges, c], axis=0) for c in cot]), LANE)
    edges = got[:, : mine * listed].reshape(xs, strip, listed, block)
    cot = got[:, mine * listed :].reshape(xs, strip, block)

    tiles = features.reshape(cols, sources // block, block)
    ids = jnp.concatenate([list_one.reshape(-1).astype(jnp.uint32), jnp.arange(blocks, dtype=jnp.uint32)])
    chosen = tiles.at[:, ids].get(mode="promise_in_bounds")
    own = chosen[:, blocks * fanout :].transpose(1, 0, 2)
    chosen = chosen[:, : blocks * fanout].reshape(cols, blocks, fanout, block)
    agg = dot("fhks,hkts->hft", chosen, adj_one).astype(BF16)
    back = dot("xrc,xrks->xkcs", cot, edges)[:, :, :by_lane]
    hits = lists[:, :, None] == jnp.arange(blocks, dtype=jnp.int32)
    back = jnp.where(hits[..., None, None], back[:, :, None], 0.0).sum((0, 1)).astype(BF16)
    at = np.arange(block)
    move = np.zeros((xs, block, strips, block), np.float32)
    for x in range(xs):
        for low in range(strips):
            move[x, :, low] = at[:, None] - low * strip == at - x * strip
            move[x, :, low, : x * strip] = move[x, :, low, (x + 1) * strip :] = 0
    sends = jnp.concatenate([agg, own, back], axis=1).reshape(xs, mids, -1, block)
    sends = dot("xmkl,xlzr->mzkr", sends, jnp.asarray(move, BF16)).astype(BF16)
    sends = sends.reshape(blocks, -1, block)
    weights = w_one.reshape(2, cols, lanes, wide).transpose(0, 2, 1, 3).reshape(-1, wide)
    got = exchange(jnp.concatenate([sends, to_all(weights, blocks)], axis=1), "z")
    inputs, back, weights = jnp.split(got, (2 * cols, 2 * cols + by_lane), axis=1)
    inputs = inputs.reshape(blocks, 2, cols, block)
    weights = weights.reshape(blocks, 2, lanes, cols, wide)
    part = dot("zikr,zijkh->jrh", inputs, weights).astype(BF16)
    back = two(jnp.sum(back.astype(F32), axis=0))

    rows = part.reshape(lanes, lanes, mine, wide).transpose(1, 0, 2, 3)
    rows = rows.reshape(lanes, lanes * mine, wide)
    got = exchange(jnp.concatenate([part, rows, to_all(back, lanes)], axis=1), LANE)
    hidden = jnp.maximum(jnp.sum(got[:, : 2 * block].astype(F32), axis=0), 0.0).astype(BF16)
    rows = hidden[block:].reshape(lanes, mine, wide).transpose(1, 0, 2).reshape(mine, hid)
    hidden = hidden[:block]
    back = got[:, 2 * block :].reshape(lanes, 2, by_lane, block)
    grad = dot("jcr,rh->jch", back[:, 0], hidden) + dot("jcr,rh->jch", back[:, 1], hidden)
    both = dot("rh,ihc->irc", rows, w_two)
    product = jnp.pad(both[0].astype(BF16), ((0, 0), (0, 2 * block - cls)))
    product = jnp.concatenate([product[:, :block], product[:, block:]], axis=0)
    grad = two(grad.reshape(blocks, by_z, wide))
    got = exchange(jnp.concatenate([grad, to_all(product, blocks)], axis=1), "z")
    grad = jnp.sum(got[:, : 2 * by_z].astype(F32), axis=0)
    grad = grad[:by_z] + grad[by_z:]
    grad = jnp.sum(exchange(to_all(grad, nodes), "node"), axis=0).astype(BF16)

    hits = lists[:, :, None] == my_x * mids + jnp.arange(mids, dtype=jnp.int32)
    hits = hits.transpose(0, 2, 1)[:, None, :, :, None]
    near = jnp.where(hits, edges[:, :, None], 0).sum(3).reshape(block, mids * block)
    product = got[:, 2 * by_z :].reshape(mids, strips, 2, 1, mine, block).transpose(0, 1, 3, 4, 2, 5)
    held = my_c == jnp.arange(cores).reshape(1, 1, cores, 1, 1, 1)
    product = jnp.where(held, product, 0).reshape(mids * block, 2 * block)
    logits = dot("rs,sc->rc", near, product).astype(BF16).reshape(lanes, mine, 2 * block)
    logits = [logits[..., :block], logits[..., block:]]

    grad = exchange(to_all(grad, blocks), "z").reshape(every, wide)[:kept]
    got = exchange(jnp.concatenate([to_all(grad, lanes), *logits], axis=1), LANE)
    logits = jnp.sum(got[:, kept:].astype(F32), axis=0)
    logits = jnp.concatenate([logits[:mine], logits[mine:]], axis=1)[:, :cls] + both[1]
    grad = got[:, :cls].transpose(0, 2, 1).reshape(hid, cls).astype(F32)
    return rows, logits, grad


def solution(mesh):
    nodes = mesh.devices.shape[1]
    fine = Mesh(mesh.devices.reshape(4, 12, 2, nodes), ("x", "z", "c", "node"))
    col = ("x", "z", "c")
    rows = ("node", *col)
    in_specs = (
        P(col, "node"),
        P(None, col, None),
        P("node", None, None, None),
        P("node", None),
        P(rows, None, None),
        P("node", None),
        P(),
        P(rows, None),
    )
    out_specs = (P(rows, None), P(rows, None), P())
    return jax.shard_map(
        per_device, mesh=fine, in_specs=in_specs, out_specs=out_specs, check_vma=False
    )
```

time: 155 us -> 155 us (level)
  blocking collectives: 43.4 us -> 29 us
  waiting for transfers between devices: 34.5 us -> 44.4 us
  other arithmetic: 6.54 us -> 16.4 us
  local copies, waits for them, and re-layouts: 17.9 us -> 12.4 us
  matrix products: 7.5 us -> 5.46 us
    psum x1 -> x0, blocking collectives: 14.4 us -> none  [per_device(): grad = lax.psum(grad, 'node').astype(BF16)]
    all_to_all x6, waiting for transfers between devices: 34.5 us -> 44.4 us  [exchange(): return lax.all_to_all(parts, axis, 0, 0, tiled=True)]
    unnamed x0 -> x7, other arithmetic: none -> 9.25 us
    dot_general x11 -> x8, matrix products: 7.5 us -> 5.46 us  [dot(): return jnp.einsum(spec, a, b, preferred_element_type=F32)]
    transpose x3 -> x2, local copies, waits for them, and re-layouts: 2.01 us -> 0.01 us  [the longest x1 0.01 us: per_device(): hidden[block:].reshape(lanes, mine, wide).transpose(1, 0, 2)]
    unnamed x29 -> x18, local copies, waits for them, and re-layouts: 3.5 us -> 1.61 us
  transfers between devices with their start and end apart: 6 -> 6, of which waited for: 5 -> 5; matrix products, arithmetic and copies ran while one was open for 10% -> 7% of each run, Pallas kernels for 0% -> 0%
where the time goes in v4:
time: 155 us; the launch traced here: 153 us
  starting transfers between devices  44.5 us (29%)
  waiting for transfers between devices  44.4 us (29%)
  blocking collectives  29 us (19%)
  other arithmetic  16.4 us (11%)
  local copies, waits for them, and re-layouts  12.4 us (8%)
  matrix products  5.46 us (4%)
    all_to_all x6, starting transfers between devices, exchange(): return lax.all_to_all(parts, axis, 0, 0, tiled=True)  44.5 us
    all_to_all x6, waiting for transfers between devices, exchange(): return lax.all_to_all(parts, axis, 0, 0, tiled=True)  44.4 us
    all_to_all x1, blocking collectives, exchange(): return lax.all_to_all(parts, axis, 0, 0, tiled=True)  29 us
    unnamed x7, other arithmetic  9.25 us
    dot_general x8, matrix products, dot(): return jnp.einsum(spec, a, b, preferred_element_type=F32)  5.46 us
  transfers between devices with their start and end apart: 6, of which 5 were waited for; matrix products, arithmetic and copies ran while one was open for 7% of the time, Pallas kernels for 0%

profile of v4, /device:TPU:1, one launch (start us, length us, event | category | flops | bytes accessed | tf_op | source)
XLA Modules:
  0.0 153.1 jit_solution(7133046660186205767)
XLA Ops:
  0.6 0.0 copy-start
  0.6 1.0 pad_slice_fusion
  1.7 1.3 fusion.12
  3.0 1.3 fusion.13
  4.3 1.3 fusion.14
  5.7 1.3 fusion.15
  7.0 1.3 fusion.16
  8.3 1.3 fusion.17
  9.6 1.3 fusion.18
  10.9 1.3 bitcast_dynamic-update-slice_fusion
  12.2 13.8 %all-to-all-start = ((bf16[8,80,128]{2,1,0:T(8,128)(2,1)}), bf16[8,80,128]{2,1,0:T(8,128)(2,1)S(1)}, u32[]{:S(2)}, u32[]{:S(2)}) async-start(bf16[8,80,128]{2,1,0:T(8,128)(2,1)} %bitcast_dynamic-update-slice_fusion), calls=%async_computation | async-start | bytes 327680 | tf_op jit(solution)/shard_map/all_to_all | solution.py:12
  26.0 0.7 convert_element_type.104
  26.7 0.1 copy.62
  26.8 0.1 concatenate.60
  26.9 0.1 fusion.21
  27.0 1.6 %gather_fusion = bf16[108,8,128]{2,1,0:T(8,128)(2,1)S(1)} fusion(bf16[8,96,128]{2,0,1:T(8,128)(2,1)} %bitcast.180, s32[1024]{0:T(1024)S(1)} %pad_clamp_fusion), kind=kCustom, calls=%fused_computation | custom fusion | bytes 442800 | tf_op jit(solution)/shard_map/gather | solution.py:58
  28.6 0.7 slice.144
  29.3 0.8 reshape.160
  30.0 0.1 constant_dynamic-slice_fusion
  30.1 0.1 copy.63
  30.2 0.0 copy-done
  30.2 1.8 %fusion.2 = bf16[12,8,128]{2,1,0:T(8,128)(2,1)S(1)} fusion(bf16[8,12,8,128]{3,0,2,1:T(8,128)(2,1)} %bitcast.170, bf16[12,8,128,128]{3,2,1,0:T(8,128)(2,1)S(1)} %copy-done), kind=kOutput, calls=%fused_computation.10 | convolution fusion | flops 25178112 | bytes 3366912 | tf_op jit(solution)/shard_map/fhks,hkts->hft/dot_general | solution.py:20
  32.1 0.7 iota_compare_fusion
  32.8 0.0 all-to-all-done
  32.8 0.3 convolution_bitcast_fusion
  33.2 1.0 select_reduce_fusion
  34.2 0.0 copy-done.1
  34.2 0.2 fusion.1
  34.4 0.1 broadcast_in_dim.113
  34.5 29.0 %all_to_all.35 = bf16[12,168,128]{2,1,0:T(8,128)(2,1)S(1)} all-to-all(bf16[12,168,128]{2,1,0:T(8,128)(2,1)S(1)} %pad_maximum_fusion.1), channel_id=1, replica_groups=mesh['x'=4,'z'=12,'c'=2,'node'=8] {'z'}, dimensions={0} | all-to-all | bytes 1032192 | tf_op jit(solution)/shard_map/all_to_all | solution.py:12
  63.6 0.3 fusion
  64.0 0.9 pad_maximum_fusion
  64.8 7.6 %all-to-all-start.2 = ((bf16[8,304,128]{2,1,0:T(8,128)(2,1)}), bf16[8,304,128]{2,1,0:T(8,128)(2,1)}, u32[]{:S(2)}, u32[]{:S(2)}) async-start(bf16[8,304,128]{2,1,0:T(8,128)(2,1)} %pad_maximum_fusion), calls=%async_computation.2 | async-start | bytes 1245184 | tf_op jit(solution)/shard_map/all_to_all | solution.py:12
  72.5 10.6 %all-to-all-done.2 = bf16[8,304,128]{2,1,0:T(8,128)(2,1)} async-done(((bf16[8,304,128]{2,1,0:T(8,128)(2,1)}), bf16[8,304,128]{2,1,0:T(8,128)(2,1)}, u32[]{:S(2)}, u32[]{:S(2)}) %all-to-all-start.2) | async-done | bytes 622624 | tf_op jit(solution)/shard_map/all_to_all | solution.py:12
  83.1 1.1 convert_reduce_fusion
  84.3 0.9 slice.151
  85.2 0.1 fusion.10
  85.4 0.2 convolution_add_fusion
  85.6 1.4 convolution_bitcast_fusion.4
  87.0 0.6 copy-done.3
  87.6 0.7 pad_maximum_fusion.3
  88.3 3.5 %all-to-all-start.3 = ((bf16[12,64,128]{2,1,0:T(8,128)(2,1)}), bf16[12,64,128]{2,1,0:T(8,128)(2,1)S(1)}, u32[]{:S(2)}, u32[]{:S(2)}) async-start(bf16[12,64,128]{2,1,0:T(8,128)(2,1)} %pad_maximum_fusion.3), calls=%async_computation.3 | async-start | bytes 393216 | tf_op jit(solution)/shard_map/all_to_all | solution.py:12
  91.9 0.0 copy-done.7
  91.9 0.1 broadcast_compare_fusion
  92.0 0.1 select_reduce_fusion.1
  92.1 0.7 copy.74
  92.8 11.3 %all-to-all-done.3 = bf16[12,64,128]{2,1,0:T(8,128)(2,1)S(1)} async-done(((bf16[12,64,128]{2,1,0:T(8,128)(2,1)}), bf16[12,64,128]{2,1,0:T(8,128)(2,1)S(1)}, u32[]{:S(2)}, u32[]{:S(2)}) %all-to-all-start.3) | async-done | bytes 196640 | tf_op jit(solution)/shard_map/all_to_all | solution.py:12
  104.2 0.1 copy.75
  104.3 0.6 broadcast_in_dim.116
  104.9 6.8 %all-to-all-start.4 = ((f32[8,16,128]{2,1,0:T(8,128)}), f32[8,16,128]{2,1,0:T(8,128)S(1)}, u32[]{:S(2)}, u32[]{:S(2)}) async-start(f32[8,16,128]{2,1,0:T(8,128)} %broadcast_in_dim.116), calls=%async_computation.4 | async-start | bytes 131072 | tf_op jit(solution)/shard_map/all_to_all | solution.py:12
  111.7 0.2 broadcast_select_fusion
  111.9 1.1 convolution_convert_fusion
  113.0 5.9 %all-to-all-done.4 = f32[8,16,128]{2,1,0:T(8,128)S(1)} async-done(((f32[8,16,128]{2,1,0:T(8,128)}), f32[8,16,128]{2,1,0:T(8,128)S(1)}, u32[]{:S(2)}, u32[]{:S(2)}) %all-to-all-start.4) | async-done | bytes 65568 | tf_op jit(solution)/shard_map/all_to_all | solution.py:12
  119.0 0.6 broadcast_in_dim.117
  119.6 4.1 %all-to-all-start.5 = ((bf16[12,16,128]{2,1,0:T(8,128)(2,1)}), bf16[12,16,128]{2,1,0:T(8,128)(2,1)S(1)}, u32[]{:S(2)}, u32[]{:S(2)}) async-start(bf16[12,16,128]{2,1,0:T(8,128)(2,1)} %broadcast_in_dim.117), calls=%async_computation.5 | async-start | bytes 98304 | tf_op jit(solution)/shard_map/all_to_all | solution.py:12
  123.7 9.8 %all-to-all-done.5 = bf16[12,16,128]{2,1,0:T(8,128)(2,1)S(1)} async-done(((bf16[12,16,128]{2,1,0:T(8,128)(2,1)}), bf16[12,16,128]{2,1,0:T(8,128)(2,1)S(1)}, u32[]{:S(2)}, u32[]{:S(2)}) %all-to-all-start.5) | async-done | bytes 49184 | tf_op jit(solution)/shard_map/all_to_all | solution.py:12
  133.5 0.8 pad_maximum_fusion.2
  134.3 8.7 %all-to-all-start.6 = ((bf16[8,192,128]{2,1,0:T(8,128)(2,1)}), bf16[8,192,128]{2,1,0:T(8,128)(2,1)S(1)}, u32[]{:S(2)}, u32[]{:S(2)}) async-start(bf16[8,192,128]{2,1,0:T(8,128)(2,1)} %pad_maximum_fusion.2), calls=%async_computation.6 | async-start | bytes 786432 | tf_op jit(solution)/shard_map/all_to_all | solution.py:12
  142.9 1.4 copy.114
  144.3 6.7 %all-to-all-done.6 = bf16[8,192,128]{2,1,0:T(8,128)(2,1)S(1)} async-done(((bf16[8,192,128]{2,1,0:T(8,128)(2,1)}), bf16[8,192,128]{2,1,0:T(8,128)(2,1)S(1)}, u32[]{:S(2)}, u32[]{:S(2)}) %all-to-all-start.6) | async-done | bytes 393248 | tf_op jit(solution)/shard_map/all_to_all | solution.py:12
  151.1 0.4 copy.113
  151.5 1.0 copy.92
  152.5 0.0 copy-done.4
  152.5 0.6 fusion.19
  (47 shorter events, 0.6 us)
Async XLA Ops:
  0.6 29.6 %copy-start = (bf16[12,8,128,128]{3,2,1,0:T(8,128)(2,1)S(1)}, bf16[12,8,128,128]{3,2,1,0:T(8,128)(2,1)}, u32[]{:S(2)}) copy-start(bf16[12,8,128,128]{3,2,1,0:T(8,128)(2,1)} %param.11) | copy-start | bytes 9437188
  12.2 20.5 %all-to-all-start = ((bf16[8,80,128]{2,1,0:T(8,128)(2,1)}), bf16[8,80,128]{2,1,0:T(8,128)(2,1)S(1)}, u32[]{:S(2)}, u32[]{:S(2)}) async-start(bf16[8,80,128]{2,1,0:T(8,128)(2,1)} %bitcast_dynamic-update-slice_fusion), calls=%async_computation | async-start | bytes 327680 | tf_op jit(solution)/shard_map/all_to_all | solution.py:12
  30.2 2.5 %copy-start.6 = (s32[4,1,4]{2,0,1:T(4,128)}, s32[4,1,4]{2,0,1:T(4,128)S(1)}, u32[]{:S(2)}) copy-start(s32[4,1,4]{2,0,1:T(4,128)S(1)} %copy.63) | copy-start | bytes 196
  32.1 2.3 %copy-start.5 = (bf16[2,8,1024]{2,1,0:T(8,128)(2,1)S(1)}, bf16[2,8,1024]{2,1,0:T(8,128)(2,1)}, u32[]{:S(2)}) copy-start(bf16[2,8,1024]{2,1,0:T(8,128)(2,1)} %param.10) | copy-start | bytes 98308
  32.8 1.4 copy-start.1
  64.8 27.0 %copy-start.7 = (s32[4,1,4]{2,0,1:T(4,128)S(1)}, s32[4,1,4]{2,0,1:T(4,128)}, u32[]{:S(2)}) copy-start(s32[4,1,4]{2,0,1:T(4,128)} %copy-done.6) | copy-start | bytes 196
  64.8 18.3 %all-to-all-start.2 = ((bf16[8,304,128]{2,1,0:T(8,128)(2,1)}), bf16[8,304,128]{2,1,0:T(8,128)(2,1)}, u32[]{:S(2)}, u32[]{:S(2)}) async-start(bf16[8,304,128]{2,1,0:T(8,128)(2,1)} %pad_maximum_fusion), calls=%async_computation.2 | async-start | bytes 1245184 | tf_op jit(solution)/shard_map/all_to_all | solution.py:12
  84.3 1.3 copy-start.2
  87.0 0.6 copy-start.3
  88.3 15.9 %all-to-all-start.3 = ((bf16[12,64,128]{2,1,0:T(8,128)(2,1)}), bf16[12,64,128]{2,1,0:T(8,128)(2,1)S(1)}, u32[]{:S(2)}, u32[]{:S(2)}) async-start(bf16[12,64,128]{2,1,0:T(8,128)(2,1)} %pad_maximum_fusion.3), calls=%async_computation.3 | async-start | bytes 393216 | tf_op jit(solution)/shard_map/all_to_all | solution.py:12
  104.9 14.0 %all-to-all-start.4 = ((f32[8,16,128]{2,1,0:T(8,128)}), f32[8,16,128]{2,1,0:T(8,128)S(1)}, u32[]{:S(2)}, u32[]{:S(2)}) async-start(f32[8,16,128]{2,1,0:T(8,128)} %broadcast_in_dim.116), calls=%async_computation.4 | async-start | bytes 131072 | tf_op jit(solution)/shard_map/all_to_all | solution.py:12
  119.6 13.9 %all-to-all-start.5 = ((bf16[12,16,128]{2,1,0:T(8,128)(2,1)}), bf16[12,16,128]{2,1,0:T(8,128)(2,1)S(1)}, u32[]{:S(2)}, u32[]{:S(2)}) async-start(bf16[12,16,128]{2,1,0:T(8,128)(2,1)} %broadcast_in_dim.117), calls=%async_computation.5 | async-start | bytes 98304 | tf_op jit(solution)/shard_map/all_to_all | solution.py:12
  134.3 16.8 %all-to-all-start.6 = ((bf16[8,192,128]{2,1,0:T(8,128)(2,1)}), bf16[8,192,128]{2,1,0:T(8,128)(2,1)S(1)}, u32[]{:S(2)}, u32[]{:S(2)}) async-start(bf16[8,192,128]{2,1,0:T(8,128)(2,1)} %pad_maximum_fusion.2), calls=%async_computation.6 | async-start | bytes 786432 | tf_op jit(solution)/shard_map/all_to_all | solution.py:12
  151.0 1.5 copy-start.4

commit v5 on v4

--- a/solution.py
+++ b/solution.py
@@ -43,23 +43,32 @@
     strips = block // strip
     mids = blocks // xs
     place, my_x, my_c = (lax.axis_index(axis) for axis in ("z", "x", "c"))
-    lists = list_two.reshape(xs, mids, listed)
-    lists = lax.dynamic_index_in_dim(lists, place // strips, 1, keepdims=False)
+    my_lane = my_x * cores + my_c
+    mine_of = jnp.arange(blocks) == mids * jnp.arange(xs)[:, None] + place // strips
+    lists = dot("xb,bk->xk", mine_of.astype(BF16), list_two.astype(BF16)).astype(jnp.int32)
 
     edges = adj_two.reshape(mine * listed, block)
-    cot = jnp.pad(cotangent, ((0, 0), (0, every - by_lane + block - cls)))
-    cot = [lax.slice_in_dim(cot, j * by_lane, j * by_lane + block, axis=1) for j in range(lanes)]
-    got = exchange(jnp.stack([jnp.concatenate([edges, c], axis=0) for c in cot]), LANE)
+    cot = jnp.pad(cotangent, ((0, 0), (0, 2 * block - cls)))
+    sends = jnp.concatenate([edges, cot[:, :block], cot[:, block:]], axis=0)
+    got = exchange(to_all(sends, lanes), LANE)
     edges = got[:, : mine * listed].reshape(xs, strip, listed, block)
-    cot = got[:, mine * listed :].reshape(xs, strip, block)
+    cot = got[:, mine * listed :].reshape(xs, cores, 2, mine, block)
+    pick = jnp.arange(2 * block)[:, None] == my_lane * by_lane + jnp.arange(by_lane)
+    pick = pick.reshape(2, block, by_lane).astype(BF16)
+    cot = dot("xchit,hts->xcis", cot, pick).astype(BF16).reshape(xs, strip, by_lane)
 
     tiles = features.reshape(cols, sources // block, block)
-    ids = jnp.concatenate([list_one.reshape(-1).astype(jnp.uint32), jnp.arange(blocks, dtype=jnp.uint32)])
-    chosen = tiles.at[:, ids].get(mode="promise_in_bounds")
-    own = chosen[:, blocks * fanout :].transpose(1, 0, 2)
-    chosen = chosen[:, : blocks * fanout].reshape(cols, blocks, fanout, block)
+    chosen = lax.gather(
+        tiles,
+        list_one.reshape(-1, 1),
+        lax.GatherDimensionNumbers((0, 2), (1,), (1,)),
+        (cols, 1, block),
+        mode="promise_in_bounds",
+    )
+    chosen = chosen.reshape(cols, blocks, fanout, block)
+    own = tiles[:, :blocks].transpose(1, 0, 2)
     agg = dot("fhks,hkts->hft", chosen, adj_one).astype(BF16)
-    back = dot("xrc,xrks->xkcs", cot, edges)[:, :, :by_lane]
+    back = dot("xrc,xrks->xkcs", cot, edges)
     hits = lists[:, :, None] == jnp.arange(blocks, dtype=jnp.int32)
     back = jnp.where(hits[..., None, None], back[:, :, None], 0.0).sum((0, 1)).astype(BF16)
     at = np.arange(block)
@@ -102,12 +111,13 @@
     product = got[:, 2 * by_z :].reshape(mids, strips, 2, 1, mine, block).transpose(0, 1, 3, 4, 2, 5)
     held = my_c == jnp.arange(cores).reshape(1, 1, cores, 1, 1, 1)
     product = jnp.where(held, product, 0).reshape(mids * block, 2 * block)
-    logits = dot("rs,sc->rc", near, product).astype(BF16).reshape(lanes, mine, 2 * block)
-    logits = [logits[..., :block], logits[..., block:]]
+    logits = dot("rs,sc->rc", near, product).reshape(lanes, mine, 2 * block)
+    logits = jnp.concatenate([logits[..., :block], logits[..., block:]], axis=1)
 
     grad = exchange(to_all(grad, blocks), "z").reshape(every, wide)[:kept]
-    got = exchange(jnp.concatenate([to_all(grad, lanes), *logits], axis=1), LANE)
+    got = exchange(jnp.concatenate([to_all(grad, lanes), two(logits)], axis=1), LANE)
     logits = jnp.sum(got[:, kept:].astype(F32), axis=0)
+    logits = logits[: 2 * mine] + logits[2 * mine :]
     logits = jnp.concatenate([logits[:mine], logits[mine:]], axis=1)[:, :cls] + both[1]
     grad = got[:, :cls].transpose(0, 2, 1).reshape(hid, cls).astype(F32)
     return rows, logits, grad

time: 155 us -> 151 us (0.974)
  other arithmetic: 16.4 us -> 9.45 us
  matrix products: 5.46 us -> 7.13 us
    unnamed x7 -> x0, other arithmetic: 9.25 us -> none
    dot_general x8 -> x10, matrix products: 5.46 us -> 7.13 us  [dot(): return jnp.einsum(spec, a, b, preferred_element_type=F32)]
  transfers between devices with their start and end apart: 6 -> 6, of which waited for: 5 -> 5; matrix products, arithmetic and copies ran while one was open for 7% -> 6% of each run, Pallas kernels for 0% -> 0%
where the time goes in v5:
time: 151 us; the launch traced here: 150 us
  waiting for transfers between devices  45.8 us (30%)
  starting transfers between devices  45.2 us (30%)
  blocking collectives  28.8 us (19%)
  local copies, waits for them, and re-layouts  12.2 us (8%)
  other arithmetic  9.45 us (6%)
  matrix products  7.13 us (5%)
    all_to_all x6, waiting for transfers between devices, exchange(): return lax.all_to_all(parts, axis, 0, 0, tiled=True)  45.8 us
    all_to_all x6, starting transfers between devices, exchange(): return lax.all_to_all(parts, axis, 0, 0, tiled=True)  45.2 us
    all_to_all x1, blocking collectives, exchange(): return lax.all_to_all(parts, axis, 0, 0, tiled=True)  28.8 us
    dot_general x10, matrix products, dot(): return jnp.einsum(spec, a, b, preferred_element_type=F32)  7.13 us
  transfers between devices with their start and end apart: 6, of which 5 were waited for; matrix products, arithmetic and copies ran while one was open for 6% of the time, Pallas kernels for 0%

profile of v5, /device:TPU:1, one launch (start us, length us, event | category | flops | bytes accessed | tf_op | source)
XLA Modules:
  0.0 149.7 jit_solution(10258368193455196957)
XLA Ops:
  0.6 0.0 copy-start
  0.6 0.9 fusion.22
  1.5 0.8 pad_maximum_fusion.6
  2.3 0.7 broadcast_in_dim.119
  3.0 13.8 %all-to-all-start = ((bf16[8,96,128]{2,1,0:T(8,128)(2,1)}), bf16[8,96,128]{2,1,0:T(8,128)(2,1)S(1)}, u32[]{:S(2)}, u32[]{:S(2)}) async-start(bf16[8,96,128]{2,1,0:T(8,128)(2,1)} %broadcast_in_dim.119), calls=%async_computation | async-start | bytes 393216 | tf_op jit(solution)/shard_map/all_to_all | solution.py:12
  16.9 0.8 copy.61
  17.6 0.1 reshape.184
  17.7 1.3 slice_bitcast_fusion.8
  19.1 1.6 %gather_fusion = bf16[96,8,128]{2,1,0:T(8,128)(2,1)S(1)} fusion(bf16[8,96,128]{2,0,1:T(8,128)(2,1)} %bitcast.141, s32[1024]{0:T(1024)S(1)} %pad_clamp_fusion), kind=kCustom, calls=%fused_computation | custom fusion | bytes 393600 | tf_op jit(solution)/shard_map/gather | solution.py:61
  20.7 0.9 convolution_convert_fusion
  21.6 0.0 copy-done
  21.6 1.5 %fusion.3 = bf16[12,8,128]{2,1,0:T(8,128)(2,1)} fusion(bf16[8,12,8,128]{3,0,2,1:T(8,128)(2,1)S(1)} %bitcast.129, bf16[12,8,128,128]{3,2,1,0:T(8,128)(2,1)S(1)} %copy-done), kind=kOutput, calls=%fused_computation.11 | convolution fusion | flops 25178112 | bytes 3366912 | tf_op jit(solution)/shard_map/fhks,hkts->hft/dot_general | solution.py:20
  23.1 0.1 iota_compare_fusion
  23.2 0.0 all-to-all-done
  23.2 0.2 fusion.2
  23.4 0.2 convolution_bitcast_fusion.2
  23.6 0.3 select_reduce_fusion
  23.9 0.8 pad_maximum_fusion.5
  24.7 1.3 fusion.1
  26.0 0.8 broadcast_in_dim.123
  26.9 28.8 %all_to_all.35 = bf16[12,168,128]{2,1,0:T(8,128)(2,1)S(1)} all-to-all(bf16[12,168,128]{2,1,0:T(8,128)(2,1)S(1)} %pad_maximum_fusion.1), channel_id=1, replica_groups=mesh['x'=4,'z'=12,'c'=2,'node'=8] {'z'}, dimensions={0} | all-to-all | bytes 1032192 | tf_op jit(solution)/shard_map/all_to_all | solution.py:12
  55.7 0.3 fusion
  56.1 0.9 pad_maximum_fusion
  56.9 7.7 %all-to-all-start.2 = ((bf16[8,304,128]{2,1,0:T(8,128)(2,1)}), bf16[8,304,128]{2,1,0:T(8,128)(2,1)}, u32[]{:S(2)}, u32[]{:S(2)}) async-start(bf16[8,304,128]{2,1,0:T(8,128)(2,1)} %pad_maximum_fusion), calls=%async_computation.2 | async-start | bytes 1245184 | tf_op jit(solution)/shard_map/all_to_all | solution.py:12
  64.6 10.6 %all-to-all-done.2 = bf16[8,304,128]{2,1,0:T(8,128)(2,1)} async-done(((bf16[8,304,128]{2,1,0:T(8,128)(2,1)}), bf16[8,304,128]{2,1,0:T(8,128)(2,1)}, u32[]{:S(2)}, u32[]{:S(2)}) %all-to-all-start.2) | async-done | bytes 622624 | tf_op jit(solution)/shard_map/all_to_all | solution.py:12
  75.3 1.1 convert_reduce_fusion
  76.4 0.0 copy-start.1
  76.4 0.6 copy-done.1
  77.1 1.4 convolution_bitcast_fusion.5
  78.5 0.9 slice.127
  79.4 0.1 fusion.8
  79.5 0.2 convolution_add_fusion
  79.7 0.0 copy-done.3
  79.8 0.7 pad_maximum_fusion.3
  80.5 3.5 %all-to-all-start.3 = ((bf16[12,64,128]{2,1,0:T(8,128)(2,1)}), bf16[12,64,128]{2,1,0:T(8,128)(2,1)S(1)}, u32[]{:S(2)}, u32[]{:S(2)}) async-start(bf16[12,64,128]{2,1,0:T(8,128)(2,1)} %pad_maximum_fusion.3), calls=%async_computation.3 | async-start | bytes 393216 | tf_op jit(solution)/shard_map/all_to_all | solution.py:12
  84.0 0.1 broadcast_compare_fusion
  84.1 0.1 select_reduce_fusion.1
  84.3 0.1 copy.73
  84.3 0.7 dot_general.41
  85.0 11.3 %all-to-all-done.3 = bf16[12,64,128]{2,1,0:T(8,128)(2,1)S(1)} async-done(((bf16[12,64,128]{2,1,0:T(8,128)(2,1)}), bf16[12,64,128]{2,1,0:T(8,128)(2,1)S(1)}, u32[]{:S(2)}, u32[]{:S(2)}) %all-to-all-start.3) | async-done | bytes 196640 | tf_op jit(solution)/shard_map/all_to_all | solution.py:12
  96.4 0.1 copy.74
  96.4 0.6 broadcast_in_dim.126
  97.1 6.8 %all-to-all-start.4 = ((f32[8,16,128]{2,1,0:T(8,128)}), f32[8,16,128]{2,1,0:T(8,128)}, u32[]{:S(2)}, u32[]{:S(2)}) async-start(f32[8,16,128]{2,1,0:T(8,128)} %broadcast_in_dim.126), calls=%async_computation.4 | async-start | bytes 131072 | tf_op jit(solution)/shard_map/all_to_all | solution.py:12
  103.9 0.2 broadcast_select_fusion
  104.1 0.1 reshape.202
  104.3 0.0 copy-start.2
  104.3 1.1 fusion.23
  105.4 5.9 %all-to-all-done.4 = f32[8,16,128]{2,1,0:T(8,128)} async-done(((f32[8,16,128]{2,1,0:T(8,128)}), f32[8,16,128]{2,1,0:T(8,128)}, u32[]{:S(2)}, u32[]{:S(2)}) %all-to-all-start.4) | async-done | bytes 65568 | tf_op jit(solution)/shard_map/all_to_all | solution.py:12
  111.3 0.9 reduce_sum.70
  112.1 0.6 broadcast_in_dim.127
  112.7 4.1 %all-to-all-start.5 = ((bf16[12,16,128]{2,1,0:T(8,128)(2,1)}), bf16[12,16,128]{2,1,0:T(8,128)(2,1)S(1)}, u32[]{:S(2)}, u32[]{:S(2)}) async-start(bf16[12,16,128]{2,1,0:T(8,128)(2,1)} %broadcast_in_dim.127), calls=%async_computation.5 | async-start | bytes 98304 | tf_op jit(solution)/shard_map/all_to_all | solution.py:12
  116.9 9.7 %all-to-all-done.5 = bf16[12,16,128]{2,1,0:T(8,128)(2,1)S(1)} async-done(((bf16[12,16,128]{2,1,0:T(8,128)(2,1)}), bf16[12,16,128]{2,1,0:T(8,128)(2,1)S(1)}, u32[]{:S(2)}, u32[]{:S(2)}) %all-to-all-start.5) | async-done | bytes 49184 | tf_op jit(solution)/shard_map/all_to_all | solution.py:12
  126.6 0.8 pad_maximum_fusion.2
  127.4 9.3 %all-to-all-start.6 = ((bf16[8,224,128]{2,1,0:T(8,128)(2,1)}), bf16[8,224,128]{2,1,0:T(8,128)(2,1)}, u32[]{:S(2)}, u32[]{:S(2)}) async-start(bf16[8,224,128]{2,1,0:T(8,128)(2,1)} %pad_maximum_fusion.2), calls=%async_computation.6 | async-start | bytes 917504 | tf_op jit(solution)/shard_map/all_to_all | solution.py:12
  136.8 0.0 copy-done.2
  136.8 0.6 copy.107
  137.4 8.3 %all-to-all-done.6 = bf16[8,224,128]{2,1,0:T(8,128)(2,1)} async-done(((bf16[8,224,128]{2,1,0:T(8,128)(2,1)}), bf16[8,224,128]{2,1,0:T(8,128)(2,1)}, u32[]{:S(2)}, u32[]{:S(2)}) %all-to-all-start.6) | async-done | bytes 458784 | tf_op jit(solution)/shard_map/all_to_all | solution.py:12
  145.7 0.9 convert_reduce_fusion.1
  146.6 0.0 copy-start.4
  146.6 1.0 convert_bitcast_fusion
  147.7 0.4 copy.106
  148.1 1.0 copy.93
  149.0 0.0 copy-done.4
  149.0 0.6 fusion.12
  (37 shorter events, 0.5 us)
Async XLA Ops:
  0.6 20.9 %copy-start = (bf16[12,8,128,128]{3,2,1,0:T(8,128)(2,1)S(1)}, bf16[12,8,128,128]{3,2,1,0:T(8,128)(2,1)}, u32[]{:S(2)}) copy-start(bf16[12,8,128,128]{3,2,1,0:T(8,128)(2,1)} %param.11) | copy-start | bytes 9437188
  3.0 20.1 %all-to-all-start = ((bf16[8,96,128]{2,1,0:T(8,128)(2,1)}), bf16[8,96,128]{2,1,0:T(8,128)(2,1)S(1)}, u32[]{:S(2)}, u32[]{:S(2)}) async-start(bf16[8,96,128]{2,1,0:T(8,128)(2,1)} %broadcast_in_dim.119), calls=%async_computation | async-start | bytes 393216 | tf_op jit(solution)/shard_map/all_to_all | solution.py:12
  56.9 18.3 %all-to-all-start.2 = ((bf16[8,304,128]{2,1,0:T(8,128)(2,1)}), bf16[8,304,128]{2,1,0:T(8,128)(2,1)}, u32[]{:S(2)}, u32[]{:S(2)}) async-start(bf16[8,304,128]{2,1,0:T(8,128)(2,1)} %pad_maximum_fusion), calls=%async_computation.2 | async-start | bytes 1245184 | tf_op jit(solution)/shard_map/all_to_all | solution.py:12
  76.4 0.6 copy-start.1
  78.4 1.3 copy-start.3
  80.5 15.9 %all-to-all-start.3 = ((bf16[12,64,128]{2,1,0:T(8,128)(2,1)}), bf16[12,64,128]{2,1,0:T(8,128)(2,1)S(1)}, u32[]{:S(2)}, u32[]{:S(2)}) async-start(bf16[12,64,128]{2,1,0:T(8,128)(2,1)} %pad_maximum_fusion.3), calls=%async_computation.3 | async-start | bytes 393216 | tf_op jit(solution)/shard_map/all_to_all | solution.py:12
  97.1 14.2 %all-to-all-start.4 = ((f32[8,16,128]{2,1,0:T(8,128)}), f32[8,16,128]{2,1,0:T(8,128)}, u32[]{:S(2)}, u32[]{:S(2)}) async-start(f32[8,16,128]{2,1,0:T(8,128)} %broadcast_in_dim.126), calls=%async_computation.4 | async-start | bytes 131072 | tf_op jit(solution)/shard_map/all_to_all | solution.py:12
  104.3 32.5 %copy-start.2 = (bf16[128,128]{1,0:T(8,128)(2,1)S(1)}, bf16[128,128]{1,0:T(8,128)(2,1)}, u32[]{:S(2)}) copy-start(bf16[128,128]{1,0:T(8,128)(2,1)} %copy-done.1) | copy-start | bytes 98308
  112.7 13.9 %all-to-all-start.5 = ((bf16[12,16,128]{2,1,0:T(8,128)(2,1)}), bf16[12,16,128]{2,1,0:T(8,128)(2,1)S(1)}, u32[]{:S(2)}, u32[]{:S(2)}) async-start(bf16[12,16,128]{2,1,0:T(8,128)(2,1)} %broadcast_in_dim.127), calls=%async_computation.5 | async-start | bytes 98304 | tf_op jit(solution)/shard_map/all_to_all | solution.py:12
  127.4 18.2 %all-to-all-start.6 = ((bf16[8,224,128]{2,1,0:T(8,128)(2,1)}), bf16[8,224,128]{2,1,0:T(8,128)(2,1)}, u32[]{:S(2)}, u32[]{:S(2)}) async-start(bf16[8,224,128]{2,1,0:T(8,128)(2,1)} %pad_maximum_fusion.2), calls=%async_computation.6 | async-start | bytes 917504 | tf_op jit(solution)/shard_map/all_to_all | solution.py:12
  146.6 2.4 %copy-start.4 = (f32[2,16,153]{2,1,0:T(8,128)S(1)}, f32[2,16,153]{2,1,0:T(8,128)}, u32[]{:S(2)}) copy-start(f32[2,16,153]{2,1,0:T(8,128)} %copy-done.3) | copy-start | bytes 58756

commit v6 on v5

--- a/solution.py
+++ b/solution.py
@@ -2,6 +2,8 @@
 import jax.numpy as jnp
 import numpy as np
 from jax import lax
+from jax.experimental import pallas as pl
+from jax.experimental.pallas import tpu as pltpu
 from jax.sharding import Mesh, PartitionSpec as P
 
 F32, BF16 = jnp.float32, jnp.bfloat16
@@ -23,6 +25,49 @@
 def two(a):
     high = a.astype(BF16)
     return jnp.concatenate([high, (a - high.astype(F32)).astype(BF16)], axis=-2)
+
+
+def middle(got, w, sends, rows, logits):
+    lanes, wide = got.shape[0], got.shape[2]
+    blocks, by_z = sends.shape[0], sends.shape[1] // 4
+    block, mine = got.shape[2], rows.shape[0]
+    pre = got[0, : 2 * block].astype(F32)
+    for j in range(1, lanes):
+        pre = pre + got[j, : 2 * block].astype(F32)
+    hidden = jnp.maximum(pre, 0.0).astype(BF16)
+    for j in range(lanes):
+        rows[:, j * wide : (j + 1) * wide] = hidden[block + j * mine : block + (j + 1) * mine]
+    hidden = hidden[:block]
+    back = got[:, 2 * block :].astype(F32)
+    half = back.shape[1] // 2
+    back = (back[:, :half] + back[:, half:]).reshape(lanes * half, block)
+    high = back.astype(BF16)
+    low = (back - high.astype(F32)).astype(BF16)
+    grad = jnp.dot(high, hidden, preferred_element_type=F32)
+    grad = grad + jnp.dot(low, hidden, preferred_element_type=F32)
+    grad = grad.reshape(blocks, by_z, wide)
+    high = grad.astype(BF16)
+    sends[:, :by_z] = high
+    sends[:, by_z : 2 * by_z] = (grad - high.astype(F32)).astype(BF16)
+    over = (((1,), (1,)), ((), ()))
+    product = lax.dot_general(rows[...], w[0], over, preferred_element_type=F32).astype(BF16)
+    logits[...] = lax.dot_general(rows[...], w[1], over, preferred_element_type=F32)
+    for z in range(blocks):
+        sends[z, 2 * by_z : 2 * by_z + mine] = product[:, :block]
+        sends[z, 2 * by_z + mine :] = product[:, block:]
+
+
+def finish(got, own, logits, grad):
+    lanes, wide = got.shape[0], got.shape[2]
+    mine, cls = logits.shape
+    kept = got.shape[1] - 2 * mine
+    part = got[0, kept:].astype(F32)
+    for j in range(1, lanes):
+        part = part + got[j, kept:].astype(F32)
+    part = jnp.concatenate([part[:mine], part[mine:]], axis=1) + own[...]
+    logits[...] = part[:, :cls]
+    for j in range(lanes):
+        grad[:, j * wide : (j + 1) * wide] = got[j, :kept].astype(F32)[:cls]
 
 
 def per_device(features, w_one, adj_one, list_one, adj_two, list_two, w_two, cotangent):
@@ -91,16 +136,17 @@
     rows = part.reshape(lanes, lanes, mine, wide).transpose(1, 0, 2, 3)
     rows = rows.reshape(lanes, lanes * mine, wide)
     got = exchange(jnp.concatenate([part, rows, to_all(back, lanes)], axis=1), LANE)
-    hidden = jnp.maximum(jnp.sum(got[:, : 2 * block].astype(F32), axis=0), 0.0).astype(BF16)
-    rows = hidden[block:].reshape(lanes, mine, wide).transpose(1, 0, 2).reshape(mine, hid)
-    hidden = hidden[:block]
-    back = got[:, 2 * block :].reshape(lanes, 2, by_lane, block)
-    grad = dot("jcr,rh->jch", back[:, 0], hidden) + dot("jcr,rh->jch", back[:, 1], hidden)
-    both = dot("rh,ihc->irc", rows, w_two)
-    product = jnp.pad(both[0].astype(BF16), ((0, 0), (0, 2 * block - cls)))
-    product = jnp.concatenate([product[:, :block], product[:, block:]], axis=0)
-    grad = two(grad.reshape(blocks, by_z, wide))
-    got = exchange(jnp.concatenate([grad, to_all(product, blocks)], axis=1), "z")
+    w = jnp.pad(w_two.transpose(0, 2, 1), ((0, 0), (0, 2 * block - cls), (0, 0)))
+    sends, rows, own_logits = pl.pallas_call(
+        middle,
+        out_shape=(
+            jax.ShapeDtypeStruct((blocks, 4 * by_z, block), BF16),
+            jax.ShapeDtypeStruct((mine, hid), BF16),
+            jax.ShapeDtypeStruct((mine, 2 * block), F32),
+        ),
+        compiler_params=pltpu.CompilerParams(vmem_limit_bytes=16 * 2**20),
+    )(got, w)
+    got = exchange(sends, "z")
     grad = jnp.sum(got[:, : 2 * by_z].astype(F32), axis=0)
     grad = grad[:by_z] + grad[by_z:]
     grad = jnp.sum(exchange(to_all(grad, nodes), "node"), axis=0).astype(BF16)
@@ -115,12 +161,16 @@
     logits = jnp.concatenate([logits[..., :block], logits[..., block:]], axis=1)
 
     grad = exchange(to_all(grad, blocks), "z").reshape(every, wide)[:kept]
-    got = exchange(jnp.concatenate([to_all(grad, lanes), two(logits)], axis=1), LANE)
-    logits = jnp.sum(got[:, kept:].astype(F32), axis=0)
-    logits = logits[: 2 * mine] + logits[2 * mine :]
-    logits = jnp.concatenate([logits[:mine], logits[mine:]], axis=1)[:, :cls] + both[1]
-    grad = got[:, :cls].transpose(0, 2, 1).reshape(hid, cls).astype(F32)
-    return rows, logits, grad
+    got = exchange(jnp.concatenate([to_all(grad, lanes), logits.astype(BF16)], axis=1), LANE)
+    logits, grad = pl.pallas_call(
+        finish,
+        out_shape=(
+            jax.ShapeDtypeStruct((mine, cls), F32),
+            jax.ShapeDtypeStruct((cls, hid), F32),
+        ),
+        compiler_params=pltpu.CompilerParams(vmem_limit_bytes=16 * 2**20),
+    )(got, own_logits)
+    return rows, logits, grad.T
 
 
 def solution(mesh):

time: 151 us -> 143 us (0.947)
  blocking collectives: 28.8 us -> 44.6 us
  waiting for transfers between devices: 45.8 us -> 35.2 us
  starting transfers between devices: 45.2 us -> 35.9 us
  other arithmetic: 9.45 us -> 4.23 us
  Pallas kernels: 0 us -> 3.12 us
  matrix products: 7.13 us -> 5.45 us
    all_to_all x1 -> x2, blocking collectives: 28.8 us -> 44.6 us  [exchange(): return lax.all_to_all(parts, axis, 0, 0, tiled=True)]
    all_to_all x6 -> x5, waiting for transfers between devices: 45.8 us -> 35.2 us  [exchange(): return lax.all_to_all(parts, axis, 0, 0, tiled=True)]
    all_to_all x6 -> x5, starting transfers between devices: 45.2 us -> 35.9 us  [exchange(): return lax.all_to_all(parts, axis, 0, 0, tiled=True)]
    pallas_call x0 -> x2, Pallas kernels: none -> 3.12 us  [the longest x1 2.2 us: per_device(): pl.pallas_call(middle, out_shape=(jax.ShapeDtypeStruct((blocks, 4 * by_z,...]
    reduce_sum x2 -> x0, other arithmetic: 2.04 us -> none  [the longest x1 1.11 us: per_device(): jnp.sum(got[:, :2 * block].astype(F32), axis=0)]
    dot_general x10 -> x7, matrix products: 7.13 us -> 5.45 us  [dot(): return jnp.einsum(spec, a, b, preferred_element_type=F32)]
    unnamed x13 -> x6, local copies, waits for them, and re-layouts: 2.4 us -> 3.23 us
  transfers between devices with their start and end apart: 6 -> 5, of which waited for: 5 -> 4; matrix products, arithmetic and copies ran while one was open for 6% -> 8% of each run, Pallas kernels for 0% -> 0%
where the time goes in v6:
time: 143 us; the launch traced here: 142 us
  blocking collectives  44.6 us (31%)
  starting transfers between devices  35.9 us (25%)
  waiting for transfers between devices  35.2 us (25%)
  local copies, waits for them, and re-layouts  12.2 us (9%)
  matrix products  5.45 us (4%)
  other arithmetic  4.23 us (3%)
  Pallas kernels  3.12 us (2%)
    all_to_all x2, blocking collectives, exchange(): return lax.all_to_all(parts, axis, 0, 0, tiled=True)  44.6 us
    all_to_all x5, starting transfers between devices, exchange(): return lax.all_to_all(parts, axis, 0, 0, tiled=True)  35.9 us
    all_to_all x5, waiting for transfers between devices, exchange(): return lax.all_to_all(parts, axis, 0, 0, tiled=True)  35.2 us
    dot_general x7, matrix products, dot(): return jnp.einsum(spec, a, b, preferred_element_type=F32)  5.45 us
    unnamed x6, local copies, waits for them, and re-layouts  3.23 us
  transfers between devices with their start and end apart: 5, of which 4 were waited for; matrix products, arithmetic and copies ran while one was open for 8% of the time, Pallas kernels for 0%

profile of v6, /device:TPU:1, one launch (start us, length us, event | category | flops | bytes accessed | tf_op | source)
XLA Modules:
  0.0 141.6 jit_solution(5365554900515010445)
XLA Ops:
  0.6 0.0 copy-start
  0.6 0.9 fusion.15
  1.5 0.8 pad_maximum_fusion.4
  2.3 0.7 broadcast_in_dim.113
  3.0 13.8 %all-to-all-start = ((bf16[8,96,128]{2,1,0:T(8,128)(2,1)}), bf16[8,96,128]{2,1,0:T(8,128)(2,1)S(1)}, u32[]{:S(2)}, u32[]{:S(2)}) async-start(bf16[8,96,128]{2,1,0:T(8,128)(2,1)} %broadcast_in_dim.113), calls=%async_computation | async-start | bytes 393216 | tf_op jit(solution)/shard_map/all_to_all | solution.py:14
  16.9 0.8 copy.38
  17.6 0.1 reshape.162
  17.7 1.3 slice_bitcast_fusion.1
  19.1 1.6 %gather_fusion = bf16[96,8,128]{2,1,0:T(8,128)(2,1)S(1)} fusion(bf16[8,96,128]{2,0,1:T(8,128)(2,1)} %bitcast.97, s32[1024]{0:T(1024)S(1)} %pad_clamp_fusion), kind=kCustom, calls=%fused_computation | custom fusion | bytes 393600 | tf_op jit(solution)/shard_map/gather | solution.py:106
  20.7 0.9 convolution_convert_fusion.1
  21.5 0.0 copy-done
  21.6 1.5 %fusion.3 = bf16[12,8,128]{2,1,0:T(8,128)(2,1)} fusion(bf16[8,12,8,128]{3,0,2,1:T(8,128)(2,1)S(1)} %bitcast.91, bf16[12,8,128,128]{3,2,1,0:T(8,128)(2,1)S(1)} %copy-done), kind=kOutput, calls=%fused_computation.11 | convolution fusion | flops 25178112 | bytes 3366912 | tf_op jit(solution)/shard_map/fhks,hkts->hft/dot_general | solution.py:22
  23.1 0.1 iota_compare_fusion
  23.2 0.0 all-to-all-done
  23.2 0.2 fusion.2
  23.4 0.2 convolution_bitcast_fusion.2
  23.6 0.3 select_reduce_fusion
  23.9 0.8 pad_maximum_fusion.3
  24.7 1.3 fusion.1
  26.0 0.8 broadcast_in_dim.117
  26.9 28.8 %all_to_all.35 = bf16[12,168,128]{2,1,0:T(8,128)(2,1)S(1)} all-to-all(bf16[12,168,128]{2,1,0:T(8,128)(2,1)S(1)} %pad_maximum_fusion.1), channel_id=1, replica_groups=mesh['x'=4,'z'=12,'c'=2,'node'=8] {'z'}, dimensions={0} | all-to-all | bytes 1032192 | tf_op jit(solution)/shard_map/all_to_all | solution.py:14
  55.7 0.3 fusion
  56.1 0.9 pad_maximum_fusion
  56.9 7.7 %all-to-all-start.2 = ((bf16[8,304,128]{2,1,0:T(8,128)(2,1)}), bf16[8,304,128]{2,1,0:T(8,128)(2,1)}, u32[]{:S(2)}, u32[]{:S(2)}) async-start(bf16[8,304,128]{2,1,0:T(8,128)(2,1)} %pad_maximum_fusion), calls=%async_computation.2 | async-start | bytes 1245184 | tf_op jit(solution)/shard_map/all_to_all | solution.py:14
  64.6 1.2 copy.72
  65.8 1.1 pad.9.w
  66.9 8.3 %all-to-all-done.2.got = bf16[8,304,128]{2,1,0:T(8,128)(2,1)} async-done(((bf16[8,304,128]{2,1,0:T(8,128)(2,1)}), bf16[8,304,128]{2,1,0:T(8,128)(2,1)}, u32[]{:S(2)}, u32[]{:S(2)}) %all-to-all-start.2) | async-done | bytes 622624 | tf_op jit(solution)/shard_map/all_to_all | solution.py:14
  75.3 0.0 copy-start.1
  75.3 1.2 copy-done.1
  76.5 2.2 %shard_map.112 = (bf16[12,64,128]{2,1,0:T(8,128)(2,1)}, bf16[16,1024]{1,0:T(8,128)(2,1)}, f32[16,256]{1,0:T(8,128)S(1)}) custom-call(bf16[8,304,128]{2,1,0:T(8,128)(2,1)} %all-to-all-done.2.got, bf16[2,256,1024]{2,1,0:T(8,128)(2,1)S(1)} %copy-done.1), custom_call_target="tpu_custom_call" | custom-call | tf_op jit(solution)/shard_map/pallas_call | solution.py:140
  78.7 3.5 %all-to-all-start.3 = ((bf16[12,64,128]{2,1,0:T(8,128)(2,1)}), bf16[12,64,128]{2,1,0:T(8,128)(2,1)S(1)}, u32[]{:S(2)}, u32[]{:S(2)}) async-start(bf16[12,64,128]{2,1,0:T(8,128)(2,1)} %get-tuple-element.9), calls=%async_computation.3 | async-start | bytes 393216 | tf_op jit(solution)/shard_map/all_to_all | solution.py:14
  82.2 0.1 broadcast_compare_fusion
  82.3 0.1 select_reduce_fusion.1
  82.5 0.1 copy.47
  82.6 0.7 dot_general.29
  83.3 11.3 %all-to-all-done.3 = bf16[12,64,128]{2,1,0:T(8,128)(2,1)S(1)} async-done(((bf16[12,64,128]{2,1,0:T(8,128)(2,1)}), bf16[12,64,128]{2,1,0:T(8,128)(2,1)S(1)}, u32[]{:S(2)}, u32[]{:S(2)}) %all-to-all-start.3) | async-done | bytes 196640 | tf_op jit(solution)/shard_map/all_to_all | solution.py:14
  94.6 0.1 copy.48
  94.7 0.6 broadcast_in_dim.119
  95.3 6.8 %all-to-all-start.4 = ((f32[8,16,128]{2,1,0:T(8,128)}), f32[8,16,128]{2,1,0:T(8,128)}, u32[]{:S(2)}, u32[]{:S(2)}) async-start(f32[8,16,128]{2,1,0:T(8,128)} %broadcast_in_dim.119), calls=%async_computation.4 | async-start | bytes 131072 | tf_op jit(solution)/shard_map/all_to_all | solution.py:14
  102.1 0.2 broadcast_select_fusion
  102.3 0.1 reshape.178
  102.5 1.1 convolution_convert_fusion
  103.6 5.9 %all-to-all-done.4 = f32[8,16,128]{2,1,0:T(8,128)} async-done(((f32[8,16,128]{2,1,0:T(8,128)}), f32[8,16,128]{2,1,0:T(8,128)}, u32[]{:S(2)}, u32[]{:S(2)}) %all-to-all-start.4) | async-done | bytes 65568 | tf_op jit(solution)/shard_map/all_to_all | solution.py:14
  109.5 0.9 reduce_sum.51
  110.3 0.6 broadcast_in_dim.120
  110.9 4.1 %all-to-all-start.5 = ((bf16[12,16,128]{2,1,0:T(8,128)(2,1)}), bf16[12,16,128]{2,1,0:T(8,128)(2,1)S(1)}, u32[]{:S(2)}, u32[]{:S(2)}) async-start(bf16[12,16,128]{2,1,0:T(8,128)(2,1)} %broadcast_in_dim.120), calls=%async_computation.5 | async-start | bytes 98304 | tf_op jit(solution)/shard_map/all_to_all | solution.py:14
  115.1 9.8 %all-to-all-done.5 = bf16[12,16,128]{2,1,0:T(8,128)(2,1)S(1)} async-done(((bf16[12,16,128]{2,1,0:T(8,128)(2,1)}), bf16[12,16,128]{2,1,0:T(8,128)(2,1)S(1)}, u32[]{:S(2)}, u32[]{:S(2)}) %all-to-all-start.5) | async-done | bytes 49184 | tf_op jit(solution)/shard_map/all_to_all | solution.py:14
  124.9 15.8 %all_to_all.36.got = bf16[8,192,128]{2,1,0:T(8,128)(2,1)S(1)} all-to-all(bf16[8,192,128]{2,1,0:T(8,128)(2,1)S(1)} %pad_maximum_fusion.2), channel_id=1, replica_groups=mesh['x'=4,'z'=12,'c'=2,'node'=8] {'x','c'}, dimensions={0} | all-to-all | bytes 786432 | tf_op jit(solution)/shard_map/all_to_all | solution.py:14
  140.7 0.9 shard_map.113
  (23 shorter events, 0.3 us)
Async XLA Ops:
  0.6 20.9 %copy-start = (bf16[12,8,128,128]{3,2,1,0:T(8,128)(2,1)S(1)}, bf16[12,8,128,128]{3,2,1,0:T(8,128)(2,1)}, u32[]{:S(2)}) copy-start(bf16[12,8,128,128]{3,2,1,0:T(8,128)(2,1)} %param.11) | copy-start | bytes 9437188
  3.0 20.1 %all-to-all-start = ((bf16[8,96,128]{2,1,0:T(8,128)(2,1)}), bf16[8,96,128]{2,1,0:T(8,128)(2,1)S(1)}, u32[]{:S(2)}, u32[]{:S(2)}) async-start(bf16[8,96,128]{2,1,0:T(8,128)(2,1)} %broadcast_in_dim.113), calls=%async_computation | async-start | bytes 393216 | tf_op jit(solution)/shard_map/all_to_all | solution.py:14
  56.9 18.3 %all-to-all-start.2 = ((bf16[8,304,128]{2,1,0:T(8,128)(2,1)}), bf16[8,304,128]{2,1,0:T(8,128)(2,1)}, u32[]{:S(2)}, u32[]{:S(2)}) async-start(bf16[8,304,128]{2,1,0:T(8,128)(2,1)} %pad_maximum_fusion), calls=%async_computation.2 | async-start | bytes 1245184 | tf_op jit(solution)/shard_map/all_to_all | solution.py:14
  75.3 1.2 copy-start.1
  78.7 15.9 %all-to-all-start.3 = ((bf16[12,64,128]{2,1,0:T(8,128)(2,1)}), bf16[12,64,128]{2,1,0:T(8,128)(2,1)S(1)}, u32[]{:S(2)}, u32[]{:S(2)}) async-start(bf16[12,64,128]{2,1,0:T(8,128)(2,1)} %get-tuple-element.9), calls=%async_computation.3 | async-start | bytes 393216 | tf_op jit(solution)/shard_map/all_to_all | solution.py:14
  95.3 14.2 %all-to-all-start.4 = ((f32[8,16,128]{2,1,0:T(8,128)}), f32[8,16,128]{2,1,0:T(8,128)}, u32[]{:S(2)}, u32[]{:S(2)}) async-start(f32[8,16,128]{2,1,0:T(8,128)} %broadcast_in_dim.119), calls=%async_computation.4 | async-start | bytes 131072 | tf_op jit(solution)/shard_map/all_to_all | solution.py:14
  110.9 13.9 %all-to-all-start.5 = ((bf16[12,16,128]{2,1,0:T(8,128)(2,1)}), bf16[12,16,128]{2,1,0:T(8,128)(2,1)S(1)}, u32[]{:S(2)}, u32[]{:S(2)}) async-start(bf16[12,16,128]{2,1,0:T(8,128)(2,1)} %broadcast_in_dim.120), calls=%async_computation.5 | async-start | bytes 98304 | tf_op jit(solution)/shard_map/all_to_all | solution.py:14

commit v7 on v6

--- a/solution.py
+++ b/solution.py
@@ -1,6 +1,7 @@
+import functools
+
 import jax
 import jax.numpy as jnp
-import numpy as np
 from jax import lax
 from jax.experimental import pallas as pl
 from jax.experimental.pallas import tpu as pltpu
@@ -25,6 +26,79 @@
 def two(a):
     high = a.astype(BF16)
     return jnp.concatenate([high, (a - high.astype(F32)).astype(BF16)], axis=-2)
+
+
+def near_rows(edges, cot, sends):
+    rows, block = edges.shape
+    mine, cls = cot.shape
+    rest = jnp.concatenate([cot[:, block:], jnp.zeros((mine, 2 * block - cls), BF16)], axis=1)
+    for j in range(sends.shape[0]):
+        sends[j, :rows] = edges[...]
+        sends[j, rows : rows + mine] = cot[:, :block]
+        sends[j, rows + mine :] = rest
+
+
+def first(xs, by_lane, spot, lists, got, agg, own, w, sends):
+    lanes, _, block = got.shape
+    blocks, cols = agg.shape[:2]
+    listed = lists.shape[1]
+    mids = blocks // xs
+    strips = blocks // mids
+    strip = block // strips
+    mine = block // lanes
+    edges = mine * listed
+    total = lanes * edges
+    over = (((1,), (1,)), ((), ()))
+    cot = [got[:, edges : edges + mine], got[:, edges + mine :]]
+    cot = jnp.concatenate([c.reshape(block, block) for c in cot], axis=1)
+    shape = (by_lane, 2 * block)
+    at = lax.broadcasted_iota(jnp.int32, shape, 1) - lax.broadcasted_iota(jnp.int32, shape, 0)
+    pick = jnp.where(at == spot[1] * by_lane, 1.0, 0.0).astype(BF16)
+    cot = lax.dot_general(pick, cot, over, preferred_element_type=F32).astype(BF16)
+    row = lax.broadcasted_iota(jnp.int32, (block, total), 0)
+    at = lax.broadcasted_iota(jnp.int32, (block, total), 1)
+    spread = jnp.where(at // listed == row, 1.0, 0.0).astype(BF16)
+    cot = jnp.dot(cot, spread, preferred_element_type=F32)
+    at = lax.broadcasted_iota(jnp.int32, (by_lane, total), 1)
+    to = jnp.full((by_lane, total), -1, jnp.int32)
+    for x in range(xs):
+        for k in range(listed):
+            here = (at // (total // xs) == x) & (at % listed == k)
+            to = jnp.where(here, lists[x * mids + spot[0], k], to)
+    back = [jnp.where(to == b, cot, 0.0).astype(BF16) for b in range(blocks)]
+    near = got[:, :edges].reshape(total, block)
+    back = [jnp.dot(b, near, preferred_element_type=F32) for b in back]
+    pad = jnp.zeros((sends.shape[1] - block - 2 * cols - by_lane, block), F32)
+    parts = []
+    for b in range(blocks):
+        mine_b = own[:, b * block : (b + 1) * block].astype(F32)
+        parts.append(jnp.concatenate([agg[b].astype(F32), mine_b, back[b], pad], axis=0))
+    high = parts[0].shape[0]
+    parts = [
+        jnp.concatenate(parts[x * mids : (x + 1) * mids], axis=0).astype(BF16) for x in range(xs)
+    ]
+    parts = jnp.concatenate(parts, axis=1)
+    row = lax.broadcasted_iota(jnp.int32, (xs * block, block), 0)
+    to = lax.broadcasted_iota(jnp.int32, (xs * block, block), 1)
+    fits = (to // strip == row // block) & (to % strip == row % strip)
+    for low in range(strips):
+        move = jnp.where(fits & (row % block // strip == low), 1.0, 0.0).astype(BF16)
+        moved = jnp.dot(parts, move, preferred_element_type=F32).astype(BF16)
+        for mid in range(mids):
+            sends[mid * strips + low, :high] = moved[mid * high : (mid + 1) * high]
+    wide = w.shape[2] // lanes
+    w = [w[i, :, j * wide : (j + 1) * wide].astype(F32) for i in range(2) for j in range(lanes)]
+    w = jnp.concatenate(w, axis=0).astype(BF16)
+    for z in range(blocks):
+        sends[z, high:] = w
+
+
+def sum_nodes(got, sends):
+    total = got[0]
+    for n in range(1, got.shape[0]):
+        total = total + got[n]
+    for z in range(sends.shape[0]):
+        sends[z] = total.astype(BF16)
 
 
 def middle(got, w, sends, rows, logits):
@@ -50,8 +124,10 @@
     sends[:, :by_z] = high
     sends[:, by_z : 2 * by_z] = (grad - high.astype(F32)).astype(BF16)
     over = (((1,), (1,)), ((), ()))
-    product = lax.dot_general(rows[...], w[0], over, preferred_element_type=F32).astype(BF16)
+    product = lax.dot_general(rows[...], w[0], over, preferred_element_type=F32)
     logits[...] = lax.dot_general(rows[...], w[1], over, preferred_element_type=F32)
+    pad = jnp.zeros((mine, 2 * block - product.shape[1]), F32)
+    product = jnp.concatenate([product, pad], axis=1).astype(BF16)
     for z in range(blocks):
         sends[z, 2 * by_z : 2 * by_z + mine] = product[:, :block]
         sends[z, 2 * by_z + mine :] = product[:, block:]
@@ -64,8 +140,8 @@
     part = got[0, kept:].astype(F32)
     for j in range(1, lanes):
         part = part + got[j, kept:].astype(F32)
-    part = jnp.concatenate([part[:mine], part[mine:]], axis=1) + own[...]
-    logits[...] = part[:, :cls]
+    part = jnp.concatenate([part[:mine], part[mine:]], axis=1)
+    logits[...] = part[:, :cls] + own[...]
     for j in range(lanes):
         grad[:, j * wide : (j + 1) * wide] = got[j, :kept].astype(F32)[:cls]
 
@@ -92,15 +168,14 @@
     mine_of = jnp.arange(blocks) == mids * jnp.arange(xs)[:, None] + place // strips
     lists = dot("xb,bk->xk", mine_of.astype(BF16), list_two.astype(BF16)).astype(jnp.int32)
 
-    edges = adj_two.reshape(mine * listed, block)
-    cot = jnp.pad(cotangent, ((0, 0), (0, 2 * block - cls)))
-    sends = jnp.concatenate([edges, cot[:, :block], cot[:, block:]], axis=0)
-    got = exchange(to_all(sends, lanes), LANE)
-    edges = got[:, : mine * listed].reshape(xs, strip, listed, block)
-    cot = got[:, mine * listed :].reshape(xs, cores, 2, mine, block)
-    pick = jnp.arange(2 * block)[:, None] == my_lane * by_lane + jnp.arange(by_lane)
-    pick = pick.reshape(2, block, by_lane).astype(BF16)
-    cot = dot("xchit,hts->xcis", cot, pick).astype(BF16).reshape(xs, strip, by_lane)
+    limit = pltpu.CompilerParams(vmem_limit_bytes=16 * 2**20)
+    got = pl.pallas_call(
+        near_rows,
+        out_shape=jax.ShapeDtypeStruct((lanes, mine * (listed + 2), block), BF16),
+        compiler_params=limit,
+    )(adj_two.reshape(mine * listed, block), cotangent)
+    near = exchange(got, LANE)
+    edges = near[:, : mine * listed].reshape(xs, strip, listed, block)
 
     tiles = features.reshape(cols, sources // block, block)
     chosen = lax.gather(
@@ -111,23 +186,28 @@
         mode="promise_in_bounds",
     )
     chosen = chosen.reshape(cols, blocks, fanout, block)
-    own = tiles[:, :blocks].transpose(1, 0, 2)
     agg = dot("fhks,hkts->hft", chosen, adj_one).astype(BF16)
-    back = dot("xrc,xrks->xkcs", cot, edges)
-    hits = lists[:, :, None] == jnp.arange(blocks, dtype=jnp.int32)
-    back = jnp.where(hits[..., None, None], back[:, :, None], 0.0).sum((0, 1)).astype(BF16)
-    at = np.arange(block)
-    move = np.zeros((xs, block, strips, block), np.float32)
-    for x in range(xs):
-        for low in range(strips):
-            move[x, :, low] = at[:, None] - low * strip == at - x * strip
-            move[x, :, low, : x * strip] = move[x, :, low, (x + 1) * strip :] = 0
-    sends = jnp.concatenate([agg, own, back], axis=1).reshape(xs, mids, -1, block)
-    sends = dot("xmkl,xlzr->mzkr", sends, jnp.asarray(move, BF16)).astype(BF16)
-    sends = sends.reshape(blocks, -1, block)
-    weights = w_one.reshape(2, cols, lanes, wide).transpose(0, 2, 1, 3).reshape(-1, wide)
-    got = exchange(jnp.concatenate([sends, to_all(weights, blocks)], axis=1), "z")
-    inputs, back, weights = jnp.split(got, (2 * cols, 2 * cols + by_lane), axis=1)
+    above = -(-(2 * cols + by_lane) // 16) * 16
+    whole = pl.BlockSpec(memory_space=pltpu.VMEM)
+    scalars = pl.BlockSpec(memory_space=pltpu.SMEM)
+    got = pl.pallas_call(
+        functools.partial(first, xs, by_lane),
+        grid=(1,),
+        in_specs=[
+            scalars,
+            scalars,
+            whole,
+            whole,
+            pl.BlockSpec((cols, blocks * block), lambda i: (0, 0)),
+            whole,
+        ],
+        out_specs=whole,
+        out_shape=jax.ShapeDtypeStruct((blocks, above + 2 * cols * lanes, block), BF16),
+        compiler_params=limit,
+    )(jnp.stack([place // strips, my_lane]), list_two, near, agg, features, w_one)
+    got = exchange(got, "z")
+    inputs, weights = got[:, : 2 * cols], got[:, above:]
+    back = got[:, 2 * cols : 2 * cols + by_lane]
     inputs = inputs.reshape(blocks, 2, cols, block)
     weights = weights.reshape(blocks, 2, lanes, cols, wide)
     part = dot("zikr,zijkh->jrh", inputs, weights).astype(BF16)
@@ -136,20 +216,23 @@
     rows = part.reshape(lanes, lanes, mine, wide).transpose(1, 0, 2, 3)
     rows = rows.reshape(lanes, lanes * mine, wide)
     got = exchange(jnp.concatenate([part, rows, to_all(back, lanes)], axis=1), LANE)
-    w = jnp.pad(w_two.transpose(0, 2, 1), ((0, 0), (0, 2 * block - cls), (0, 0)))
     sends, rows, own_logits = pl.pallas_call(
         middle,
         out_shape=(
             jax.ShapeDtypeStruct((blocks, 4 * by_z, block), BF16),
             jax.ShapeDtypeStruct((mine, hid), BF16),
-            jax.ShapeDtypeStruct((mine, 2 * block), F32),
+            jax.ShapeDtypeStruct((mine, cls), F32),
         ),
-        compiler_params=pltpu.CompilerParams(vmem_limit_bytes=16 * 2**20),
-    )(got, w)
+        compiler_params=limit,
+    )(got, w_two.transpose(0, 2, 1))
     got = exchange(sends, "z")
     grad = jnp.sum(got[:, : 2 * by_z].astype(F32), axis=0)
     grad = grad[:by_z] + grad[by_z:]
-    grad = jnp.sum(exchange(to_all(grad, nodes), "node"), axis=0).astype(BF16)
+    grad = pl.pallas_call(
+        sum_nodes,
+        out_shape=jax.ShapeDtypeStruct((blocks, by_z, wide), BF16),
+        compiler_params=limit,
+    )(exchange(to_all(grad, nodes), "node"))
 
     hits = lists[:, :, None] == my_x * mids + jnp.arange(mids, dtype=jnp.int32)
     hits = hits.transpose(0, 2, 1)[:, None, :, :, None]
@@ -160,7 +243,7 @@
     logits = dot("rs,sc->rc", near, product).reshape(lanes, mine, 2 * block)
     logits = jnp.concatenate([logits[..., :block], logits[..., block:]], axis=1)
 
-    grad = exchange(to_all(grad, blocks), "z").reshape(every, wide)[:kept]
+    grad = exchange(grad, "z").reshape(every, wide)[:kept]
     got = exchange(jnp.concatenate([to_all(grad, lanes), logits.astype(BF16)], axis=1), LANE)
     logits, grad = pl.pallas_call(
         finish,
@@ -168,7 +251,7 @@
             jax.ShapeDtypeStruct((mine, cls), F32),
             jax.ShapeDtypeStruct((cls, hid), F32),
         ),
-        compiler_params=pltpu.CompilerParams(vmem_limit_bytes=16 * 2**20),
+        compiler_params=limit,
     )(got, own_logits)
     return rows, logits, grad.T
 

time: 143 us -> 142 us (level)
  waiting for transfers between devices: 35.2 us -> 30.7 us
  Pallas kernels: 3.12 us -> 5.83 us
    all_to_all x5, waiting for transfers between devices: 35.2 us -> 30.7 us  [exchange(): return lax.all_to_all(parts, axis, 0, 0, tiled=True)]
    unnamed x6 -> x23, local copies, waits for them, and re-layouts: 3.23 us -> 7.18 us
    pallas_call x0 -> x3, Pallas kernels: none -> 2.81 us  [the longest x1 1.47 us: per_device(): pl.pallas_call(functools.partial(first, xs, by_lane), grid=(1,), in_specs...]
    broadcast_in_dim x6 -> x3, local copies, waits for them, and re-layouts: 2.85 us -> 0.69 us  [to_all(): return jnp.broadcast_to(part[None], (size, *part.shape))]
    concatenate x3 -> x0, other arithmetic: 1.64 us -> none  [the longest x1 0.83 us: per_device(): sends = jnp.concatenate([edges, cot[:, :block], cot[:, block:]], axis=0)]
    dot_general x7 -> x4, matrix products: 5.45 us -> 4.76 us  [dot(): return jnp.einsum(spec, a, b, preferred_element_type=F32)]
  transfers between devices with their start and end apart: 5 -> 5, of which waited for: 4 -> 5; matrix products, arithmetic and copies ran while one was open for 8% -> 11% of each run, Pallas kernels for 0% -> 0%
where the time goes in v7:
time: 142 us; the launch traced here: 140 us
  blocking collectives  45.2 us (32%)
  starting transfers between devices  35.9 us (25%)
  waiting for transfers between devices  30.7 us (22%)
  local copies, waits for them, and re-layouts  12.6 us (9%)
  Pallas kernels  5.83 us (4%)
  matrix products  4.76 us (3%)
  other arithmetic  4.61 us (3%)
    all_to_all x2, blocking collectives, exchange(): return lax.all_to_all(parts, axis, 0, 0, tiled=True)  45.2 us
    all_to_all x5, starting transfers between devices, exchange(): return lax.all_to_all(parts, axis, 0, 0, tiled=True)  35.9 us
    all_to_all x5, waiting for transfers between devices, exchange(): return lax.all_to_all(parts, axis, 0, 0, tiled=True)  30.7 us
    unnamed x23, local copies, waits for them, and re-layouts  7.18 us
    dot_general x4, matrix products, dot(): return jnp.einsum(spec, a, b, preferred_element_type=F32)  4.76 us
  transfers between devices with their start and end apart: 5, of which 5 were waited for; matrix products, arithmetic and copies ran while one was open for 11% of the time, Pallas kernels for 0%

profile of v7, /device:TPU:1, one launch (start us, length us, event | category | flops | bytes accessed | tf_op | source)
XLA Modules:
  0.0 140.5 jit_solution(7221942570604978725)
XLA Ops:
  0.6 0.0 copy-start
  0.6 0.0 copy-start.5
  0.7 0.9 copy-done.5
  1.5 0.0 copy-start.6
  1.5 0.8 copy-done.6
  2.3 0.7 shard_map.103
  3.0 13.8 %all-to-all-start = ((bf16[8,96,128]{2,1,0:T(8,128)(2,1)}), bf16[8,96,128]{2,1,0:T(8,128)(2,1)S(1)}, u32[]{:S(2)}, u32[]{:S(2)}) async-start(bf16[8,96,128]{2,1,0:T(8,128)(2,1)} %shard_map.103), calls=%async_computation | async-start | bytes 393216 | tf_op jit(solution)/shard_map/all_to_all | solution.py:15
  16.8 0.8 copy.25
  17.6 0.1 reshape.107
  17.7 2.3 %gather_fusion = bf16[96,8,128]{2,1,0:T(8,128)(2,1)} fusion(bf16[8,96,128]{2,0,1:T(8,128)(2,1)} %bitcast.47, s32[1024]{0:T(1024)S(1)} %pad_clamp_fusion), kind=kCustom, calls=%fused_computation | custom fusion | bytes 393600 | tf_op jit(solution)/shard_map/gather | solution.py:181
  19.9 0.0 copy-done
  19.9 0.0 copy-start.8
  19.9 0.0 copy-start.2
  19.9 2.5 %fusion.1.agg = bf16[12,8,128]{2,1,0:T(8,128)(2,1)} fusion(bf16[8,12,8,128]{3,0,2,1:T(8,128)(2,1)} %bitcast.53, bf16[12,8,128,128]{3,2,1,0:T(8,128)(2,1)S(1)} %copy-done), kind=kOutput, calls=%fused_computation.5 | convolution fusion | flops 25178112 | bytes 3366912 | tf_op jit(solution)/shard_map/fhks,hkts->hft/dot_general | solution.py:23
  22.4 0.0 copy-done.8
  22.4 0.1 copy.26.lists
  22.5 0.1 pad_add_fusion.spot
  22.6 0.1 all-to-all-done.got
  22.7 0.0 copy-done.2
  22.7 0.0 copy-start.3
  22.7 0.7 copy-done.3
  23.5 0.0 copy-start.4
  23.5 0.8 copy-done.4
  24.2 1.5 %shard_map.104 = bf16[12,176,128]{2,1,0:T(8,128)(2,1)S(1)} custom-call(s32[2]{0:T(128)S(1)} %pad_add_fusion.spot, s32[12,4]{1,0:T(8,128)S(1)} %copy.26.lists, bf16[8,96,128]{2,1,0:T(8,128)(2,1)S(1)} %all-to-all-done.got, bf16[12,8,128]{2,1,0:T(8,128)(2,1)S(1)} %copy-done.3, bf16[8,12288]{1,0:T(8,128)(2,1)S(1)} %copy-done.2, bf16[2,8,1024]{2,1,0:T(8,128)(2,1)S(1)} %copy-done.4), custom_call_target="tpu_custom_call" | custom-call | tf_op jit(solution)/shard_map/pallas_call | solution.py:193
  25.7 29.4 %all_to_all.35 = bf16[12,176,128]{2,1,0:T(8,128)(2,1)S(1)} all-to-all(bf16[12,176,128]{2,1,0:T(8,128)(2,1)S(1)} %shard_map.104), channel_id=1, replica_groups=mesh['x'=4,'z'=12,'c'=2,'node'=8] {'z'}, dimensions={0} | all-to-all | bytes 1081344 | tf_op jit(solution)/shard_map/all_to_all | solution.py:15
  55.2 0.3 fusion
  55.5 0.9 pad_maximum_fusion
  56.4 7.7 %all-to-all-start.2 = ((bf16[8,304,128]{2,1,0:T(8,128)(2,1)}), bf16[8,304,128]{2,1,0:T(8,128)(2,1)}, u32[]{:S(2)}, u32[]{:S(2)}) async-start(bf16[8,304,128]{2,1,0:T(8,128)(2,1)} %pad_maximum_fusion), calls=%async_computation.2 | async-start | bytes 1245184 | tf_op jit(solution)/shard_map/all_to_all | solution.py:15
  64.1 2.1 %copy.44 = bf16[2,1024,153]{1,2,0:T(8,128)(2,1)} copy(bf16[2,1024,153]{1,0,2:T(2,128)(2,1)} %param.14) | data formatting | bytes 1253376 | tf_op args[6]
  66.2 0.6 iota_compare_fusion.2
  66.7 0.5 multiply_add_fusion
  67.2 0.5 iota_add_fusion
  67.8 6.9 %all-to-all-done.2.got = bf16[8,304,128]{2,1,0:T(8,128)(2,1)} async-done(((bf16[8,304,128]{2,1,0:T(8,128)(2,1)}), bf16[8,304,128]{2,1,0:T(8,128)(2,1)}, u32[]{:S(2)}, u32[]{:S(2)}) %all-to-all-start.2) | async-done | bytes 622624 | tf_op jit(solution)/shard_map/all_to_all | solution.py:15
  74.7 0.0 copy-start.1
  74.7 1.1 copy-done.1
  75.8 2.1 %shard_map.105 = (bf16[12,64,128]{2,1,0:T(8,128)(2,1)}, bf16[16,1024]{1,0:T(8,128)(2,1)}, f32[16,153]{1,0:T(8,128)S(1)}) custom-call(bf16[8,304,128]{2,1,0:T(8,128)(2,1)} %all-to-all-done.2.got, bf16[2,153,1024]{2,1,0:T(8,128)(2,1)S(1)} %bitcast.46), custom_call_target="tpu_custom_call" | custom-call | tf_op jit(solution)/shard_map/pallas_call | solution.py:219
  77.9 3.5 %all-to-all-start.3 = ((bf16[12,64,128]{2,1,0:T(8,128)(2,1)}), bf16[12,64,128]{2,1,0:T(8,128)(2,1)S(1)}, u32[]{:S(2)}, u32[]{:S(2)}) async-start(bf16[12,64,128]{2,1,0:T(8,128)(2,1)} %get-tuple-element.9), calls=%async_computation.3 | async-start | bytes 393216 | tf_op jit(solution)/shard_map/all_to_all | solution.py:15
  81.5 0.9 convolution_convert_fusion.1
  82.3 0.7 broadcast_compare_fusion
  83.1 0.0 copy-start.9
  83.1 0.1 select_reduce_fusion
  83.2 0.1 copy.32
  83.3 0.7 dot_general.17
  84.0 0.0 copy-start.7
  84.0 9.7 %all-to-all-done.3 = bf16[12,64,128]{2,1,0:T(8,128)(2,1)S(1)} async-done(((bf16[12,64,128]{2,1,0:T(8,128)(2,1)}), bf16[12,64,128]{2,1,0:T(8,128)(2,1)S(1)}, u32[]{:S(2)}, u32[]{:S(2)}) %all-to-all-start.3) | async-done | bytes 196640 | tf_op jit(solution)/shard_map/all_to_all | solution.py:15
  93.8 0.7 copy.33
  94.5 0.6 broadcast_in_dim.70
  95.1 6.8 %all-to-all-start.4 = ((f32[8,16,128]{2,1,0:T(8,128)}), f32[8,16,128]{2,1,0:T(8,128)S(1)}, u32[]{:S(2)}, u32[]{:S(2)}) async-start(f32[8,16,128]{2,1,0:T(8,128)} %broadcast_in_dim.70), calls=%async_computation.4 | async-start | bytes 131072 | tf_op jit(solution)/shard_map/all_to_all | solution.py:15
  102.0 0.0 copy-done.9
  102.0 1.1 broadcast_select_fusion
  103.1 0.8 reshape.117
  103.9 0.0 copy-done.7
  103.9 1.1 convolution_convert_fusion
  105.0 4.2 %all-to-all-done.4.got = f32[8,16,128]{2,1,0:T(8,128)S(1)} async-done(((f32[8,16,128]{2,1,0:T(8,128)}), f32[8,16,128]{2,1,0:T(8,128)S(1)}, u32[]{:S(2)}, u32[]{:S(2)}) %all-to-all-start.4) | async-done | bytes 65568 | tf_op jit(solution)/shard_map/all_to_all | solution.py:15
  109.2 0.6 shard_map.106
  109.8 4.1 %all-to-all-start.5 = ((bf16[12,16,128]{2,1,0:T(8,128)(2,1)}), bf16[12,16,128]{2,1,0:T(8,128)(2,1)S(1)}, u32[]{:S(2)}, u32[]{:S(2)}) async-start(bf16[12,16,128]{2,1,0:T(8,128)(2,1)} %shard_map.106), calls=%async_computation.5 | async-start | bytes 98304 | tf_op jit(solution)/shard_map/all_to_all | solution.py:15
  113.9 9.8 %all-to-all-done.5 = bf16[12,16,128]{2,1,0:T(8,128)(2,1)S(1)} async-done(((bf16[12,16,128]{2,1,0:T(8,128)(2,1)}), bf16[12,16,128]{2,1,0:T(8,128)(2,1)S(1)}, u32[]{:S(2)}, u32[]{:S(2)}) %all-to-all-start.5) | async-done | bytes 49184 | tf_op jit(solution)/shard_map/all_to_all | solution.py:15
  123.8 15.8 %all_to_all.36.got = bf16[8,192,128]{2,1,0:T(8,128)(2,1)S(1)} all-to-all(bf16[8,192,128]{2,1,0:T(8,128)(2,1)S(1)} %pad_maximum_fusion.1), channel_id=1, replica_groups=mesh['x'=4,'z'=12,'c'=2,'node'=8] {'x','c'}, dimensions={0} | all-to-all | bytes 786432 | tf_op jit(solution)/shard_map/all_to_all | solution.py:15
  139.6 0.9 shard_map.107
  (16 shorter events, 0.2 us)
Async XLA Ops:
  0.6 19.3 %copy-start = (bf16[12,8,128,128]{3,2,1,0:T(8,128)(2,1)S(1)}, bf16[12,8,128,128]{3,2,1,0:T(8,128)(2,1)}, u32[]{:S(2)}) copy-start(bf16[12,8,128,128]{3,2,1,0:T(8,128)(2,1)} %param.10) | copy-start | bytes 9437188
  0.6 0.9 copy-start.5
  1.5 0.8 copy-start.6
  3.0 19.7 %all-to-all-start = ((bf16[8,96,128]{2,1,0:T(8,128)(2,1)}), bf16[8,96,128]{2,1,0:T(8,128)(2,1)S(1)}, u32[]{:S(2)}, u32[]{:S(2)}) async-start(bf16[8,96,128]{2,1,0:T(8,128)(2,1)} %shard_map.103), calls=%async_computation | async-start | bytes 393216 | tf_op jit(solution)/shard_map/all_to_all | solution.py:15
  19.9 2.5 %copy-start.8 = (s32[12,4]{0,1:T(4,128)S(1)}, s32[12,4]{0,1:T(4,128)}, u32[]{:S(2)}) copy-start(s32[12,4]{0,1:T(4,128)} %param.13) | copy-start | bytes 580
  19.9 2.8 %copy-start.2 = (bf16[8,12288]{1,0:T(8,128)(2,1)S(1)}, bf16[8,12288]{1,0:T(8,128)(2,1)}, u32[]{:S(2)}) copy-start(bf16[8,12288]{1,0:T(8,128)(2,1)} %own.1) | copy-start | bytes 589828
  22.7 0.7 copy-start.3
  23.5 0.8 copy-start.4
  56.4 18.3 %all-to-all-start.2 = ((bf16[8,304,128]{2,1,0:T(8,128)(2,1)}), bf16[8,304,128]{2,1,0:T(8,128)(2,1)}, u32[]{:S(2)}, u32[]{:S(2)}) async-start(bf16[8,304,128]{2,1,0:T(8,128)(2,1)} %pad_maximum_fusion), calls=%async_computation.2 | async-start | bytes 1245184 | tf_op jit(solution)/shard_map/all_to_all | solution.py:15
  74.7 1.1 copy-start.1
  77.9 15.8 %all-to-all-start.3 = ((bf16[12,64,128]{2,1,0:T(8,128)(2,1)}), bf16[12,64,128]{2,1,0:T(8,128)(2,1)S(1)}, u32[]{:S(2)}, u32[]{:S(2)}) async-start(bf16[12,64,128]{2,1,0:T(8,128)(2,1)} %get-tuple-element.9), calls=%async_computation.3 | async-start | bytes 393216 | tf_op jit(solution)/shard_map/all_to_all | solution.py:15
  83.1 18.9 %copy-start.9 = (pred[2]{0:T(512)(128)(4,1)S(1)}, pred[2]{0:T(512)(128)(4,1)}, u32[]{:S(2)}) copy-start(pred[2]{0:T(512)(128)(4,1)} %iota_compare_fusion.2) | copy-start | bytes 10
  84.0 19.9 %copy-start.7 = (bf16[8,16,384]{2,1,0:T(8,128)(2,1)S(1)}, bf16[8,16,384]{2,1,0:T(8,128)(2,1)}, u32[]{:S(2)}) copy-start(bf16[8,16,384]{2,1,0:T(8,128)(2,1)} %dot_general.17) | copy-start | bytes 294916
  95.1 14.1 %all-to-all-start.4 = ((f32[8,16,128]{2,1,0:T(8,128)}), f32[8,16,128]{2,1,0:T(8,128)S(1)}, u32[]{:S(2)}, u32[]{:S(2)}) async-start(f32[8,16,128]{2,1,0:T(8,128)} %broadcast_in_dim.70), calls=%async_computation.4 | async-start | bytes 131072 | tf_op jit(solution)/shard_map/all_to_all | solution.py:15
  109.8 13.9 %all-to-all-start.5 = ((bf16[12,16,128]{2,1,0:T(8,128)(2,1)}), bf16[12,16,128]{2,1,0:T(8,128)(2,1)S(1)}, u32[]{:S(2)}, u32[]{:S(2)}) async-start(bf16[12,16,128]{2,1,0:T(8,128)(2,1)} %shard_map.106), calls=%async_computation.5 | async-start | bytes 98304 | tf_op jit(solution)/shard_map/all_to_all | solution.py:15

commit v8 on v7

--- a/solution.py
+++ b/solution.py
@@ -28,7 +28,15 @@
     return jnp.concatenate([high, (a - high.astype(F32)).astype(BF16)], axis=-2)
 
 
-def near_rows(edges, cot, sends):
+def near_rows(edges_in, cot_in, sends, edges, cot, sems):
+    copies = [
+        pltpu.make_async_copy(edges_in, edges, sems.at[0]),
+        pltpu.make_async_copy(cot_in, cot, sems.at[1]),
+    ]
+    for copy in copies:
+        copy.start()
+    for copy in copies:
+        copy.wait()
     rows, block = edges.shape
     mine, cls = cot.shape
     rest = jnp.concatenate([cot[:, block:], jnp.zeros((mine, 2 * block - cls), BF16)], axis=1)
@@ -38,7 +46,13 @@
         sends[j, rows + mine :] = rest
 
 
-def first(xs, by_lane, spot, lists, got, agg, own, w, sends):
+def first(xs, by_lane, spot, lists, got, agg_in, own, w_in, sends, agg, w, sems):
+    copies = [
+        pltpu.make_async_copy(agg_in, agg, sems.at[0]),
+        pltpu.make_async_copy(w_in, w, sems.at[1]),
+    ]
+    for copy in copies:
+        copy.start()
     lanes, _, block = got.shape
     blocks, cols = agg.shape[:2]
     listed = lists.shape[1]
@@ -68,6 +82,8 @@
     back = [jnp.where(to == b, cot, 0.0).astype(BF16) for b in range(blocks)]
     near = got[:, :edges].reshape(total, block)
     back = [jnp.dot(b, near, preferred_element_type=F32) for b in back]
+    for copy in copies:
+        copy.wait()
     pad = jnp.zeros((sends.shape[1] - block - 2 * cols - by_lane, block), F32)
     parts = []
     for b in range(blocks):
@@ -101,7 +117,9 @@
         sends[z] = total.astype(BF16)
 
 
-def middle(got, w, sends, rows, logits):
+def middle(got, w_in, sends, rows, logits, w, sem):
+    copy = pltpu.make_async_copy(w_in, w, sem)
+    copy.start()
     lanes, wide = got.shape[0], got.shape[2]
     blocks, by_z = sends.shape[0], sends.shape[1] // 4
     block, mine = got.shape[2], rows.shape[0]
@@ -124,6 +142,7 @@
     sends[:, :by_z] = high
     sends[:, by_z : 2 * by_z] = (grad - high.astype(F32)).astype(BF16)
     over = (((1,), (1,)), ((), ()))
+    copy.wait()
     product = lax.dot_general(rows[...], w[0], over, preferred_element_type=F32)
     logits[...] = lax.dot_general(rows[...], w[1], over, preferred_element_type=F32)
     pad = jnp.zeros((mine, 2 * block - product.shape[1]), F32)
@@ -131,6 +150,33 @@
     for z in range(blocks):
         sends[z, 2 * by_z : 2 * by_z + mine] = product[:, :block]
         sends[z, 2 * by_z + mine :] = product[:, block:]
+
+
+def sum_z(got, sends):
+    by_z = sends.shape[1]
+    total = got[0, : 2 * by_z].astype(F32)
+    for z in range(1, got.shape[0]):
+        total = total + got[z, : 2 * by_z].astype(F32)
+    total = total[:by_z] + total[by_z:]
+    for n in range(sends.shape[0]):
+        sends[n] = total
+
+
+def partial_logits(spot, got, near, sends):
+    lanes, block = sends.shape[0], sends.shape[2]
+    mine = sends.shape[1] // 2
+    cores = near.shape[1] // (got.shape[0] * mine)
+    above = got.shape[1] - 2 * mine
+    rows = []
+    for z in range(got.shape[0]):
+        product = jnp.concatenate([got[z, above : above + mine], got[z, above + mine :]], axis=1)
+        for c in range(cores):
+            rows.append(jnp.where(spot[2] == c, product, jnp.zeros_like(product)))
+    rows = jnp.concatenate(rows, axis=0)
+    part = jnp.dot(near[...], rows, preferred_element_type=F32).astype(BF16)
+    for j in range(lanes):
+        sends[j, :mine] = part[j * mine : (j + 1) * mine, :block]
+        sends[j, mine:] = part[j * mine : (j + 1) * mine, block:]
 
 
 def finish(got, own, logits, grad):
@@ -169,9 +215,19 @@
     lists = dot("xb,bk->xk", mine_of.astype(BF16), list_two.astype(BF16)).astype(jnp.int32)
 
     limit = pltpu.CompilerParams(vmem_limit_bytes=16 * 2**20)
+    wide_limit = pltpu.CompilerParams(vmem_limit_bytes=60 * 2**20)
+    away = pl.BlockSpec(memory_space=pltpu.HBM)
+    whole = pl.BlockSpec(memory_space=pltpu.VMEM)
+    scalars = pl.BlockSpec(memory_space=pltpu.SMEM)
     got = pl.pallas_call(
         near_rows,
+        in_specs=[away, away],
         out_shape=jax.ShapeDtypeStruct((lanes, mine * (listed + 2), block), BF16),
+        scratch_shapes=[
+            pltpu.VMEM((mine * listed, block), BF16),
+            pltpu.VMEM((mine, cls), BF16),
+            pltpu.SemaphoreType.DMA((2,)),
+        ],
         compiler_params=limit,
     )(adj_two.reshape(mine * listed, block), cotangent)
     near = exchange(got, LANE)
@@ -188,8 +244,7 @@
     chosen = chosen.reshape(cols, blocks, fanout, block)
     agg = dot("fhks,hkts->hft", chosen, adj_one).astype(BF16)
     above = -(-(2 * cols + by_lane) // 16) * 16
-    whole = pl.BlockSpec(memory_space=pltpu.VMEM)
-    scalars = pl.BlockSpec(memory_space=pltpu.SMEM)
+    spot = jnp.stack([place // strips, my_lane, my_c])
     got = pl.pallas_call(
         functools.partial(first, xs, by_lane),
         grid=(1,),
@@ -197,14 +252,19 @@
             scalars,
             scalars,
             whole,
-            whole,
+            away,
             pl.BlockSpec((cols, blocks * block), lambda i: (0, 0)),
-            whole,
+            away,
         ],
         out_specs=whole,
         out_shape=jax.ShapeDtypeStruct((blocks, above + 2 * cols * lanes, block), BF16),
-        compiler_params=limit,
-    )(jnp.stack([place // strips, my_lane]), list_two, near, agg, features, w_one)
+        scratch_shapes=[
+            pltpu.VMEM(agg.shape, BF16),
+            pltpu.VMEM(w_one.shape, BF16),
+            pltpu.SemaphoreType.DMA((2,)),
+        ],
+        compiler_params=wide_limit,
+    )(spot, list_two, near, agg, features, w_one)
     got = exchange(got, "z")
     inputs, weights = got[:, : 2 * cols], got[:, above:]
     back = got[:, 2 * cols : 2 * cols + by_lane]
@@ -218,33 +278,39 @@
     got = exchange(jnp.concatenate([part, rows, to_all(back, lanes)], axis=1), LANE)
     sends, rows, own_logits = pl.pallas_call(
         middle,
+        in_specs=[whole, away],
+        scratch_shapes=[pltpu.VMEM((2, cls, hid), BF16), pltpu.SemaphoreType.DMA],
         out_shape=(
             jax.ShapeDtypeStruct((blocks, 4 * by_z, block), BF16),
             jax.ShapeDtypeStruct((mine, hid), BF16),
             jax.ShapeDtypeStruct((mine, cls), F32),
         ),
-        compiler_params=limit,
+        compiler_params=wide_limit,
     )(got, w_two.transpose(0, 2, 1))
     got = exchange(sends, "z")
-    grad = jnp.sum(got[:, : 2 * by_z].astype(F32), axis=0)
-    grad = grad[:by_z] + grad[by_z:]
+    grad = pl.pallas_call(
+        sum_z,
+        out_shape=jax.ShapeDtypeStruct((nodes, by_z, wide), F32),
+        compiler_params=limit,
+    )(got)
     grad = pl.pallas_call(
         sum_nodes,
         out_shape=jax.ShapeDtypeStruct((blocks, by_z, wide), BF16),
         compiler_params=limit,
-    )(exchange(to_all(grad, nodes), "node"))
+    )(exchange(grad, "node"))
 
     hits = lists[:, :, None] == my_x * mids + jnp.arange(mids, dtype=jnp.int32)
     hits = hits.transpose(0, 2, 1)[:, None, :, :, None]
     near = jnp.where(hits, edges[:, :, None], 0).sum(3).reshape(block, mids * block)
-    product = got[:, 2 * by_z :].reshape(mids, strips, 2, 1, mine, block).transpose(0, 1, 3, 4, 2, 5)
-    held = my_c == jnp.arange(cores).reshape(1, 1, cores, 1, 1, 1)
-    product = jnp.where(held, product, 0).reshape(mids * block, 2 * block)
-    logits = dot("rs,sc->rc", near, product).reshape(lanes, mine, 2 * block)
-    logits = jnp.concatenate([logits[..., :block], logits[..., block:]], axis=1)
+    logits = pl.pallas_call(
+        partial_logits,
+        in_specs=[scalars, whole, whole],
+        out_shape=jax.ShapeDtypeStruct((lanes, 2 * mine, block), BF16),
+        compiler_params=limit,
+    )(spot, got, near)
 
     grad = exchange(grad, "z").reshape(every, wide)[:kept]
-    got = exchange(jnp.concatenate([to_all(grad, lanes), logits.astype(BF16)], axis=1), LANE)
+    got = exchange(jnp.concatenate([to_all(grad, lanes), logits], axis=1), LANE)
     logits, grad = pl.pallas_call(
         finish,
         out_shape=(

time: 142 us -> 143 us (level)
  waiting for transfers between devices: 30.7 us -> 37.1 us
  local copies, waits for them, and re-layouts: 12.6 us -> 8.53 us
  Pallas kernels: 5.83 us -> 9.87 us
  other arithmetic: 4.61 us -> 1.82 us
  matrix products: 4.76 us -> 1.99 us
    all_to_all x5, waiting for transfers between devices: 30.7 us -> 37.1 us  [exchange(): return lax.all_to_all(parts, axis, 0, 0, tiled=True)]
    dot_general x4 -> x3, matrix products: 4.76 us -> 1.99 us  [dot(): return jnp.einsum(spec, a, b, preferred_element_type=F32)]
    pallas_call x2 -> x4, Pallas kernels: 2.81 us -> 5.3 us  [the longest x1 3.18 us: per_device(): pl.pallas_call(middle, in_specs=[whole, away], scratch_shapes=[pltpu.VMEM...]
    pallas_call x1, Pallas kernels: 1.47 us -> 3.02 us  [per_device(): pl.pallas_call(functools.partial(first, xs, by_lane), grid=(1,), in_specs...]
    unnamed x23 -> x18, local copies, waits for them, and re-layouts: 7.18 us -> 5.88 us
  transfers between devices with their start and end apart: 5 -> 5, of which waited for: 5 -> 5; matrix products, arithmetic and copies ran while one was open for 11% -> 6% of each run, Pallas kernels for 0% -> 1%
where the time goes in v8:
time: 143 us; the launch traced here: 142 us
  blocking collectives  46.1 us (32%)
  waiting for transfers between devices  37.1 us (26%)
  starting transfers between devices  35.7 us (25%)
  Pallas kernels  9.87 us (7%)
  local copies, waits for them, and re-layouts  8.53 us (6%)
  matrix products  1.99 us (1%)
  other arithmetic  1.82 us (1%)
    all_to_all x2, blocking collectives, exchange(): return lax.all_to_all(parts, axis, 0, 0, tiled=True)  46.1 us
    all_to_all x5, waiting for transfers between devices, exchange(): return lax.all_to_all(parts, axis, 0, 0, tiled=True)  37.1 us
    all_to_all x5, starting transfers between devices, exchange(): return lax.all_to_all(parts, axis, 0, 0, tiled=True)  35.7 us
    unnamed x18, local copies, waits for them, and re-layouts  5.88 us
    pallas_call x1, Pallas kernels, per_device(): pl.pallas_call(middle, in_specs=[whole, away], scratch_shapes=[pltpu.VMEM...  3.18 us
    pallas_call x1, Pallas kernels, per_device(): pl.pallas_call(functools.partial(first, xs, by_lane), grid=(1,), in_specs...  3.02 us
  transfers between devices with their start and end apart: 5, of which 5 were waited for; matrix products, arithmetic and copies ran while one was open for 6% of the time, Pallas kernels for 1%

profile of v8, /device:TPU:1, one launch (start us, length us, event | category | flops | bytes accessed | tf_op | source)
XLA Modules:
  0.0 142.0 jit_solution(17923652835947650673)
XLA Ops:
  0.6 0.0 copy-start
  0.6 0.0 copy-start.1
  0.7 0.9 copy-done.1
  1.5 0.0 copy-start.3
  1.5 0.8 copy-done.3
  2.3 0.7 shard_map.103
  3.0 13.8 %all-to-all-start = ((bf16[8,96,128]{2,1,0:T(8,128)(2,1)}), bf16[8,96,128]{2,1,0:T(8,128)(2,1)S(1)}, u32[]{:S(2)}, u32[]{:S(2)}) async-start(bf16[8,96,128]{2,1,0:T(8,128)(2,1)} %shard_map.103), calls=%async_computation | async-start | bytes 393216 | tf_op jit(solution)/shard_map/all_to_all | solution.py:15
  16.9 0.8 copy.23
  17.6 0.1 reshape.63
  17.7 1.6 %gather_fusion = bf16[96,8,128]{2,1,0:T(8,128)(2,1)S(1)} fusion(bf16[8,96,128]{2,0,1:T(8,128)(2,1)} %bitcast.53, s32[1024]{0:T(1024)S(1)} %pad_clamp_fusion), kind=kCustom, calls=%fused_computation | custom fusion | bytes 393600 | tf_op jit(solution)/shard_map/gather | solution.py:237
  19.3 0.0 copy-done
  19.3 0.0 copy-start.6
  19.3 1.5 %fusion.1.agg_in = bf16[12,8,128]{2,1,0:T(8,128)(2,1)} fusion(bf16[8,12,8,128]{3,0,2,1:T(8,128)(2,1)S(1)} %bitcast.54, bf16[12,8,128,128]{3,2,1,0:T(8,128)(2,1)S(1)} %copy-done), kind=kOutput, calls=%fused_computation.4 | convolution fusion | flops 25178112 | bytes 3366912 | tf_op jit(solution)/shard_map/fhks,hkts->hft/dot_general | solution.py:23
  20.9 0.0 copy-done.6
  20.9 0.7 copy.24.lists
  21.6 0.7 pad_add_fusion.spot
  22.2 0.6 all-to-all-done.got
  22.8 0.0 copy-start.5
  22.8 0.7 copy-done.5
  23.4 3.0 %shard_map.104 = bf16[12,176,128]{2,1,0:T(8,128)(2,1)} custom-call(s32[3]{0:T(128)} %pad_add_fusion.spot, s32[12,4]{1,0:T(8,128)} %copy.24.lists, bf16[8,96,128]{2,1,0:T(8,128)(2,1)} %copy-done.5, bf16[12,8,128]{2,1,0:T(8,128)(2,1)} %fusion.1.agg_in, bf16[8,12288]{1,0:T(8,128)(2,1)} %own.1, bf16[2,8,1024]{2,1,0:T(8,128)(2,1)} %w_in.1), custom_call_target="tpu_custom_call" | custom-call | tf_op jit(solution)/shard_map/pallas_call | solution.py:248
  26.5 29.6 %all_to_all.35 = bf16[12,176,128]{2,1,0:T(8,128)(2,1)S(1)} all-to-all(bf16[12,176,128]{2,1,0:T(8,128)(2,1)} %shard_map.104), channel_id=1, replica_groups=mesh['x'=4,'z'=12,'c'=2,'node'=8] {'z'}, dimensions={0} | all-to-all | bytes 1081344 | tf_op jit(solution)/shard_map/all_to_all | solution.py:15
  56.1 0.3 fusion
  56.5 0.9 pad_maximum_fusion
  57.4 7.4 %all-to-all-start.2 = ((bf16[8,304,128]{2,1,0:T(8,128)(2,1)}), bf16[8,304,128]{2,1,0:T(8,128)(2,1)}, u32[]{:S(2)}, u32[]{:S(2)}) async-start(bf16[8,304,128]{2,1,0:T(8,128)(2,1)} %pad_maximum_fusion), calls=%async_computation.2 | async-start | bytes 1245184 | tf_op jit(solution)/shard_map/all_to_all | solution.py:15
  64.8 2.1 %copy.43 = bf16[2,1024,153]{1,2,0:T(8,128)(2,1)} copy(bf16[2,1024,153]{1,0,2:T(2,128)(2,1)} %param.14) | data formatting | bytes 1253376 | tf_op args[6]
  66.9 8.6 %all-to-all-done.2.got = bf16[8,304,128]{2,1,0:T(8,128)(2,1)} async-done(((bf16[8,304,128]{2,1,0:T(8,128)(2,1)}), bf16[8,304,128]{2,1,0:T(8,128)(2,1)}, u32[]{:S(2)}, u32[]{:S(2)}) %all-to-all-start.2) | async-done | bytes 622624 | tf_op jit(solution)/shard_map/all_to_all | solution.py:15
  75.4 0.0 slice-start
  75.4 3.2 %shard_map.105 = (bf16[12,64,128]{2,1,0:T(8,128)(2,1)}, bf16[16,1024]{1,0:T(8,128)(2,1)}, f32[16,153]{1,0:T(8,128)}) custom-call(bf16[8,304,128]{2,1,0:T(8,128)(2,1)} %all-to-all-done.2.got, bf16[2,153,1024]{2,1,0:T(8,128)(2,1)} %bitcast.47), custom_call_target="tpu_custom_call" | custom-call | tf_op jit(solution)/shard_map/pallas_call | solution.py:279
  78.6 0.0 copy-start.4
  78.7 3.5 %all-to-all-start.3 = ((bf16[12,64,128]{2,1,0:T(8,128)(2,1)}), bf16[12,64,128]{2,1,0:T(8,128)(2,1)S(1)}, u32[]{:S(2)}, u32[]{:S(2)}) async-start(bf16[12,64,128]{2,1,0:T(8,128)(2,1)} %get-tuple-element.9), calls=%async_computation.3 | async-start | bytes 393216 | tf_op jit(solution)/shard_map/all_to_all | solution.py:15
  82.2 12.3 %all-to-all-done.3.got = bf16[12,64,128]{2,1,0:T(8,128)(2,1)S(1)} async-done(((bf16[12,64,128]{2,1,0:T(8,128)(2,1)}), bf16[12,64,128]{2,1,0:T(8,128)(2,1)S(1)}, u32[]{:S(2)}, u32[]{:S(2)}) %all-to-all-start.3) | async-done | bytes 196640 | tf_op jit(solution)/shard_map/all_to_all | solution.py:15
  94.5 0.6 shard_map.106
  95.2 6.8 %all-to-all-start.4 = ((f32[8,16,128]{2,1,0:T(8,128)}), f32[8,16,128]{2,1,0:T(8,128)S(1)}, u32[]{:S(2)}, u32[]{:S(2)}) async-start(f32[8,16,128]{2,1,0:T(8,128)} %shard_map.106), calls=%async_computation.4 | async-start | bytes 131072 | tf_op jit(solution)/shard_map/all_to_all | solution.py:15
  102.0 0.2 convolution_convert_fusion
  102.2 7.0 %all-to-all-done.4.got = f32[8,16,128]{2,1,0:T(8,128)S(1)} async-done(((f32[8,16,128]{2,1,0:T(8,128)}), f32[8,16,128]{2,1,0:T(8,128)S(1)}, u32[]{:S(2)}, u32[]{:S(2)}) %all-to-all-start.4) | async-done | bytes 65568 | tf_op jit(solution)/shard_map/all_to_all | solution.py:15
  109.2 0.6 shard_map.107
  109.8 4.1 %all-to-all-start.5 = ((bf16[12,16,128]{2,1,0:T(8,128)(2,1)}), bf16[12,16,128]{2,1,0:T(8,128)(2,1)}, u32[]{:S(2)}, u32[]{:S(2)}) async-start(bf16[12,16,128]{2,1,0:T(8,128)(2,1)} %shard_map.107), calls=%async_computation.5 | async-start | bytes 98304 | tf_op jit(solution)/shard_map/all_to_all | solution.py:15
  114.0 0.1 broadcast_compare_fusion
  114.1 0.0 slice-done
  114.1 0.1 select_reduce_fusion
  114.2 0.1 copy.30
  114.3 0.0 copy-start.2
  114.3 0.0 copy-done.4
  114.4 0.7 shard_map.108
  115.1 8.6 %all-to-all-done.5 = bf16[12,16,128]{2,1,0:T(8,128)(2,1)} async-done(((bf16[12,16,128]{2,1,0:T(8,128)(2,1)}), bf16[12,16,128]{2,1,0:T(8,128)(2,1)}, u32[]{:S(2)}, u32[]{:S(2)}) %all-to-all-start.5) | async-done | bytes 49184 | tf_op jit(solution)/shard_map/all_to_all | solution.py:15
  123.7 0.8 slice.26
  124.6 16.5 %all_to_all.36.got = bf16[8,192,128]{2,1,0:T(8,128)(2,1)S(1)} all-to-all(bf16[8,192,128]{2,1,0:T(8,128)(2,1)S(1)} %pad_maximum_fusion.1), channel_id=1, replica_groups=mesh['x'=4,'z'=12,'c'=2,'node'=8] {'x','c'}, dimensions={0} | all-to-all | bytes 786432 | tf_op jit(solution)/shard_map/all_to_all | solution.py:15
  141.1 0.0 copy-done.2
  141.1 0.9 shard_map.109
  (13 shorter events, 0.2 us)
Async XLA Ops:
  0.6 18.7 %copy-start = (bf16[12,8,128,128]{3,2,1,0:T(8,128)(2,1)S(1)}, bf16[12,8,128,128]{3,2,1,0:T(8,128)(2,1)}, u32[]{:S(2)}) copy-start(bf16[12,8,128,128]{3,2,1,0:T(8,128)(2,1)} %param.10) | copy-start | bytes 9437188
  0.6 0.9 copy-start.1
  1.5 0.8 copy-start.3
  3.0 19.7 %all-to-all-start = ((bf16[8,96,128]{2,1,0:T(8,128)(2,1)}), bf16[8,96,128]{2,1,0:T(8,128)(2,1)S(1)}, u32[]{:S(2)}, u32[]{:S(2)}) async-start(bf16[8,96,128]{2,1,0:T(8,128)(2,1)} %shard_map.103), calls=%async_computation | async-start | bytes 393216 | tf_op jit(solution)/shard_map/all_to_all | solution.py:15
  19.3 1.5 %copy-start.6 = (s32[12,4]{0,1:T(4,128)S(1)}, s32[12,4]{0,1:T(4,128)}, u32[]{:S(2)}) copy-start(s32[12,4]{0,1:T(4,128)} %param.13) | copy-start | bytes 580
  22.8 0.7 copy-start.5
  57.4 18.1 %all-to-all-start.2 = ((bf16[8,304,128]{2,1,0:T(8,128)(2,1)}), bf16[8,304,128]{2,1,0:T(8,128)(2,1)}, u32[]{:S(2)}, u32[]{:S(2)}) async-start(bf16[8,304,128]{2,1,0:T(8,128)(2,1)} %pad_maximum_fusion), calls=%async_computation.2 | async-start | bytes 1245184 | tf_op jit(solution)/shard_map/all_to_all | solution.py:15
  75.4 38.6 %slice-start = ((bf16[8,96,128]{2,1,0:T(8,128)(2,1)}), bf16[8,64,128]{2,1,0:T(8,128)(2,1)S(1)}, s32[]{:S(2)}) async-start(bf16[8,96,128]{2,1,0:T(8,128)(2,1)} %copy-done.5), calls=%async_computation.7 | async-start | bytes 262144 | tf_op jit(solution)/shard_map/slice | solution.py:234
  78.6 35.7 %copy-start.4 = (s32[3]{0:T(128)S(1)}, s32[3]{0:T(128)}, u32[]{:S(2)}) copy-start(s32[3]{0:T(128)} %pad_add_fusion.spot) | copy-start | bytes 40
  78.7 15.9 %all-to-all-start.3 = ((bf16[12,64,128]{2,1,0:T(8,128)(2,1)}), bf16[12,64,128]{2,1,0:T(8,128)(2,1)S(1)}, u32[]{:S(2)}, u32[]{:S(2)}) async-start(bf16[12,64,128]{2,1,0:T(8,128)(2,1)} %get-tuple-element.9), calls=%async_computation.3 | async-start | bytes 393216 | tf_op jit(solution)/shard_map/all_to_all | solution.py:15
  95.2 14.0 %all-to-all-start.4 = ((f32[8,16,128]{2,1,0:T(8,128)}), f32[8,16,128]{2,1,0:T(8,128)S(1)}, u32[]{:S(2)}, u32[]{:S(2)}) async-start(f32[8,16,128]{2,1,0:T(8,128)} %shard_map.106), calls=%async_computation.4 | async-start | bytes 131072 | tf_op jit(solution)/shard_map/all_to_all | solution.py:15
  109.8 13.9 %all-to-all-start.5 = ((bf16[12,16,128]{2,1,0:T(8,128)(2,1)}), bf16[12,16,128]{2,1,0:T(8,128)(2,1)}, u32[]{:S(2)}, u32[]{:S(2)}) async-start(bf16[12,16,128]{2,1,0:T(8,128)(2,1)} %shard_map.107), calls=%async_computation.5 | async-start | bytes 98304 | tf_op jit(solution)/shard_map/all_to_all | solution.py:15
  114.3 26.7 %copy-start.2 = (f32[16,153]{1,0:T(8,128)S(1)}, f32[16,153]{1,0:T(8,128)}, u32[]{:S(2)}) copy-start(f32[16,153]{1,0:T(8,128)} %get-tuple-element.10.own) | copy-start | bytes 29380

commit v9 on v8

--- a/solution.py
+++ b/solution.py
@@ -46,7 +46,7 @@
         sends[j, rows + mine :] = rest
 
 
-def first(xs, by_lane, spot, lists, got, agg_in, own, w_in, sends, agg, w, sems):
+def first(xs, by_lane, lists, got, agg_in, own, w_in, sends, edges_out, agg, w, sems):
     copies = [
         pltpu.make_async_copy(agg_in, agg, sems.at[0]),
         pltpu.make_async_copy(w_in, w, sems.at[1]),
@@ -55,11 +55,13 @@
         copy.start()
     lanes, _, block = got.shape
     blocks, cols = agg.shape[:2]
-    listed = lists.shape[1]
+    listed = lists.shape[0]
     mids = blocks // xs
     strips = blocks // mids
     strip = block // strips
     mine = block // lanes
+    my_x, my_mid = lax.axis_index("x"), lax.axis_index("z") // strips
+    my_lane = my_x * (lanes // xs) + lax.axis_index("c")
     edges = mine * listed
     total = lanes * edges
     over = (((1,), (1,)), ((), ()))
@@ -67,21 +69,27 @@
     cot = jnp.concatenate([c.reshape(block, block) for c in cot], axis=1)
     shape = (by_lane, 2 * block)
     at = lax.broadcasted_iota(jnp.int32, shape, 1) - lax.broadcasted_iota(jnp.int32, shape, 0)
-    pick = jnp.where(at == spot[1] * by_lane, 1.0, 0.0).astype(BF16)
+    pick = jnp.where(at == my_lane * by_lane, 1.0, 0.0).astype(BF16)
     cot = lax.dot_general(pick, cot, over, preferred_element_type=F32).astype(BF16)
     row = lax.broadcasted_iota(jnp.int32, (block, total), 0)
     at = lax.broadcasted_iota(jnp.int32, (block, total), 1)
-    spread = jnp.where(at // listed == row, 1.0, 0.0).astype(BF16)
+    fits = at // listed == row
+    spread = jnp.where(fits, 1.0, 0.0).astype(BF16)
     cot = jnp.dot(cot, spread, preferred_element_type=F32)
-    at = lax.broadcasted_iota(jnp.int32, (by_lane, total), 1)
-    to = jnp.full((by_lane, total), -1, jnp.int32)
+    at = lax.broadcasted_iota(jnp.int32, (8, total), 1)
+    to = jnp.full((8, total), -1, jnp.int32)
     for x in range(xs):
         for k in range(listed):
             here = (at // (total // xs) == x) & (at % listed == k)
-            to = jnp.where(here, lists[x * mids + spot[0], k], to)
-    back = [jnp.where(to == b, cot, 0.0).astype(BF16) for b in range(blocks)]
+            to = jnp.where(here, lists[k, x * mids + my_mid], to)
+    to = jnp.concatenate([to] * (block // 8), axis=0)
+    back = [jnp.where(to[:by_lane] == b, cot, 0.0).astype(BF16) for b in range(blocks)]
     near = got[:, :edges].reshape(total, block)
     back = [jnp.dot(b, near, preferred_element_type=F32) for b in back]
+    for mid in range(mids):
+        take = jnp.where(fits & (to == my_x * mids + mid), 1.0, 0.0).astype(BF16)
+        take = jnp.dot(take, near, preferred_element_type=F32).astype(BF16)
+        edges_out[:, mid * block : (mid + 1) * block] = take
     for copy in copies:
         copy.wait()
     pad = jnp.zeros((sends.shape[1] - block - 2 * cols - by_lane, block), F32)
@@ -162,21 +170,31 @@
         sends[n] = total
 
 
-def partial_logits(spot, got, near, sends):
+def partial_logits(got, near, sends):
     lanes, block = sends.shape[0], sends.shape[2]
     mine = sends.shape[1] // 2
     cores = near.shape[1] // (got.shape[0] * mine)
     above = got.shape[1] - 2 * mine
+    my_c = lax.axis_index("c")
     rows = []
     for z in range(got.shape[0]):
         product = jnp.concatenate([got[z, above : above + mine], got[z, above + mine :]], axis=1)
         for c in range(cores):
-            rows.append(jnp.where(spot[2] == c, product, jnp.zeros_like(product)))
+            rows.append(jnp.where(my_c == c, product, jnp.zeros_like(product)))
     rows = jnp.concatenate(rows, axis=0)
     part = jnp.dot(near[...], rows, preferred_element_type=F32).astype(BF16)
     for j in range(lanes):
         sends[j, :mine] = part[j * mine : (j + 1) * mine, :block]
         sends[j, mine:] = part[j * mine : (j + 1) * mine, block:]
+
+
+def last(grad, logits, sends):
+    kept = sends.shape[1] - logits.shape[1]
+    by_z = grad.shape[1]
+    for j in range(sends.shape[0]):
+        for z in range(kept // by_z):
+            sends[j, z * by_z : (z + 1) * by_z] = grad[z]
+        sends[j, kept:] = logits[j]
 
 
 def finish(got, own, logits, grad):
@@ -209,11 +227,6 @@
     strip = mine * cores
     strips = block // strip
     mids = blocks // xs
-    place, my_x, my_c = (lax.axis_index(axis) for axis in ("z", "x", "c"))
-    my_lane = my_x * cores + my_c
-    mine_of = jnp.arange(blocks) == mids * jnp.arange(xs)[:, None] + place // strips
-    lists = dot("xb,bk->xk", mine_of.astype(BF16), list_two.astype(BF16)).astype(jnp.int32)
-
     limit = pltpu.CompilerParams(vmem_limit_bytes=16 * 2**20)
     wide_limit = pltpu.CompilerParams(vmem_limit_bytes=60 * 2**20)
     away = pl.BlockSpec(memory_space=pltpu.HBM)
@@ -228,10 +241,9 @@
             pltpu.VMEM((mine, cls), BF16),
             pltpu.SemaphoreType.DMA((2,)),
         ],
-        compiler_params=limit,
+        compiler_params=wide_limit,
     )(adj_two.reshape(mine * listed, block), cotangent)
     near = exchange(got, LANE)
-    edges = near[:, : mine * listed].reshape(xs, strip, listed, block)
 
     tiles = features.reshape(cols, sources // block, block)
     chosen = lax.gather(
@@ -244,27 +256,28 @@
     chosen = chosen.reshape(cols, blocks, fanout, block)
     agg = dot("fhks,hkts->hft", chosen, adj_one).astype(BF16)
     above = -(-(2 * cols + by_lane) // 16) * 16
-    spot = jnp.stack([place // strips, my_lane, my_c])
-    got = pl.pallas_call(
+    got, near = pl.pallas_call(
         functools.partial(first, xs, by_lane),
         grid=(1,),
         in_specs=[
-            scalars,
             scalars,
             whole,
             away,
             pl.BlockSpec((cols, blocks * block), lambda i: (0, 0)),
             away,
         ],
-        out_specs=whole,
-        out_shape=jax.ShapeDtypeStruct((blocks, above + 2 * cols * lanes, block), BF16),
+        out_specs=(whole, whole),
+        out_shape=(
+            jax.ShapeDtypeStruct((blocks, above + 2 * cols * lanes, block), BF16),
+            jax.ShapeDtypeStruct((block, mids * block), BF16),
+        ),
         scratch_shapes=[
             pltpu.VMEM(agg.shape, BF16),
             pltpu.VMEM(w_one.shape, BF16),
             pltpu.SemaphoreType.DMA((2,)),
         ],
         compiler_params=wide_limit,
-    )(spot, list_two, near, agg, features, w_one)
+    )(list_two.T, near, agg, features, w_one)
     got = exchange(got, "z")
     inputs, weights = got[:, : 2 * cols], got[:, above:]
     back = got[:, 2 * cols : 2 * cols + by_lane]
@@ -299,18 +312,19 @@
         compiler_params=limit,
     )(exchange(grad, "node"))
 
-    hits = lists[:, :, None] == my_x * mids + jnp.arange(mids, dtype=jnp.int32)
-    hits = hits.transpose(0, 2, 1)[:, None, :, :, None]
-    near = jnp.where(hits, edges[:, :, None], 0).sum(3).reshape(block, mids * block)
     logits = pl.pallas_call(
         partial_logits,
-        in_specs=[scalars, whole, whole],
+        in_specs=[whole, whole],
         out_shape=jax.ShapeDtypeStruct((lanes, 2 * mine, block), BF16),
         compiler_params=limit,
-    )(spot, got, near)
-
-    grad = exchange(grad, "z").reshape(every, wide)[:kept]
-    got = exchange(jnp.concatenate([to_all(grad, lanes), logits], axis=1), LANE)
+    )(got, near)
+
+    got = pl.pallas_call(
+        last,
+        out_shape=jax.ShapeDtypeStruct((lanes, kept + 2 * mine, block), BF16),
+        compiler_params=limit,
+    )(exchange(grad, "z"), logits)
+    got = exchange(got, LANE)
     logits, grad = pl.pallas_call(
         finish,
         out_shape=(

time: 143 us -> 139 us (0.972)
  blocking collectives: 46.1 us -> 74.6 us
  waiting for transfers between devices: 37.1 us -> 18.4 us
  starting transfers between devices: 35.7 us -> 24.9 us
  local copies, waits for them, and re-layouts: 8.53 us -> 6.65 us
    all_to_all x2 -> x4, blocking collectives: 46.1 us -> 74.6 us  [exchange(): return lax.all_to_all(parts, axis, 0, 0, tiled=True)]
    all_to_all x5 -> x3, waiting for transfers between devices: 37.1 us -> 18.4 us  [exchange(): return lax.all_to_all(parts, axis, 0, 0, tiled=True)]
    all_to_all x5 -> x3, starting transfers between devices: 35.7 us -> 24.9 us  [exchange(): return lax.all_to_all(parts, axis, 0, 0, tiled=True)]
    unnamed x18 -> x10, local copies, waits for them, and re-layouts: 5.88 us -> 4.25 us
  transfers between devices with their start and end apart: 5 -> 3, of which waited for: 5 -> 3; matrix products, arithmetic and copies ran while one was open for 6% -> 6% of each run, Pallas kernels for 1% -> 0%
where the time goes in v9:
time: 139 us; the launch traced here: 138 us
  blocking collectives  74.6 us (54%)
  starting transfers between devices  24.9 us (18%)
  waiting for transfers between devices  18.4 us (13%)
  Pallas kernels  9.44 us (7%)
  local copies, waits for them, and re-layouts  6.65 us (5%)
  matrix products  2.72 us (2%)
    all_to_all x4, blocking collectives, exchange(): return lax.all_to_all(parts, axis, 0, 0, tiled=True)  74.6 us
    all_to_all x3, starting transfers between devices, exchange(): return lax.all_to_all(parts, axis, 0, 0, tiled=True)  24.9 us
    all_to_all x3, waiting for transfers between devices, exchange(): return lax.all_to_all(parts, axis, 0, 0, tiled=True)  18.4 us
    unnamed x10, local copies, waits for them, and re-layouts  4.25 us
    pallas_call x1, Pallas kernels, per_device(): pl.pallas_call(middle, in_specs=[whole, away], scratch_shapes=[pltpu.VMEM...  3.15 us
    pallas_call x1, Pallas kernels, per_device(): pl.pallas_call(functools.partial(first, xs, by_lane), grid=(1,), in_specs...  2.89 us
  transfers between devices with their start and end apart: 3, of which 3 were waited for; matrix products, arithmetic and copies ran while one was open for 6% of the time, Pallas kernels for 0%

profile of v9, /device:TPU:1, one launch (start us, length us, event | category | flops | bytes accessed | tf_op | source)
XLA Modules:
  0.0 138.4 jit_solution(13197040271394125358)
XLA Ops:
  0.6 0.0 copy-start
  0.6 1.6 %shard_map.103 = bf16[8,96,128]{2,1,0:T(8,128)(2,1)} custom-call(bf16[64,128]{1,0:T(8,128)(2,1)} %bitcast.43, bf16[16,153]{1,0:T(8,128)(2,1)} %cot_in.1), custom_call_target="tpu_custom_call" | custom-call | tf_op jit(solution)/shard_map/pallas_call | solution.py:235
  2.2 13.8 %all-to-all-start = ((bf16[8,96,128]{2,1,0:T(8,128)(2,1)}), bf16[8,96,128]{2,1,0:T(8,128)(2,1)S(1)}, u32[]{:S(2)}, u32[]{:S(2)}) async-start(bf16[8,96,128]{2,1,0:T(8,128)(2,1)} %shard_map.103), calls=%async_computation | async-start | bytes 393216 | tf_op jit(solution)/shard_map/all_to_all | solution.py:15
  16.1 0.8 copy.16
  16.8 0.1 reshape.41
  16.9 2.3 %gather_fusion = bf16[96,8,128]{2,1,0:T(8,128)(2,1)} fusion(bf16[8,96,128]{2,0,1:T(8,128)(2,1)} %bitcast.41, s32[1024]{0:T(1024)S(1)} %pad_clamp_fusion), kind=kCustom, calls=%fused_computation | custom fusion | bytes 393600 | tf_op jit(solution)/shard_map/gather | solution.py:249
  19.2 0.0 copy-done
  19.2 2.5 %fusion.1.agg_in = bf16[12,8,128]{2,1,0:T(8,128)(2,1)} fusion(bf16[8,12,8,128]{3,0,2,1:T(8,128)(2,1)} %bitcast.42, bf16[12,8,128,128]{3,2,1,0:T(8,128)(2,1)S(1)} %copy-done), kind=kOutput, calls=%fused_computation.4 | convolution fusion | flops 25178112 | bytes 3366912 | tf_op jit(solution)/shard_map/fhks,hkts->hft/dot_general | solution.py:23
  21.7 0.3 all-to-all-done.got
  22.0 0.0 copy-start.3
  22.0 0.7 copy-done.3
  22.7 2.9 %shard_map.104 = (bf16[12,176,128]{2,1,0:T(8,128)(2,1)}, bf16[128,384]{1,0:T(8,128)(2,1)}) custom-call(s32[4,12]{1,0:T(4,128)} %bitcast.44, bf16[8,96,128]{2,1,0:T(8,128)(2,1)} %copy-done.3, bf16[12,8,128]{2,1,0:T(8,128)(2,1)} %fusion.1.agg_in, bf16[8,12288]{1,0:T(8,128)(2,1)} %own.1, bf16[2,8,1024]{2,1,0:T(8,128)(2,1)} %w_in.1), custom_call_target="tpu_custom_call" | custom-call | tf_op jit(solution)/shard_map/pallas_call | solution.py:259
  25.6 29.6 %all_to_all.35 = bf16[12,176,128]{2,1,0:T(8,128)(2,1)S(1)} all-to-all(bf16[12,176,128]{2,1,0:T(8,128)(2,1)} %get-tuple-element.10), channel_id=1, replica_groups=mesh['x'=4,'z'=12,'c'=2,'node'=8] {'z'}, dimensions={0} | all-to-all | bytes 1081344 | tf_op jit(solution)/shard_map/all_to_all | solution.py:15
  55.2 0.3 fusion
  55.6 0.9 pad_maximum_fusion
  56.4 7.5 %all-to-all-start.2 = ((bf16[8,304,128]{2,1,0:T(8,128)(2,1)}), bf16[8,304,128]{2,1,0:T(8,128)(2,1)}, u32[]{:S(2)}, u32[]{:S(2)}) async-start(bf16[8,304,128]{2,1,0:T(8,128)(2,1)} %pad_maximum_fusion), calls=%async_computation.2 | async-start | bytes 1245184 | tf_op jit(solution)/shard_map/all_to_all | solution.py:15
  63.9 2.1 %copy.33 = bf16[2,1024,153]{1,2,0:T(8,128)(2,1)} copy(bf16[2,1024,153]{1,0,2:T(2,128)(2,1)} %param.14) | data formatting | bytes 1253376 | tf_op args[6]
  66.0 0.0 copy-start.1
  66.0 8.6 %all-to-all-done.2.got = bf16[8,304,128]{2,1,0:T(8,128)(2,1)} async-done(((bf16[8,304,128]{2,1,0:T(8,128)(2,1)}), bf16[8,304,128]{2,1,0:T(8,128)(2,1)}, u32[]{:S(2)}, u32[]{:S(2)}) %all-to-all-start.2) | async-done | bytes 622624 | tf_op jit(solution)/shard_map/all_to_all | solution.py:15
  74.5 3.2 %shard_map.105 = (bf16[12,64,128]{2,1,0:T(8,128)(2,1)}, bf16[16,1024]{1,0:T(8,128)(2,1)}, f32[16,153]{1,0:T(8,128)}) custom-call(bf16[8,304,128]{2,1,0:T(8,128)(2,1)} %all-to-all-done.2.got, bf16[2,153,1024]{2,1,0:T(8,128)(2,1)} %bitcast.36), custom_call_target="tpu_custom_call" | custom-call | tf_op jit(solution)/shard_map/pallas_call | solution.py:292
  77.7 15.9 %all_to_all.36.got = bf16[12,64,128]{2,1,0:T(8,128)(2,1)S(1)} all-to-all(bf16[12,64,128]{2,1,0:T(8,128)(2,1)} %get-tuple-element.12), channel_id=1, replica_groups=mesh['x'=4,'z'=12,'c'=2,'node'=8] {'z'}, dimensions={0} | all-to-all | bytes 393216 | tf_op jit(solution)/shard_map/all_to_all | solution.py:15
  93.6 14.0 %all_to_all.37.got = f32[8,16,128]{2,1,0:T(8,128)S(1)} all-to-all(f32[8,16,128]{2,1,0:T(8,128)S(1)} %shard_map.106), channel_id=1, replica_groups=mesh['x'=4,'z'=12,'c'=2,'node'=8] {'node'}, dimensions={0} | all-to-all | bytes 131072 | tf_op jit(solution)/shard_map/all_to_all | solution.py:15
  107.5 0.6 shard_map.107
  108.2 3.6 %all-to-all-start.5 = ((bf16[12,16,128]{2,1,0:T(8,128)(2,1)}), bf16[12,16,128]{2,1,0:T(8,128)(2,1)S(1)}, u32[]{:S(2)}, u32[]{:S(2)}) async-start(bf16[12,16,128]{2,1,0:T(8,128)(2,1)} %shard_map.107), calls=%async_computation.5 | async-start | bytes 98304 | tf_op jit(solution)/shard_map/all_to_all | solution.py:15
  111.8 0.0 copy-done.1
  111.8 0.2 shard_map.108.logits
  112.0 9.5 %all-to-all-done.5.grad = bf16[12,16,128]{2,1,0:T(8,128)(2,1)S(1)} async-done(((bf16[12,16,128]{2,1,0:T(8,128)(2,1)}), bf16[12,16,128]{2,1,0:T(8,128)(2,1)S(1)}, u32[]{:S(2)}, u32[]{:S(2)}) %all-to-all-start.5) | async-done | bytes 49184 | tf_op jit(solution)/shard_map/all_to_all | solution.py:15
  121.6 15.2 %all_to_all.38.got = bf16[8,192,128]{2,1,0:T(8,128)(2,1)S(1)} all-to-all(bf16[8,192,128]{2,1,0:T(8,128)(2,1)S(1)} %shard_map.109), channel_id=1, replica_groups=mesh['x'=4,'z'=12,'c'=2,'node'=8] {'x','c'}, dimensions={0} | all-to-all | bytes 786432 | tf_op jit(solution)/shard_map/all_to_all | solution.py:15
  136.7 0.0 copy-start.2
  136.7 0.7 copy-done.2
  137.5 0.9 shard_map.110
  (9 shorter events, 0.2 us)
Async XLA Ops:
  0.6 18.6 %copy-start = (bf16[12,8,128,128]{3,2,1,0:T(8,128)(2,1)S(1)}, bf16[12,8,128,128]{3,2,1,0:T(8,128)(2,1)}, u32[]{:S(2)}) copy-start(bf16[12,8,128,128]{3,2,1,0:T(8,128)(2,1)} %param.10) | copy-start | bytes 9437188
  2.2 19.7 %all-to-all-start = ((bf16[8,96,128]{2,1,0:T(8,128)(2,1)}), bf16[8,96,128]{2,1,0:T(8,128)(2,1)S(1)}, u32[]{:S(2)}, u32[]{:S(2)}) async-start(bf16[8,96,128]{2,1,0:T(8,128)(2,1)} %shard_map.103), calls=%async_computation | async-start | bytes 393216 | tf_op jit(solution)/shard_map/all_to_all | solution.py:15
  22.0 0.7 copy-start.3
  56.4 18.1 %all-to-all-start.2 = ((bf16[8,304,128]{2,1,0:T(8,128)(2,1)}), bf16[8,304,128]{2,1,0:T(8,128)(2,1)}, u32[]{:S(2)}, u32[]{:S(2)}) async-start(bf16[8,304,128]{2,1,0:T(8,128)(2,1)} %pad_maximum_fusion), calls=%async_computation.2 | async-start | bytes 1245184 | tf_op jit(solution)/shard_map/all_to_all | solution.py:15
  66.0 45.8 %copy-start.1 = (bf16[128,384]{1,0:T(8,128)(2,1)S(1)}, bf16[128,384]{1,0:T(8,128)(2,1)}, u32[]{:S(2)}) copy-start(bf16[128,384]{1,0:T(8,128)(2,1)} %get-tuple-element.13.near) | copy-start | bytes 294916
  108.2 13.3 %all-to-all-start.5 = ((bf16[12,16,128]{2,1,0:T(8,128)(2,1)}), bf16[12,16,128]{2,1,0:T(8,128)(2,1)S(1)}, u32[]{:S(2)}, u32[]{:S(2)}) async-start(bf16[12,16,128]{2,1,0:T(8,128)(2,1)} %shard_map.107), calls=%async_computation.5 | async-start | bytes 98304 | tf_op jit(solution)/shard_map/all_to_all | solution.py:15
  136.7 0.7 copy-start.2

commit v10 on v9

--- a/solution.py
+++ b/solution.py
@@ -44,6 +44,18 @@
         sends[j, :rows] = edges[...]
         sends[j, rows : rows + mine] = cot[:, :block]
         sends[j, rows + mine :] = rest
+
+
+def pick_blocks(lists, tiles_in, chosen, tiles, sem):
+    copy = pltpu.make_async_copy(tiles_in, tiles, sem)
+    copy.start()
+    copy.wait()
+    fanout, blocks = lists.shape
+    block = chosen.shape[2]
+    for b in range(blocks):
+        for k in range(fanout):
+            at = pl.multiple_of(lists[k, b] * block, block)
+            chosen[b * fanout + k] = tiles[:, pl.ds(at, block)]
 
 
 def first(xs, by_lane, lists, got, agg_in, own, w_in, sends, edges_out, agg, w, sems):
@@ -170,12 +182,13 @@
         sends[n] = total
 
 
-def partial_logits(got, near, sends):
+def partial_logits(got, near, own_in, sends, own):
     lanes, block = sends.shape[0], sends.shape[2]
     mine = sends.shape[1] // 2
     cores = near.shape[1] // (got.shape[0] * mine)
     above = got.shape[1] - 2 * mine
     my_c = lax.axis_index("c")
+    own[...] = own_in[...]
     rows = []
     for z in range(got.shape[0]):
         product = jnp.concatenate([got[z, above : above + mine], got[z, above + mine :]], axis=1)
@@ -245,16 +258,15 @@
     )(adj_two.reshape(mine * listed, block), cotangent)
     near = exchange(got, LANE)
 
-    tiles = features.reshape(cols, sources // block, block)
-    chosen = lax.gather(
-        tiles,
-        list_one.reshape(-1, 1),
-        lax.GatherDimensionNumbers((0, 2), (1,), (1,)),
-        (cols, 1, block),
-        mode="promise_in_bounds",
-    )
-    chosen = chosen.reshape(cols, blocks, fanout, block)
-    agg = dot("fhks,hkts->hft", chosen, adj_one).astype(BF16)
+    chosen = pl.pallas_call(
+        pick_blocks,
+        in_specs=[scalars, away],
+        out_shape=jax.ShapeDtypeStruct((blocks * fanout, cols, block), BF16),
+        scratch_shapes=[pltpu.VMEM((cols, sources), BF16), pltpu.SemaphoreType.DMA],
+        compiler_params=limit,
+    )(list_one.T, features)
+    chosen = chosen.reshape(blocks, fanout, cols, block)
+    agg = dot("hkfs,hkts->hft", chosen, adj_one).astype(BF16)
     above = -(-(2 * cols + by_lane) // 16) * 16
     got, near = pl.pallas_call(
         functools.partial(first, xs, by_lane),
@@ -312,12 +324,14 @@
         compiler_params=limit,
     )(exchange(grad, "node"))
 
-    logits = pl.pallas_call(
+    logits, own_logits = pl.pallas_call(
         partial_logits,
-        in_specs=[whole, whole],
-        out_shape=jax.ShapeDtypeStruct((lanes, 2 * mine, block), BF16),
-        compiler_params=limit,
-    )(got, near)
+        out_shape=(
+            jax.ShapeDtypeStruct((lanes, 2 * mine, block), BF16),
+            jax.ShapeDtypeStruct((mine, cls), F32),
+        ),
+        compiler_params=limit,
+    )(got, near, own_logits)
 
     got = pl.pallas_call(
         last,

time: 139 us -> 139 us (level)
    gather x1 -> x0, local copies, waits for them, and re-layouts: 2.26 us -> none  [per_device(): lax.gather(tiles, list_one.reshape(-1, 1), lax.GatherDimensionNumbers((0,...]
    unnamed x10 -> x17, local copies, waits for them, and re-layouts: 4.25 us -> 5.69 us
  transfers between devices with their start and end apart: 3 -> 3, of which waited for: 3 -> 3; matrix products, arithmetic and copies ran while one was open for 6% -> 3% of each run, Pallas kernels for 0% -> 1%
where the time goes in v10:
time: 139 us; the launch traced here: 138 us
  blocking collectives  74.6 us (54%)
  starting transfers between devices  24.9 us (18%)
  waiting for transfers between devices  18.5 us (13%)
  Pallas kernels  10.4 us (7%)
  local copies, waits for them, and re-layouts  5.75 us (4%)
  matrix products  1.8 us (1%)
    all_to_all x4, blocking collectives, exchange(): return lax.all_to_all(parts, axis, 0, 0, tiled=True)  74.6 us
    all_to_all x3, starting transfers between devices, exchange(): return lax.all_to_all(parts, axis, 0, 0, tiled=True)  24.9 us
    all_to_all x3, waiting for transfers between devices, exchange(): return lax.all_to_all(parts, axis, 0, 0, tiled=True)  18.5 us
    unnamed x17, local copies, waits for them, and re-layouts  5.69 us
    pallas_call x1, Pallas kernels, per_device(): pl.pallas_call(middle, in_specs=[whole, away], scratch_shapes=[pltpu.VMEM...  3.15 us
    pallas_call x1, Pallas kernels, per_device(): pl.pallas_call(functools.partial(first, xs, by_lane), grid=(1,), in_specs...  2.89 us
  transfers between devices with their start and end apart: 3, of which 3 were waited for; matrix products, arithmetic and copies ran while one was open for 3% of the time, Pallas kernels for 1%

profile of v10, /device:TPU:1, one launch (start us, length us, event | category | flops | bytes accessed | tf_op | source)
XLA Modules:
  0.0 137.6 jit_solution(12230464199098929345)
XLA Ops:
  0.6 0.0 copy-start
  0.6 1.6 %shard_map.103 = bf16[8,96,128]{2,1,0:T(8,128)(2,1)} custom-call(bf16[64,128]{1,0:T(8,128)(2,1)} %bitcast.41, bf16[16,153]{1,0:T(8,128)(2,1)} %cot_in.1), custom_call_target="tpu_custom_call" | custom-call | tf_op jit(solution)/shard_map/pallas_call | solution.py:248
  2.2 13.8 %all-to-all-start = ((bf16[8,96,128]{2,1,0:T(8,128)(2,1)}), bf16[8,96,128]{2,1,0:T(8,128)(2,1)S(1)}, u32[]{:S(2)}, u32[]{:S(2)}) async-start(bf16[8,96,128]{2,1,0:T(8,128)(2,1)} %shard_map.103), calls=%async_computation | async-start | bytes 393216 | tf_op jit(solution)/shard_map/all_to_all | solution.py:15
  16.1 0.0 copy-start.1
  16.1 0.9 copy-done.1
  17.0 0.0 copy-start.6
  17.0 0.7 copy-done.6
  17.7 1.0 shard_map.104
  18.7 0.0 copy-done
  18.7 1.5 %fusion.1.agg_in = bf16[12,8,128]{2,1,0:T(8,128)(2,1)} fusion(bf16[12,8,8,128]{3,2,1,0:T(8,128)(2,1)S(1)} %bitcast.34, bf16[12,8,128,128]{3,2,1,0:T(8,128)(2,1)S(1)} %copy-done), kind=kOutput, calls=%fused_computation.3 | convolution fusion | flops 25178112 | bytes 3366912 | tf_op jit(solution)/shard_map/hkfs,hkts->hft/dot_general | solution.py:23
  20.2 1.7 %all-to-all-done.got = bf16[8,96,128]{2,1,0:T(8,128)(2,1)S(1)} async-done(((bf16[8,96,128]{2,1,0:T(8,128)(2,1)}), bf16[8,96,128]{2,1,0:T(8,128)(2,1)S(1)}, u32[]{:S(2)}, u32[]{:S(2)}) %all-to-all-start) | async-done | bytes 196640 | tf_op jit(solution)/shard_map/all_to_all | solution.py:15
  22.0 0.0 copy-start.7
  22.0 0.7 copy-done.7
  22.7 2.9 %shard_map.105 = (bf16[12,176,128]{2,1,0:T(8,128)(2,1)}, bf16[128,384]{1,0:T(8,128)(2,1)}) custom-call(s32[4,12]{1,0:T(4,128)} %bitcast.42, bf16[8,96,128]{2,1,0:T(8,128)(2,1)} %copy-done.7, bf16[12,8,128]{2,1,0:T(8,128)(2,1)} %fusion.1.agg_in, bf16[8,12288]{1,0:T(8,128)(2,1)} %own.1, bf16[2,8,1024]{2,1,0:T(8,128)(2,1)} %w_in.1), custom_call_target="tpu_custom_call" | custom-call | tf_op jit(solution)/shard_map/pallas_call | solution.py:271
  25.5 29.6 %all_to_all.35 = bf16[12,176,128]{2,1,0:T(8,128)(2,1)S(1)} all-to-all(bf16[12,176,128]{2,1,0:T(8,128)(2,1)} %get-tuple-element.12), channel_id=1, replica_groups=mesh['x'=4,'z'=12,'c'=2,'node'=8] {'z'}, dimensions={0} | all-to-all | bytes 1081344 | tf_op jit(solution)/shard_map/all_to_all | solution.py:15
  55.2 0.3 fusion
  55.6 0.9 pad_maximum_fusion
  56.4 7.4 %all-to-all-start.2 = ((bf16[8,304,128]{2,1,0:T(8,128)(2,1)}), bf16[8,304,128]{2,1,0:T(8,128)(2,1)}, u32[]{:S(2)}, u32[]{:S(2)}) async-start(bf16[8,304,128]{2,1,0:T(8,128)(2,1)} %pad_maximum_fusion), calls=%async_computation.2 | async-start | bytes 1245184 | tf_op jit(solution)/shard_map/all_to_all | solution.py:15
  63.9 2.1 %copy.27 = bf16[2,1024,153]{1,2,0:T(8,128)(2,1)} copy(bf16[2,1024,153]{1,0,2:T(2,128)(2,1)} %param.14) | data formatting | bytes 1253376 | tf_op args[6]
  65.9 0.0 copy-start.2
  65.9 8.6 %all-to-all-done.2.got = bf16[8,304,128]{2,1,0:T(8,128)(2,1)} async-done(((bf16[8,304,128]{2,1,0:T(8,128)(2,1)}), bf16[8,304,128]{2,1,0:T(8,128)(2,1)}, u32[]{:S(2)}, u32[]{:S(2)}) %all-to-all-start.2) | async-done | bytes 622624 | tf_op jit(solution)/shard_map/all_to_all | solution.py:15
  74.5 3.1 %shard_map.106 = (bf16[12,64,128]{2,1,0:T(8,128)(2,1)}, bf16[16,1024]{1,0:T(8,128)(2,1)}, f32[16,153]{1,0:T(8,128)}) custom-call(bf16[8,304,128]{2,1,0:T(8,128)(2,1)} %all-to-all-done.2.got, bf16[2,153,1024]{2,1,0:T(8,128)(2,1)} %bitcast.36), custom_call_target="tpu_custom_call" | custom-call | tf_op jit(solution)/shard_map/pallas_call | solution.py:304
  77.7 15.9 %all_to_all.36.got = bf16[12,64,128]{2,1,0:T(8,128)(2,1)S(1)} all-to-all(bf16[12,64,128]{2,1,0:T(8,128)(2,1)} %get-tuple-element.14), channel_id=1, replica_groups=mesh['x'=4,'z'=12,'c'=2,'node'=8] {'z'}, dimensions={0} | all-to-all | bytes 393216 | tf_op jit(solution)/shard_map/all_to_all | solution.py:15
  93.6 13.9 %all_to_all.37.got = f32[8,16,128]{2,1,0:T(8,128)S(1)} all-to-all(f32[8,16,128]{2,1,0:T(8,128)S(1)} %shard_map.107), channel_id=1, replica_groups=mesh['x'=4,'z'=12,'c'=2,'node'=8] {'node'}, dimensions={0} | all-to-all | bytes 131072 | tf_op jit(solution)/shard_map/all_to_all | solution.py:15
  107.5 0.6 shard_map.108
  108.2 3.6 %all-to-all-start.5 = ((bf16[12,16,128]{2,1,0:T(8,128)(2,1)}), bf16[12,16,128]{2,1,0:T(8,128)(2,1)S(1)}, u32[]{:S(2)}, u32[]{:S(2)}) async-start(bf16[12,16,128]{2,1,0:T(8,128)(2,1)} %shard_map.108), calls=%async_computation.5 | async-start | bytes 98304 | tf_op jit(solution)/shard_map/all_to_all | solution.py:15
  111.8 0.0 copy-done.2
  111.8 0.0 copy-start.3
  111.8 0.7 copy-done.3
  112.5 0.2 shard_map.109
  112.7 0.0 copy-start.4
  112.7 0.6 copy-done.4
  113.3 8.1 %all-to-all-done.5.grad = bf16[12,16,128]{2,1,0:T(8,128)(2,1)S(1)} async-done(((bf16[12,16,128]{2,1,0:T(8,128)(2,1)}), bf16[12,16,128]{2,1,0:T(8,128)(2,1)S(1)}, u32[]{:S(2)}, u32[]{:S(2)}) %all-to-all-start.5) | async-done | bytes 49184 | tf_op jit(solution)/shard_map/all_to_all | solution.py:15
  121.5 0.0 copy-start.5
  121.5 15.2 %all_to_all.38.got = bf16[8,192,128]{2,1,0:T(8,128)(2,1)S(1)} all-to-all(bf16[8,192,128]{2,1,0:T(8,128)(2,1)S(1)} %shard_map.110), channel_id=1, replica_groups=mesh['x'=4,'z'=12,'c'=2,'node'=8] {'x','c'}, dimensions={0} | all-to-all | bytes 786432 | tf_op jit(solution)/shard_map/all_to_all | solution.py:15
  136.7 0.0 copy-done.5
  136.7 0.9 shard_map.111
  (8 shorter events, 0.2 us)
Async XLA Ops:
  0.6 18.1 %copy-start = (bf16[12,8,128,128]{3,2,1,0:T(8,128)(2,1)S(1)}, bf16[12,8,128,128]{3,2,1,0:T(8,128)(2,1)}, u32[]{:S(2)}) copy-start(bf16[12,8,128,128]{3,2,1,0:T(8,128)(2,1)} %param.10) | copy-start | bytes 9437188
  2.2 19.7 %all-to-all-start = ((bf16[8,96,128]{2,1,0:T(8,128)(2,1)}), bf16[8,96,128]{2,1,0:T(8,128)(2,1)S(1)}, u32[]{:S(2)}, u32[]{:S(2)}) async-start(bf16[8,96,128]{2,1,0:T(8,128)(2,1)} %shard_map.103), calls=%async_computation | async-start | bytes 393216 | tf_op jit(solution)/shard_map/all_to_all | solution.py:15
  16.1 0.9 copy-start.1
  17.0 0.7 copy-start.6
  22.0 0.7 copy-start.7
  56.4 18.1 %all-to-all-start.2 = ((bf16[8,304,128]{2,1,0:T(8,128)(2,1)}), bf16[8,304,128]{2,1,0:T(8,128)(2,1)}, u32[]{:S(2)}, u32[]{:S(2)}) async-start(bf16[8,304,128]{2,1,0:T(8,128)(2,1)} %pad_maximum_fusion), calls=%async_computation.2 | async-start | bytes 1245184 | tf_op jit(solution)/shard_map/all_to_all | solution.py:15
  65.9 45.9 %copy-start.2 = (bf16[128,384]{1,0:T(8,128)(2,1)S(1)}, bf16[128,384]{1,0:T(8,128)(2,1)}, u32[]{:S(2)}) copy-start(bf16[128,384]{1,0:T(8,128)(2,1)} %get-tuple-element.15.near) | copy-start | bytes 294916
  108.2 13.3 %all-to-all-start.5 = ((bf16[12,16,128]{2,1,0:T(8,128)(2,1)}), bf16[12,16,128]{2,1,0:T(8,128)(2,1)S(1)}, u32[]{:S(2)}, u32[]{:S(2)}) async-start(bf16[12,16,128]{2,1,0:T(8,128)(2,1)} %shard_map.108), calls=%async_computation.5 | async-start | bytes 98304 | tf_op jit(solution)/shard_map/all_to_all | solution.py:15
  111.8 0.7 copy-start.3
  112.7 0.6 copy-start.4
  121.5 15.2 %copy-start.5 = (f32[16,153]{1,0:T(8,128)S(1)}, f32[16,153]{1,0:T(8,128)}, u32[]{:S(2)}) copy-start(f32[16,153]{1,0:T(8,128)} %copy-done.4) | copy-start | bytes 29380

commit v11 on v10

--- a/solution.py
+++ b/solution.py
@@ -46,25 +46,25 @@
         sends[j, rows + mine :] = rest
 
 
-def pick_blocks(lists, tiles_in, chosen, tiles, sem):
-    copy = pltpu.make_async_copy(tiles_in, tiles, sem)
-    copy.start()
-    copy.wait()
+def pick_blocks(lists, tiles_in, w_in, chosen, own, w, tiles, sems):
+    copies = [
+        pltpu.make_async_copy(tiles_in, tiles, sems.at[0]),
+        pltpu.make_async_copy(w_in, w, sems.at[1]),
+    ]
+    for copy in copies:
+        copy.start()
+    for copy in copies:
+        copy.wait()
     fanout, blocks = lists.shape
     block = chosen.shape[2]
+    own[...] = tiles[:, : blocks * block]
     for b in range(blocks):
         for k in range(fanout):
             at = pl.multiple_of(lists[k, b] * block, block)
             chosen[b * fanout + k] = tiles[:, pl.ds(at, block)]
 
 
-def first(xs, by_lane, lists, got, agg_in, own, w_in, sends, edges_out, agg, w, sems):
-    copies = [
-        pltpu.make_async_copy(agg_in, agg, sems.at[0]),
-        pltpu.make_async_copy(w_in, w, sems.at[1]),
-    ]
-    for copy in copies:
-        copy.start()
+def first(xs, by_lane, lists, got, agg, own, w, sends, edges_out):
     lanes, _, block = got.shape
     blocks, cols = agg.shape[:2]
     listed = lists.shape[0]
@@ -102,8 +102,6 @@
         take = jnp.where(fits & (to == my_x * mids + mid), 1.0, 0.0).astype(BF16)
         take = jnp.dot(take, near, preferred_element_type=F32).astype(BF16)
         edges_out[:, mid * block : (mid + 1) * block] = take
-    for copy in copies:
-        copy.wait()
     pad = jnp.zeros((sends.shape[1] - block - 2 * cols - by_lane, block), F32)
     parts = []
     for b in range(blocks):
@@ -258,38 +256,30 @@
     )(adj_two.reshape(mine * listed, block), cotangent)
     near = exchange(got, LANE)
 
-    chosen = pl.pallas_call(
+    chosen, own, w = pl.pallas_call(
         pick_blocks,
-        in_specs=[scalars, away],
-        out_shape=jax.ShapeDtypeStruct((blocks * fanout, cols, block), BF16),
-        scratch_shapes=[pltpu.VMEM((cols, sources), BF16), pltpu.SemaphoreType.DMA],
-        compiler_params=limit,
-    )(list_one.T, features)
+        in_specs=[scalars, away, away],
+        out_shape=(
+            jax.ShapeDtypeStruct((blocks * fanout, cols, block), BF16),
+            jax.ShapeDtypeStruct((cols, blocks * block), BF16),
+            jax.ShapeDtypeStruct(w_one.shape, BF16),
+        ),
+        scratch_shapes=[pltpu.VMEM((cols, sources), BF16), pltpu.SemaphoreType.DMA((2,))],
+        compiler_params=limit,
+    )(list_one.T, features, w_one)
     chosen = chosen.reshape(blocks, fanout, cols, block)
     agg = dot("hkfs,hkts->hft", chosen, adj_one).astype(BF16)
     above = -(-(2 * cols + by_lane) // 16) * 16
     got, near = pl.pallas_call(
         functools.partial(first, xs, by_lane),
-        grid=(1,),
-        in_specs=[
-            scalars,
-            whole,
-            away,
-            pl.BlockSpec((cols, blocks * block), lambda i: (0, 0)),
-            away,
-        ],
+        in_specs=[scalars, whole, whole, whole, whole],
         out_specs=(whole, whole),
         out_shape=(
             jax.ShapeDtypeStruct((blocks, above + 2 * cols * lanes, block), BF16),
             jax.ShapeDtypeStruct((block, mids * block), BF16),
         ),
-        scratch_shapes=[
-            pltpu.VMEM(agg.shape, BF16),
-            pltpu.VMEM(w_one.shape, BF16),
-            pltpu.SemaphoreType.DMA((2,)),
-        ],
-        compiler_params=wide_limit,
-    )(list_two.T, near, agg, features, w_one)
+        compiler_params=limit,
+    )(list_two.T, near, agg, own, w)
     got = exchange(got, "z")
     inputs, weights = got[:, : 2 * cols], got[:, above:]
     back = got[:, 2 * cols : 2 * cols + by_lane]

time: 139 us -> 136 us (0.978)
  Pallas kernels: 10.4 us -> 9.01 us
    pallas_call x2, Pallas kernels: 3.88 us -> 2.47 us  [the longest x1 1.42 us: per_device(): pl.pallas_call(functools.partial(first, xs, by_lane), in_specs=[scalars,...]
  transfers between devices with their start and end apart: 3 -> 3, of which waited for: 3 -> 3; matrix products, arithmetic and copies ran while one was open for 3% -> 2% of each run, Pallas kernels for 1% -> 1%
where the time goes in v11:
time: 136 us; the launch traced here: 135 us
  blocking collectives  74.4 us (55%)
  starting transfers between devices  24.9 us (18%)
  waiting for transfers between devices  18.3 us (13%)
  Pallas kernels  9.01 us (7%)
  local copies, waits for them, and re-layouts  5.83 us (4%)
    all_to_all x4, blocking collectives, exchange(): return lax.all_to_all(parts, axis, 0, 0, tiled=True)  74.4 us
    all_to_all x3, starting transfers between devices, exchange(): return lax.all_to_all(parts, axis, 0, 0, tiled=True)  24.9 us
    all_to_all x3, waiting for transfers between devices, exchange(): return lax.all_to_all(parts, axis, 0, 0, tiled=True)  18.3 us
    unnamed x17, local copies, waits for them, and re-layouts  5.77 us
    pallas_call x1, Pallas kernels, per_device(): pl.pallas_call(middle, in_specs=[whole, away], scratch_shapes=[pltpu.VMEM...  3.14 us
  transfers between devices with their start and end apart: 3, of which 3 were waited for; matrix products, arithmetic and copies ran while one was open for 2% of the time, Pallas kernels for 1%

profile of v11, /device:TPU:1, one launch (start us, length us, event | category | flops | bytes accessed | tf_op | source)
XLA Modules:
  0.0 135.3 jit_solution(16123670133985011430)
XLA Ops:
  0.6 0.0 copy-start
  0.6 1.6 %shard_map.103 = bf16[8,96,128]{2,1,0:T(8,128)(2,1)} custom-call(bf16[64,128]{1,0:T(8,128)(2,1)} %bitcast.42, bf16[16,153]{1,0:T(8,128)(2,1)} %cot_in.1), custom_call_target="tpu_custom_call" | custom-call | tf_op jit(solution)/shard_map/pallas_call | solution.py:246
  2.2 13.8 %all-to-all-start = ((bf16[8,96,128]{2,1,0:T(8,128)(2,1)}), bf16[8,96,128]{2,1,0:T(8,128)(2,1)S(1)}, u32[]{:S(2)}, u32[]{:S(2)}) async-start(bf16[8,96,128]{2,1,0:T(8,128)(2,1)} %shard_map.103), calls=%async_computation | async-start | bytes 393216 | tf_op jit(solution)/shard_map/all_to_all | solution.py:15
  16.1 0.0 copy-start.1
  16.1 0.9 copy-done.1
  17.0 0.0 copy-start.2
  17.0 0.8 copy-done.2
  17.8 0.0 copy-start.6
  17.8 0.7 copy-done.6
  18.4 1.0 shard_map.104
  19.5 0.0 copy-done
  19.5 0.0 copy-start.7
  19.5 0.9 fusion.1.agg
  20.4 1.6 %all-to-all-done.got = bf16[8,96,128]{2,1,0:T(8,128)(2,1)S(1)} async-done(((bf16[8,96,128]{2,1,0:T(8,128)(2,1)}), bf16[8,96,128]{2,1,0:T(8,128)(2,1)S(1)}, u32[]{:S(2)}, u32[]{:S(2)}) %all-to-all-start) | async-done | bytes 196640 | tf_op jit(solution)/shard_map/all_to_all | solution.py:15
  22.0 0.0 copy-done.7
  22.0 1.4 %shard_map.105 = (bf16[12,176,128]{2,1,0:T(8,128)(2,1)S(1)}, bf16[128,384]{1,0:T(8,128)(2,1)S(1)}) custom-call(s32[4,12]{1,0:T(4,128)S(1)} %bitcast.36, bf16[8,96,128]{2,1,0:T(8,128)(2,1)S(1)} %all-to-all-done.got, bf16[12,8,128]{2,1,0:T(8,128)(2,1)S(1)} %fusion.1.agg, bf16[8,1536]{1,0:T(8,128)(2,1)S(1)} %get-tuple-element.16.own, ...), custom_call_target="tpu_custom_call" | custom-call | tf_op jit(solution)/shard_map/pallas_call | solution.py:273
  23.4 29.4 %all_to_all.35 = bf16[12,176,128]{2,1,0:T(8,128)(2,1)S(1)} all-to-all(bf16[12,176,128]{2,1,0:T(8,128)(2,1)S(1)} %get-tuple-element.18), channel_id=1, replica_groups=mesh['x'=4,'z'=12,'c'=2,'node'=8] {'z'}, dimensions={0} | all-to-all | bytes 1081344 | tf_op jit(solution)/shard_map/all_to_all | solution.py:15
  52.9 0.3 fusion
  53.2 0.9 pad_maximum_fusion
  54.1 7.4 %all-to-all-start.2 = ((bf16[8,304,128]{2,1,0:T(8,128)(2,1)}), bf16[8,304,128]{2,1,0:T(8,128)(2,1)}, u32[]{:S(2)}, u32[]{:S(2)}) async-start(bf16[8,304,128]{2,1,0:T(8,128)(2,1)} %pad_maximum_fusion), calls=%async_computation.2 | async-start | bytes 1245184 | tf_op jit(solution)/shard_map/all_to_all | solution.py:15
  61.5 2.1 %copy.27 = bf16[2,1024,153]{1,2,0:T(8,128)(2,1)} copy(bf16[2,1024,153]{1,0,2:T(2,128)(2,1)} %param.14) | data formatting | bytes 1253376 | tf_op args[6]
  63.6 8.6 %all-to-all-done.2.got = bf16[8,304,128]{2,1,0:T(8,128)(2,1)} async-done(((bf16[8,304,128]{2,1,0:T(8,128)(2,1)}), bf16[8,304,128]{2,1,0:T(8,128)(2,1)}, u32[]{:S(2)}, u32[]{:S(2)}) %all-to-all-start.2) | async-done | bytes 622624 | tf_op jit(solution)/shard_map/all_to_all | solution.py:15
  72.2 3.1 %shard_map.106 = (bf16[12,64,128]{2,1,0:T(8,128)(2,1)}, bf16[16,1024]{1,0:T(8,128)(2,1)}, f32[16,153]{1,0:T(8,128)}) custom-call(bf16[8,304,128]{2,1,0:T(8,128)(2,1)} %all-to-all-done.2.got, bf16[2,153,1024]{2,1,0:T(8,128)(2,1)} %bitcast.37), custom_call_target="tpu_custom_call" | custom-call | tf_op jit(solution)/shard_map/pallas_call | solution.py:294
  75.3 15.9 %all_to_all.36.got = bf16[12,64,128]{2,1,0:T(8,128)(2,1)S(1)} all-to-all(bf16[12,64,128]{2,1,0:T(8,128)(2,1)} %get-tuple-element.20), channel_id=1, replica_groups=mesh['x'=4,'z'=12,'c'=2,'node'=8] {'z'}, dimensions={0} | all-to-all | bytes 393216 | tf_op jit(solution)/shard_map/all_to_all | solution.py:15
  91.2 14.0 %all_to_all.37.got = f32[8,16,128]{2,1,0:T(8,128)S(1)} all-to-all(f32[8,16,128]{2,1,0:T(8,128)S(1)} %shard_map.107), channel_id=1, replica_groups=mesh['x'=4,'z'=12,'c'=2,'node'=8] {'node'}, dimensions={0} | all-to-all | bytes 131072 | tf_op jit(solution)/shard_map/all_to_all | solution.py:15
  105.2 0.6 shard_map.108
  105.8 3.6 %all-to-all-start.5 = ((bf16[12,16,128]{2,1,0:T(8,128)(2,1)}), bf16[12,16,128]{2,1,0:T(8,128)(2,1)S(1)}, u32[]{:S(2)}, u32[]{:S(2)}) async-start(bf16[12,16,128]{2,1,0:T(8,128)(2,1)} %shard_map.108), calls=%async_computation.5 | async-start | bytes 98304 | tf_op jit(solution)/shard_map/all_to_all | solution.py:15
  109.4 0.0 copy-start.3
  109.4 0.7 copy-done.3
  110.1 0.2 shard_map.109
  110.3 0.0 copy-start.4
  110.4 0.6 copy-done.4
  111.0 8.2 %all-to-all-done.5.grad = bf16[12,16,128]{2,1,0:T(8,128)(2,1)S(1)} async-done(((bf16[12,16,128]{2,1,0:T(8,128)(2,1)}), bf16[12,16,128]{2,1,0:T(8,128)(2,1)S(1)}, u32[]{:S(2)}, u32[]{:S(2)}) %all-to-all-start.5) | async-done | bytes 49184 | tf_op jit(solution)/shard_map/all_to_all | solution.py:15
  119.1 0.0 copy-start.5
  119.2 15.2 %all_to_all.38.got = bf16[8,192,128]{2,1,0:T(8,128)(2,1)S(1)} all-to-all(bf16[8,192,128]{2,1,0:T(8,128)(2,1)S(1)} %shard_map.110), channel_id=1, replica_groups=mesh['x'=4,'z'=12,'c'=2,'node'=8] {'x','c'}, dimensions={0} | all-to-all | bytes 786432 | tf_op jit(solution)/shard_map/all_to_all | solution.py:15
  134.4 0.0 copy-done.5
  134.4 0.9 shard_map.111
  (8 shorter events, 0.2 us)
Async XLA Ops:
  0.6 18.9 %copy-start = (bf16[12,8,128,128]{3,2,1,0:T(8,128)(2,1)S(1)}, bf16[12,8,128,128]{3,2,1,0:T(8,128)(2,1)}, u32[]{:S(2)}) copy-start(bf16[12,8,128,128]{3,2,1,0:T(8,128)(2,1)} %param.10) | copy-start | bytes 9437188
  2.2 19.7 %all-to-all-start = ((bf16[8,96,128]{2,1,0:T(8,128)(2,1)}), bf16[8,96,128]{2,1,0:T(8,128)(2,1)S(1)}, u32[]{:S(2)}, u32[]{:S(2)}) async-start(bf16[8,96,128]{2,1,0:T(8,128)(2,1)} %shard_map.103), calls=%async_computation | async-start | bytes 393216 | tf_op jit(solution)/shard_map/all_to_all | solution.py:15
  16.1 0.9 copy-start.1
  17.0 0.8 copy-start.2
  17.8 0.7 copy-start.6
  19.5 2.5 %copy-start.7 = (s32[12,4]{0,1:T(4,128)S(1)}, s32[12,4]{0,1:T(4,128)}, u32[]{:S(2)}) copy-start(s32[12,4]{0,1:T(4,128)} %param.13) | copy-start | bytes 580
  54.1 18.1 %all-to-all-start.2 = ((bf16[8,304,128]{2,1,0:T(8,128)(2,1)}), bf16[8,304,128]{2,1,0:T(8,128)(2,1)}, u32[]{:S(2)}, u32[]{:S(2)}) async-start(bf16[8,304,128]{2,1,0:T(8,128)(2,1)} %pad_maximum_fusion), calls=%async_computation.2 | async-start | bytes 1245184 | tf_op jit(solution)/shard_map/all_to_all | solution.py:15
  105.8 13.3 %all-to-all-start.5 = ((bf16[12,16,128]{2,1,0:T(8,128)(2,1)}), bf16[12,16,128]{2,1,0:T(8,128)(2,1)S(1)}, u32[]{:S(2)}, u32[]{:S(2)}) async-start(bf16[12,16,128]{2,1,0:T(8,128)(2,1)} %shard_map.108), calls=%async_computation.5 | async-start | bytes 98304 | tf_op jit(solution)/shard_map/all_to_all | solution.py:15
  109.4 0.7 copy-start.3
  110.3 0.6 copy-start.4
  119.1 15.2 %copy-start.5 = (f32[16,153]{1,0:T(8,128)S(1)}, f32[16,153]{1,0:T(8,128)}, u32[]{:S(2)}) copy-start(f32[16,153]{1,0:T(8,128)} %copy-done.4) | copy-start | bytes 29380

commit v12 on v11

--- a/solution.py
+++ b/solution.py
@@ -102,7 +102,7 @@
         take = jnp.where(fits & (to == my_x * mids + mid), 1.0, 0.0).astype(BF16)
         take = jnp.dot(take, near, preferred_element_type=F32).astype(BF16)
         edges_out[:, mid * block : (mid + 1) * block] = take
-    pad = jnp.zeros((sends.shape[1] - block - 2 * cols - by_lane, block), F32)
+    pad = jnp.zeros((-(2 * cols + by_lane) % 16, block), F32)
     parts = []
     for b in range(blocks):
         mine_b = own[:, b * block : (b + 1) * block].astype(F32)
@@ -119,12 +119,14 @@
         move = jnp.where(fits & (row % block // strip == low), 1.0, 0.0).astype(BF16)
         moved = jnp.dot(parts, move, preferred_element_type=F32).astype(BF16)
         for mid in range(mids):
-            sends[mid * strips + low, :high] = moved[mid * high : (mid + 1) * high]
+            at = mid * high + 2 * cols
+            sends[mid * strips + low, : 2 * cols] = moved[mid * high : at]
+            sends[mid * strips + low, 2 * cols + block :] = moved[at : at + by_lane]
     wide = w.shape[2] // lanes
     w = [w[i, :, j * wide : (j + 1) * wide].astype(F32) for i in range(2) for j in range(lanes)]
     w = jnp.concatenate(w, axis=0).astype(BF16)
     for z in range(blocks):
-        sends[z, high:] = w
+        sends[z, 2 * cols : 2 * cols + block] = w
 
 
 def sum_nodes(got, sends):
@@ -139,8 +141,8 @@
     copy = pltpu.make_async_copy(w_in, w, sem)
     copy.start()
     lanes, wide = got.shape[0], got.shape[2]
-    blocks, by_z = sends.shape[0], sends.shape[1] // 4
-    block, mine = got.shape[2], rows.shape[0]
+    blocks, block, mine = sends.shape[0], got.shape[2], rows.shape[0]
+    by_z = (got.shape[1] - 2 * block) // 2 * lanes // blocks
     pre = got[0, : 2 * block].astype(F32)
     for j in range(1, lanes):
         pre = pre + got[j, : 2 * block].astype(F32)
@@ -164,10 +166,13 @@
     product = lax.dot_general(rows[...], w[0], over, preferred_element_type=F32)
     logits[...] = lax.dot_general(rows[...], w[1], over, preferred_element_type=F32)
     pad = jnp.zeros((mine, 2 * block - product.shape[1]), F32)
-    product = jnp.concatenate([product, pad], axis=1).astype(BF16)
+    product = jnp.concatenate([product, pad], axis=1)
+    rest = product[:, block : block + block // 2]
+    rest = jnp.concatenate([rest[: mine // 2], rest[mine // 2 :]], axis=1).astype(BF16)
+    product = product[:, :block].astype(BF16)
     for z in range(blocks):
-        sends[z, 2 * by_z : 2 * by_z + mine] = product[:, :block]
-        sends[z, 2 * by_z + mine :] = product[:, block:]
+        sends[z, 2 * by_z : 2 * by_z + mine] = product
+        sends[z, 2 * by_z + mine :] = rest
 
 
 def sum_z(got, sends):
@@ -184,12 +189,16 @@
     lanes, block = sends.shape[0], sends.shape[2]
     mine = sends.shape[1] // 2
     cores = near.shape[1] // (got.shape[0] * mine)
-    above = got.shape[1] - 2 * mine
+    above = got.shape[1] - mine - mine // 2
+    none = jnp.zeros((mine, block // 2), F32)
     my_c = lax.axis_index("c")
     own[...] = own_in[...]
     rows = []
     for z in range(got.shape[0]):
-        product = jnp.concatenate([got[z, above : above + mine], got[z, above + mine :]], axis=1)
+        rest = got[z, above + mine :].astype(F32)
+        rest = jnp.concatenate([rest[:, : block // 2], rest[:, block // 2 :]], axis=0)
+        rest = jnp.concatenate([rest, none], axis=1).astype(BF16)
+        product = jnp.concatenate([got[z, above : above + mine], rest], axis=1)
         for c in range(cores):
             rows.append(jnp.where(my_c == c, product, jnp.zeros_like(product)))
     rows = jnp.concatenate(rows, axis=0)
@@ -269,20 +278,19 @@
     )(list_one.T, features, w_one)
     chosen = chosen.reshape(blocks, fanout, cols, block)
     agg = dot("hkfs,hkts->hft", chosen, adj_one).astype(BF16)
-    above = -(-(2 * cols + by_lane) // 16) * 16
+    above = 2 * cols + 2 * cols * lanes
     got, near = pl.pallas_call(
         functools.partial(first, xs, by_lane),
         in_specs=[scalars, whole, whole, whole, whole],
         out_specs=(whole, whole),
         out_shape=(
-            jax.ShapeDtypeStruct((blocks, above + 2 * cols * lanes, block), BF16),
+            jax.ShapeDtypeStruct((blocks, above + by_lane, block), BF16),
             jax.ShapeDtypeStruct((block, mids * block), BF16),
         ),
         compiler_params=limit,
     )(list_two.T, near, agg, own, w)
     got = exchange(got, "z")
-    inputs, weights = got[:, : 2 * cols], got[:, above:]
-    back = got[:, 2 * cols : 2 * cols + by_lane]
+    inputs, weights, back = jnp.split(got, (2 * cols, above), axis=1)
     inputs = inputs.reshape(blocks, 2, cols, block)
     weights = weights.reshape(blocks, 2, lanes, cols, wide)
     part = dot("zikr,zijkh->jrh", inputs, weights).astype(BF16)
@@ -296,7 +304,7 @@
         in_specs=[whole, away],
         scratch_shapes=[pltpu.VMEM((2, cls, hid), BF16), pltpu.SemaphoreType.DMA],
         out_shape=(
-            jax.ShapeDtypeStruct((blocks, 4 * by_z, block), BF16),
+            jax.ShapeDtypeStruct((blocks, 2 * by_z + mine + mine // 2, block), BF16),
             jax.ShapeDtypeStruct((mine, hid), BF16),
             jax.ShapeDtypeStruct((mine, cls), F32),
         ),

time: 136 us -> 135 us (level)
  blocking collectives: 74.4 us -> 72.3 us
    all_to_all x4, blocking collectives: 74.4 us -> 72.3 us  [exchange(): return lax.all_to_all(parts, axis, 0, 0, tiled=True)]
    unnamed x17 -> x13, local copies, waits for them, and re-layouts: 5.77 us -> 5.17 us
where the time goes in v12:
time: 135 us; the launch traced here: 134 us
  blocking collectives  72.3 us (54%)
  starting transfers between devices  25.7 us (19%)
  waiting for transfers between devices  18.9 us (14%)
  Pallas kernels  9.13 us (7%)
  local copies, waits for them, and re-layouts  5.23 us (4%)
    all_to_all x4, blocking collectives, exchange(): return lax.all_to_all(parts, axis, 0, 0, tiled=True)  72.3 us
    all_to_all x3, starting transfers between devices, exchange(): return lax.all_to_all(parts, axis, 0, 0, tiled=True)  25.7 us
    all_to_all x3, waiting for transfers between devices, exchange(): return lax.all_to_all(parts, axis, 0, 0, tiled=True)  18.9 us
    unnamed x13, local copies, waits for them, and re-layouts  5.17 us
    pallas_call x1, Pallas kernels, per_device(): pl.pallas_call(middle, in_specs=[whole, away], scratch_shapes=[pltpu.VMEM...  3.2 us
  transfers between devices with their start and end apart: 3, of which 3 were waited for; matrix products, arithmetic and copies ran while one was open for 2% of the time, Pallas kernels for 1%

profile of v12, /device:TPU:1, one launch (start us, length us, event | category | flops | bytes accessed | tf_op | source)
XLA Modules:
  0.0 134.2 jit_solution(10824085161139871517)
XLA Ops:
  0.6 0.0 copy-start
  0.6 1.6 %shard_map.103 = bf16[8,96,128]{2,1,0:T(8,128)(2,1)} custom-call(bf16[64,128]{1,0:T(8,128)(2,1)} %bitcast.42, bf16[16,153]{1,0:T(8,128)(2,1)} %cot_in.1), custom_call_target="tpu_custom_call" | custom-call | tf_op jit(solution)/shard_map/pallas_call | solution.py:255
  2.2 13.8 %all-to-all-start = ((bf16[8,96,128]{2,1,0:T(8,128)(2,1)}), bf16[8,96,128]{2,1,0:T(8,128)(2,1)S(1)}, u32[]{:S(2)}, u32[]{:S(2)}) async-start(bf16[8,96,128]{2,1,0:T(8,128)(2,1)} %shard_map.103), calls=%async_computation | async-start | bytes 393216 | tf_op jit(solution)/shard_map/all_to_all | solution.py:15
  16.1 0.0 copy-start.1
  16.1 0.9 copy-done.1
  17.0 0.0 copy-start.2
  17.0 0.8 copy-done.2
  17.8 0.0 copy-start.4
  17.8 0.7 copy-done.4
  18.4 1.0 shard_map.104
  19.5 0.0 copy-done
  19.5 0.0 copy-start.5
  19.5 0.9 fusion.1.agg
  20.4 1.6 %all-to-all-done.got = bf16[8,96,128]{2,1,0:T(8,128)(2,1)S(1)} async-done(((bf16[8,96,128]{2,1,0:T(8,128)(2,1)}), bf16[8,96,128]{2,1,0:T(8,128)(2,1)S(1)}, u32[]{:S(2)}, u32[]{:S(2)}) %all-to-all-start) | async-done | bytes 196640 | tf_op jit(solution)/shard_map/all_to_all | solution.py:15
  22.0 0.0 copy-done.5
  22.0 1.4 %shard_map.105 = (bf16[12,168,128]{2,1,0:T(8,128)(2,1)S(1)}, bf16[128,384]{1,0:T(8,128)(2,1)S(1)}) custom-call(s32[4,12]{1,0:T(4,128)S(1)} %bitcast.36, bf16[8,96,128]{2,1,0:T(8,128)(2,1)S(1)} %all-to-all-done.got, bf16[12,8,128]{2,1,0:T(8,128)(2,1)S(1)} %fusion.1.agg, bf16[8,1536]{1,0:T(8,128)(2,1)S(1)} %get-tuple-element.16.own, ...), custom_call_target="tpu_custom_call" | custom-call | tf_op jit(solution)/shard_map/pallas_call | solution.py:282
  23.4 28.6 %all_to_all.35 = bf16[12,168,128]{2,1,0:T(8,128)(2,1)S(1)} all-to-all(bf16[12,168,128]{2,1,0:T(8,128)(2,1)S(1)} %get-tuple-element.18), channel_id=1, replica_groups=mesh['x'=4,'z'=12,'c'=2,'node'=8] {'z'}, dimensions={0} | all-to-all | bytes 1032192 | tf_op jit(solution)/shard_map/all_to_all | solution.py:15
  52.1 0.3 fusion
  52.4 0.9 pad_maximum_fusion
  53.3 7.7 %all-to-all-start.2 = ((bf16[8,304,128]{2,1,0:T(8,128)(2,1)}), bf16[8,304,128]{2,1,0:T(8,128)(2,1)}, u32[]{:S(2)}, u32[]{:S(2)}) async-start(bf16[8,304,128]{2,1,0:T(8,128)(2,1)} %pad_maximum_fusion), calls=%async_computation.2 | async-start | bytes 1245184 | tf_op jit(solution)/shard_map/all_to_all | solution.py:15
  61.0 2.1 %copy.27 = bf16[2,1024,153]{1,2,0:T(8,128)(2,1)} copy(bf16[2,1024,153]{1,0,2:T(2,128)(2,1)} %param.14) | data formatting | bytes 1253376 | tf_op args[6]
  63.1 8.6 %all-to-all-done.2.got = bf16[8,304,128]{2,1,0:T(8,128)(2,1)} async-done(((bf16[8,304,128]{2,1,0:T(8,128)(2,1)}), bf16[8,304,128]{2,1,0:T(8,128)(2,1)}, u32[]{:S(2)}, u32[]{:S(2)}) %all-to-all-start.2) | async-done | bytes 622624 | tf_op jit(solution)/shard_map/all_to_all | solution.py:15
  71.7 3.2 %shard_map.106 = (bf16[12,56,128]{2,1,0:T(8,128)(2,1)}, bf16[16,1024]{1,0:T(8,128)(2,1)}, f32[16,153]{1,0:T(8,128)}) custom-call(bf16[8,304,128]{2,1,0:T(8,128)(2,1)} %all-to-all-done.2.got, bf16[2,153,1024]{2,1,0:T(8,128)(2,1)} %bitcast.37), custom_call_target="tpu_custom_call" | custom-call | tf_op jit(solution)/shard_map/pallas_call | solution.py:302
  74.9 15.0 %all_to_all.36.got = bf16[12,56,128]{2,1,0:T(8,128)(2,1)S(1)} all-to-all(bf16[12,56,128]{2,1,0:T(8,128)(2,1)} %get-tuple-element.20), channel_id=1, replica_groups=mesh['x'=4,'z'=12,'c'=2,'node'=8] {'z'}, dimensions={0} | all-to-all | bytes 344064 | tf_op jit(solution)/shard_map/all_to_all | solution.py:15
  89.9 13.8 %all_to_all.37.got = f32[8,16,128]{2,1,0:T(8,128)S(1)} all-to-all(f32[8,16,128]{2,1,0:T(8,128)S(1)} %shard_map.107), channel_id=1, replica_groups=mesh['x'=4,'z'=12,'c'=2,'node'=8] {'node'}, dimensions={0} | all-to-all | bytes 131072 | tf_op jit(solution)/shard_map/all_to_all | solution.py:15
  103.8 0.6 shard_map.108
  104.4 4.1 %all-to-all-start.5 = ((bf16[12,16,128]{2,1,0:T(8,128)(2,1)}), bf16[12,16,128]{2,1,0:T(8,128)(2,1)S(1)}, u32[]{:S(2)}, u32[]{:S(2)}) async-start(bf16[12,16,128]{2,1,0:T(8,128)(2,1)} %shard_map.108), calls=%async_computation.5 | async-start | bytes 98304 | tf_op jit(solution)/shard_map/all_to_all | solution.py:15
  108.5 0.0 copy-start.3
  108.6 0.7 copy-done.3
  109.3 0.3 shard_map.109
  109.5 8.8 %all-to-all-done.5.grad = bf16[12,16,128]{2,1,0:T(8,128)(2,1)S(1)} async-done(((bf16[12,16,128]{2,1,0:T(8,128)(2,1)}), bf16[12,16,128]{2,1,0:T(8,128)(2,1)S(1)}, u32[]{:S(2)}, u32[]{:S(2)}) %all-to-all-start.5) | async-done | bytes 49184 | tf_op jit(solution)/shard_map/all_to_all | solution.py:15
  118.3 14.9 %all_to_all.38.got = bf16[8,192,128]{2,1,0:T(8,128)(2,1)S(1)} all-to-all(bf16[8,192,128]{2,1,0:T(8,128)(2,1)S(1)} %shard_map.110), channel_id=1, replica_groups=mesh['x'=4,'z'=12,'c'=2,'node'=8] {'x','c'}, dimensions={0} | all-to-all | bytes 786432 | tf_op jit(solution)/shard_map/all_to_all | solution.py:15
  133.2 0.9 shard_map.111
  (8 shorter events, 0.2 us)
Async XLA Ops:
  0.6 18.9 %copy-start = (bf16[12,8,128,128]{3,2,1,0:T(8,128)(2,1)S(1)}, bf16[12,8,128,128]{3,2,1,0:T(8,128)(2,1)}, u32[]{:S(2)}) copy-start(bf16[12,8,128,128]{3,2,1,0:T(8,128)(2,1)} %param.10) | copy-start | bytes 9437188
  2.2 19.7 %all-to-all-start = ((bf16[8,96,128]{2,1,0:T(8,128)(2,1)}), bf16[8,96,128]{2,1,0:T(8,128)(2,1)S(1)}, u32[]{:S(2)}, u32[]{:S(2)}) async-start(bf16[8,96,128]{2,1,0:T(8,128)(2,1)} %shard_map.103), calls=%async_computation | async-start | bytes 393216 | tf_op jit(solution)/shard_map/all_to_all | solution.py:15
  16.1 0.9 copy-start.1
  17.0 0.8 copy-start.2
  17.8 0.7 copy-start.4
  19.5 2.5 %copy-start.5 = (s32[12,4]{0,1:T(4,128)S(1)}, s32[12,4]{0,1:T(4,128)}, u32[]{:S(2)}) copy-start(s32[12,4]{0,1:T(4,128)} %param.13) | copy-start | bytes 580
  53.3 18.4 %all-to-all-start.2 = ((bf16[8,304,128]{2,1,0:T(8,128)(2,1)}), bf16[8,304,128]{2,1,0:T(8,128)(2,1)}, u32[]{:S(2)}, u32[]{:S(2)}) async-start(bf16[8,304,128]{2,1,0:T(8,128)(2,1)} %pad_maximum_fusion), calls=%async_computation.2 | async-start | bytes 1245184 | tf_op jit(solution)/shard_map/all_to_all | solution.py:15
  104.4 13.9 %all-to-all-start.5 = ((bf16[12,16,128]{2,1,0:T(8,128)(2,1)}), bf16[12,16,128]{2,1,0:T(8,128)(2,1)S(1)}, u32[]{:S(2)}, u32[]{:S(2)}) async-start(bf16[12,16,128]{2,1,0:T(8,128)(2,1)} %shard_map.108), calls=%async_computation.5 | async-start | bytes 98304 | tf_op jit(solution)/shard_map/all_to_all | solution.py:15
  108.5 0.7 copy-start.3

commit v13 on v12

--- a/solution.py
+++ b/solution.py
@@ -248,6 +248,7 @@
     strips = block // strip
     mids = blocks // xs
     limit = pltpu.CompilerParams(vmem_limit_bytes=16 * 2**20)
+    pick_limit = pltpu.CompilerParams(vmem_limit_bytes=64 * 2**20 - 3650 * 2**10)
     wide_limit = pltpu.CompilerParams(vmem_limit_bytes=60 * 2**20)
     away = pl.BlockSpec(memory_space=pltpu.HBM)
     whole = pl.BlockSpec(memory_space=pltpu.VMEM)
@@ -274,7 +275,7 @@
             jax.ShapeDtypeStruct(w_one.shape, BF16),
         ),
         scratch_shapes=[pltpu.VMEM((cols, sources), BF16), pltpu.SemaphoreType.DMA((2,))],
-        compiler_params=limit,
+        compiler_params=pick_limit,
     )(list_one.T, features, w_one)
     chosen = chosen.reshape(blocks, fanout, cols, block)
     agg = dot("hkfs,hkts->hft", chosen, adj_one).astype(BF16)

time: 135 us -> 135 us (level)
  local copies, waits for them, and re-layouts: 5.23 us -> 2.87 us
  Pallas kernels: 9.13 us -> 10.6 us
    unnamed x13 -> x11, local copies, waits for them, and re-layouts: 5.17 us -> 2.81 us
    pallas_call x1, Pallas kernels: 1.04 us -> 2.48 us  [per_device(): pl.pallas_call(pick_blocks, in_specs=[scalars, away, away], out_shape=(ja...]
  transfers between devices with their start and end apart: 3 -> 3, of which waited for: 3 -> 3; matrix products, arithmetic and copies ran while one was open for 2% -> 3% of each run, Pallas kernels for 1% -> 2%
where the time goes in v13:
time: 135 us; the launch traced here: 134 us
  blocking collectives  72.3 us (54%)
  starting transfers between devices  25.7 us (19%)
  waiting for transfers between devices  18.9 us (14%)
  Pallas kernels  10.6 us (8%)
  local copies, waits for them, and re-layouts  2.87 us (2%)
  matrix products  2.12 us (2%)
    all_to_all x4, blocking collectives, exchange(): return lax.all_to_all(parts, axis, 0, 0, tiled=True)  72.3 us
    all_to_all x3, starting transfers between devices, exchange(): return lax.all_to_all(parts, axis, 0, 0, tiled=True)  25.7 us
    all_to_all x3, waiting for transfers between devices, exchange(): return lax.all_to_all(parts, axis, 0, 0, tiled=True)  18.9 us
    pallas_call x1, Pallas kernels, per_device(): pl.pallas_call(middle, in_specs=[whole, away], scratch_shapes=[pltpu.VMEM...  3.21 us
    unnamed x11, local copies, waits for them, and re-layouts  2.81 us
  transfers between devices with their start and end apart: 3, of which 3 were waited for; matrix products, arithmetic and copies ran while one was open for 3% of the time, Pallas kernels for 2%

profile of v13, /device:TPU:1, one launch (start us, length us, event | category | flops | bytes accessed | tf_op | source)
XLA Modules:
  0.0 134.2 jit_solution(1513894257828936145)
XLA Ops:
  0.6 0.0 copy-start
  0.6 1.6 %shard_map.103 = bf16[8,96,128]{2,1,0:T(8,128)(2,1)} custom-call(bf16[64,128]{1,0:T(8,128)(2,1)} %bitcast.41, bf16[16,153]{1,0:T(8,128)(2,1)} %cot_in.1), custom_call_target="tpu_custom_call" | custom-call | tf_op jit(solution)/shard_map/pallas_call | solution.py:256
  2.2 13.8 %all-to-all-start = ((bf16[8,96,128]{2,1,0:T(8,128)(2,1)}), bf16[8,96,128]{2,1,0:T(8,128)(2,1)S(1)}, u32[]{:S(2)}, u32[]{:S(2)}) async-start(bf16[8,96,128]{2,1,0:T(8,128)(2,1)} %shard_map.103), calls=%async_computation | async-start | bytes 393216 | tf_op jit(solution)/shard_map/all_to_all | solution.py:15
  16.1 2.5 %shard_map.104 = (bf16[96,8,128]{2,1,0:T(8,128)(2,1)}, bf16[8,1536]{1,0:T(8,128)(2,1)}, bf16[2,8,1024]{2,1,0:T(8,128)(2,1)}) custom-call(s32[8,12]{1,0:T(8,128)} %bitcast.42, bf16[8,12288]{1,0:T(8,128)(2,1)} %tiles_in.1, bf16[2,8,1024]{2,1,0:T(8,128)(2,1)} %w_in.1), custom_call_target="tpu_custom_call" | custom-call | tf_op jit(solution)/shard_map/pallas_call | solution.py:269
  18.6 0.0 copy-done
  18.6 0.0 copy-start.1
  18.6 0.0 copy-start.2
  18.6 0.0 copy-start.4
  18.6 1.8 %fusion.1.agg = bf16[12,8,128]{2,1,0:T(8,128)(2,1)S(1)} fusion(bf16[12,8,8,128]{3,2,1,0:T(8,128)(2,1)} %bitcast.40, bf16[12,8,128,128]{3,2,1,0:T(8,128)(2,1)S(1)} %copy-done), kind=kOutput, calls=%fused_computation.3 | convolution fusion | flops 25178112 | bytes 3366912 | tf_op jit(solution)/shard_map/hkfs,hkts->hft/dot_general | solution.py:23
  20.4 1.5 %all-to-all-done.got = bf16[8,96,128]{2,1,0:T(8,128)(2,1)S(1)} async-done(((bf16[8,96,128]{2,1,0:T(8,128)(2,1)}), bf16[8,96,128]{2,1,0:T(8,128)(2,1)S(1)}, u32[]{:S(2)}, u32[]{:S(2)}) %all-to-all-start) | async-done | bytes 196640 | tf_op jit(solution)/shard_map/all_to_all | solution.py:15
  22.0 0.0 copy-done.1
  22.0 0.0 copy-done.2
  22.0 0.0 copy-done.4
  22.0 1.4 %shard_map.105 = (bf16[12,168,128]{2,1,0:T(8,128)(2,1)S(1)}, bf16[128,384]{1,0:T(8,128)(2,1)S(1)}) custom-call(s32[4,12]{1,0:T(4,128)S(1)} %bitcast.34, bf16[8,96,128]{2,1,0:T(8,128)(2,1)S(1)} %all-to-all-done.got, bf16[12,8,128]{2,1,0:T(8,128)(2,1)S(1)} %fusion.1.agg, bf16[8,1536]{1,0:T(8,128)(2,1)S(1)} %copy-done.2, bf16[2,8,1024]{2,1,0:T(8,128)(2,1)S(1)} %copy-done.1), custom_call_target="tpu_custom_call" | custom-call | tf_op jit(solution)/shard_map/pallas_call | solution.py:283
  23.4 28.6 %all_to_all.35 = bf16[12,168,128]{2,1,0:T(8,128)(2,1)S(1)} all-to-all(bf16[12,168,128]{2,1,0:T(8,128)(2,1)S(1)} %get-tuple-element.18), channel_id=1, replica_groups=mesh['x'=4,'z'=12,'c'=2,'node'=8] {'z'}, dimensions={0} | all-to-all | bytes 1032192 | tf_op jit(solution)/shard_map/all_to_all | solution.py:15
  52.1 0.3 fusion
  52.4 0.9 pad_maximum_fusion
  53.3 7.7 %all-to-all-start.2 = ((bf16[8,304,128]{2,1,0:T(8,128)(2,1)}), bf16[8,304,128]{2,1,0:T(8,128)(2,1)}, u32[]{:S(2)}, u32[]{:S(2)}) async-start(bf16[8,304,128]{2,1,0:T(8,128)(2,1)} %pad_maximum_fusion), calls=%async_computation.2 | async-start | bytes 1245184 | tf_op jit(solution)/shard_map/all_to_all | solution.py:15
  61.0 2.1 %copy.27 = bf16[2,1024,153]{1,2,0:T(8,128)(2,1)} copy(bf16[2,1024,153]{1,0,2:T(2,128)(2,1)} %param.14) | data formatting | bytes 1253376 | tf_op args[6]
  63.1 8.6 %all-to-all-done.2.got = bf16[8,304,128]{2,1,0:T(8,128)(2,1)} async-done(((bf16[8,304,128]{2,1,0:T(8,128)(2,1)}), bf16[8,304,128]{2,1,0:T(8,128)(2,1)}, u32[]{:S(2)}, u32[]{:S(2)}) %all-to-all-start.2) | async-done | bytes 622624 | tf_op jit(solution)/shard_map/all_to_all | solution.py:15
  71.7 3.2 %shard_map.106 = (bf16[12,56,128]{2,1,0:T(8,128)(2,1)}, bf16[16,1024]{1,0:T(8,128)(2,1)}, f32[16,153]{1,0:T(8,128)}) custom-call(bf16[8,304,128]{2,1,0:T(8,128)(2,1)} %all-to-all-done.2.got, bf16[2,153,1024]{2,1,0:T(8,128)(2,1)} %bitcast.35), custom_call_target="tpu_custom_call" | custom-call | tf_op jit(solution)/shard_map/pallas_call | solution.py:303
  74.9 15.0 %all_to_all.36.got = bf16[12,56,128]{2,1,0:T(8,128)(2,1)S(1)} all-to-all(bf16[12,56,128]{2,1,0:T(8,128)(2,1)} %get-tuple-element.20), channel_id=1, replica_groups=mesh['x'=4,'z'=12,'c'=2,'node'=8] {'z'}, dimensions={0} | all-to-all | bytes 344064 | tf_op jit(solution)/shard_map/all_to_all | solution.py:15
  89.9 13.8 %all_to_all.37.got = f32[8,16,128]{2,1,0:T(8,128)S(1)} all-to-all(f32[8,16,128]{2,1,0:T(8,128)S(1)} %shard_map.107), channel_id=1, replica_groups=mesh['x'=4,'z'=12,'c'=2,'node'=8] {'node'}, dimensions={0} | all-to-all | bytes 131072 | tf_op jit(solution)/shard_map/all_to_all | solution.py:15
  103.8 0.6 shard_map.108
  104.4 4.1 %all-to-all-start.5 = ((bf16[12,16,128]{2,1,0:T(8,128)(2,1)}), bf16[12,16,128]{2,1,0:T(8,128)(2,1)S(1)}, u32[]{:S(2)}, u32[]{:S(2)}) async-start(bf16[12,16,128]{2,1,0:T(8,128)(2,1)} %shard_map.108), calls=%async_computation.5 | async-start | bytes 98304 | tf_op jit(solution)/shard_map/all_to_all | solution.py:15
  108.5 0.0 copy-start.3
  108.6 0.7 copy-done.3
  109.3 0.3 shard_map.109
  109.5 8.8 %all-to-all-done.5.grad = bf16[12,16,128]{2,1,0:T(8,128)(2,1)S(1)} async-done(((bf16[12,16,128]{2,1,0:T(8,128)(2,1)}), bf16[12,16,128]{2,1,0:T(8,128)(2,1)S(1)}, u32[]{:S(2)}, u32[]{:S(2)}) %all-to-all-start.5) | async-done | bytes 49184 | tf_op jit(solution)/shard_map/all_to_all | solution.py:15
  118.3 14.9 %all_to_all.38.got = bf16[8,192,128]{2,1,0:T(8,128)(2,1)S(1)} all-to-all(bf16[8,192,128]{2,1,0:T(8,128)(2,1)S(1)} %shard_map.110), channel_id=1, replica_groups=mesh['x'=4,'z'=12,'c'=2,'node'=8] {'x','c'}, dimensions={0} | all-to-all | bytes 786432 | tf_op jit(solution)/shard_map/all_to_all | solution.py:15
  133.2 0.9 shard_map.111
  (8 shorter events, 0.2 us)
Async XLA Ops:
  0.6 17.9 %copy-start = (bf16[12,8,128,128]{3,2,1,0:T(8,128)(2,1)S(1)}, bf16[12,8,128,128]{3,2,1,0:T(8,128)(2,1)}, u32[]{:S(2)}) copy-start(bf16[12,8,128,128]{3,2,1,0:T(8,128)(2,1)} %param.10) | copy-start | bytes 9437188
  2.2 19.7 %all-to-all-start = ((bf16[8,96,128]{2,1,0:T(8,128)(2,1)}), bf16[8,96,128]{2,1,0:T(8,128)(2,1)S(1)}, u32[]{:S(2)}, u32[]{:S(2)}) async-start(bf16[8,96,128]{2,1,0:T(8,128)(2,1)} %shard_map.103), calls=%async_computation | async-start | bytes 393216 | tf_op jit(solution)/shard_map/all_to_all | solution.py:15
  18.6 3.4 %copy-start.1 = (bf16[2,8,1024]{2,1,0:T(8,128)(2,1)S(1)}, bf16[2,8,1024]{2,1,0:T(8,128)(2,1)}, u32[]{:S(2)}) copy-start(bf16[2,8,1024]{2,1,0:T(8,128)(2,1)} %get-tuple-element.17.w) | copy-start | bytes 98308
  18.6 3.4 %copy-start.2 = (bf16[8,1536]{1,0:T(8,128)(2,1)S(1)}, bf16[8,1536]{1,0:T(8,128)(2,1)}, u32[]{:S(2)}) copy-start(bf16[8,1536]{1,0:T(8,128)(2,1)} %get-tuple-element.16.own) | copy-start | bytes 73732
  18.6 3.4 %copy-start.4 = (s32[12,4]{0,1:T(4,128)S(1)}, s32[12,4]{0,1:T(4,128)}, u32[]{:S(2)}) copy-start(s32[12,4]{0,1:T(4,128)} %param.13) | copy-start | bytes 580
  53.3 18.4 %all-to-all-start.2 = ((bf16[8,304,128]{2,1,0:T(8,128)(2,1)}), bf16[8,304,128]{2,1,0:T(8,128)(2,1)}, u32[]{:S(2)}, u32[]{:S(2)}) async-start(bf16[8,304,128]{2,1,0:T(8,128)(2,1)} %pad_maximum_fusion), calls=%async_computation.2 | async-start | bytes 1245184 | tf_op jit(solution)/shard_map/all_to_all | solution.py:15
  104.4 13.9 %all-to-all-start.5 = ((bf16[12,16,128]{2,1,0:T(8,128)(2,1)}), bf16[12,16,128]{2,1,0:T(8,128)(2,1)S(1)}, u32[]{:S(2)}, u32[]{:S(2)}) async-start(bf16[12,16,128]{2,1,0:T(8,128)(2,1)} %shard_map.108), calls=%async_computation.5 | async-start | bytes 98304 | tf_op jit(solution)/shard_map/all_to_all | solution.py:15
  108.5 0.7 copy-start.3

commit v14 on v13

--- a/solution.py
+++ b/solution.py
@@ -46,15 +46,10 @@
         sends[j, rows + mine :] = rest
 
 
-def pick_blocks(lists, tiles_in, w_in, chosen, own, w, tiles, sems):
-    copies = [
-        pltpu.make_async_copy(tiles_in, tiles, sems.at[0]),
-        pltpu.make_async_copy(w_in, w, sems.at[1]),
-    ]
-    for copy in copies:
-        copy.start()
-    for copy in copies:
-        copy.wait()
+def pick_blocks(lists, tiles_in, chosen, own, tiles, sem):
+    copy = pltpu.make_async_copy(tiles_in, tiles, sem)
+    copy.start()
+    copy.wait()
     fanout, blocks = lists.shape
     block = chosen.shape[2]
     own[...] = tiles[:, : blocks * block]
@@ -266,17 +261,16 @@
     )(adj_two.reshape(mine * listed, block), cotangent)
     near = exchange(got, LANE)
 
-    chosen, own, w = pl.pallas_call(
+    chosen, own = pl.pallas_call(
         pick_blocks,
-        in_specs=[scalars, away, away],
+        in_specs=[scalars, away],
         out_shape=(
             jax.ShapeDtypeStruct((blocks * fanout, cols, block), BF16),
             jax.ShapeDtypeStruct((cols, blocks * block), BF16),
-            jax.ShapeDtypeStruct(w_one.shape, BF16),
-        ),
-        scratch_shapes=[pltpu.VMEM((cols, sources), BF16), pltpu.SemaphoreType.DMA((2,))],
+        ),
+        scratch_shapes=[pltpu.VMEM((cols, sources), BF16), pltpu.SemaphoreType.DMA],
         compiler_params=pick_limit,
-    )(list_one.T, features, w_one)
+    )(list_one.T, features)
     chosen = chosen.reshape(blocks, fanout, cols, block)
     agg = dot("hkfs,hkts->hft", chosen, adj_one).astype(BF16)
     above = 2 * cols + 2 * cols * lanes
@@ -289,7 +283,7 @@
             jax.ShapeDtypeStruct((block, mids * block), BF16),
         ),
         compiler_params=limit,
-    )(list_two.T, near, agg, own, w)
+    )(list_two.T, near, agg, own, w_one)
     got = exchange(got, "z")
     inputs, weights, back = jnp.split(got, (2 * cols, above), axis=1)
     inputs = inputs.reshape(blocks, 2, cols, block)

time: 135 us -> 135 us (level)
  no operation moved by 1% of the time
where the time goes in v14:
time: 135 us; the launch traced here: 134 us
  blocking collectives  72.3 us (54%)
  starting transfers between devices  25.7 us (19%)
  waiting for transfers between devices  18.9 us (14%)
  Pallas kernels  10.6 us (8%)
  local copies, waits for them, and re-layouts  2.87 us (2%)
  matrix products  2.11 us (2%)
    all_to_all x4, blocking collectives, exchange(): return lax.all_to_all(parts, axis, 0, 0, tiled=True)  72.3 us
    all_to_all x3, starting transfers between devices, exchange(): return lax.all_to_all(parts, axis, 0, 0, tiled=True)  25.7 us
    all_to_all x3, waiting for transfers between devices, exchange(): return lax.all_to_all(parts, axis, 0, 0, tiled=True)  18.9 us
    pallas_call x1, Pallas kernels, per_device(): pl.pallas_call(middle, in_specs=[whole, away], scratch_shapes=[pltpu.VMEM...  3.21 us
    unnamed x11, local copies, waits for them, and re-layouts  2.81 us
  transfers between devices with their start and end apart: 3, of which 3 were waited for; matrix products, arithmetic and copies ran while one was open for 3% of the time, Pallas kernels for 2%

profile of v14, /device:TPU:1, one launch (start us, length us, event | category | flops | bytes accessed | tf_op | source)
XLA Modules:
  0.0 134.2 jit_solution(3681043061347491978)
XLA Ops:
  0.6 0.0 copy-start
  0.6 1.6 %shard_map.103 = bf16[8,96,128]{2,1,0:T(8,128)(2,1)} custom-call(bf16[64,128]{1,0:T(8,128)(2,1)} %bitcast.41, bf16[16,153]{1,0:T(8,128)(2,1)} %cot_in.1), custom_call_target="tpu_custom_call" | custom-call | tf_op jit(solution)/shard_map/pallas_call | solution.py:251
  2.2 13.8 %all-to-all-start = ((bf16[8,96,128]{2,1,0:T(8,128)(2,1)}), bf16[8,96,128]{2,1,0:T(8,128)(2,1)S(1)}, u32[]{:S(2)}, u32[]{:S(2)}) async-start(bf16[8,96,128]{2,1,0:T(8,128)(2,1)} %shard_map.103), calls=%async_computation | async-start | bytes 393216 | tf_op jit(solution)/shard_map/all_to_all | solution.py:15
  16.1 2.5 %shard_map.104 = (bf16[96,8,128]{2,1,0:T(8,128)(2,1)}, bf16[8,1536]{1,0:T(8,128)(2,1)}) custom-call(s32[8,12]{1,0:T(8,128)} %bitcast.42, bf16[8,12288]{1,0:T(8,128)(2,1)} %tiles_in.1), custom_call_target="tpu_custom_call" | custom-call | tf_op jit(solution)/shard_map/pallas_call | solution.py:264
  18.5 0.0 copy-done
  18.5 0.0 copy-start.1
  18.6 0.0 copy-start.2
  18.6 0.0 copy-start.4
  18.6 1.8 %fusion.1.agg = bf16[12,8,128]{2,1,0:T(8,128)(2,1)S(1)} fusion(bf16[12,8,8,128]{3,2,1,0:T(8,128)(2,1)} %bitcast.40, bf16[12,8,128,128]{3,2,1,0:T(8,128)(2,1)S(1)} %copy-done), kind=kOutput, calls=%fused_computation.3 | convolution fusion | flops 25178112 | bytes 3366912 | tf_op jit(solution)/shard_map/hkfs,hkts->hft/dot_general | solution.py:23
  20.4 1.5 %all-to-all-done.got = bf16[8,96,128]{2,1,0:T(8,128)(2,1)S(1)} async-done(((bf16[8,96,128]{2,1,0:T(8,128)(2,1)}), bf16[8,96,128]{2,1,0:T(8,128)(2,1)S(1)}, u32[]{:S(2)}, u32[]{:S(2)}) %all-to-all-start) | async-done | bytes 196640 | tf_op jit(solution)/shard_map/all_to_all | solution.py:15
  22.0 0.0 copy-done.1
  22.0 0.0 copy-done.2
  22.0 0.0 copy-done.4
  22.0 1.4 %shard_map.105 = (bf16[12,168,128]{2,1,0:T(8,128)(2,1)S(1)}, bf16[128,384]{1,0:T(8,128)(2,1)S(1)}) custom-call(s32[4,12]{1,0:T(4,128)S(1)} %bitcast.34, bf16[8,96,128]{2,1,0:T(8,128)(2,1)S(1)} %all-to-all-done.got, bf16[12,8,128]{2,1,0:T(8,128)(2,1)S(1)} %fusion.1.agg, bf16[8,1536]{1,0:T(8,128)(2,1)S(1)} %copy-done.2, bf16[2,8,1024]{2,1,0:T(8,128)(2,1)S(1)} %copy-done.1), custom_call_target="tpu_custom_call" | custom-call | tf_op jit(solution)/shard_map/pallas_call | solution.py:277
  23.4 28.6 %all_to_all.35 = bf16[12,168,128]{2,1,0:T(8,128)(2,1)S(1)} all-to-all(bf16[12,168,128]{2,1,0:T(8,128)(2,1)S(1)} %get-tuple-element.16), channel_id=1, replica_groups=mesh['x'=4,'z'=12,'c'=2,'node'=8] {'z'}, dimensions={0} | all-to-all | bytes 1032192 | tf_op jit(solution)/shard_map/all_to_all | solution.py:15
  52.1 0.3 fusion
  52.4 0.9 pad_maximum_fusion
  53.3 7.7 %all-to-all-start.2 = ((bf16[8,304,128]{2,1,0:T(8,128)(2,1)}), bf16[8,304,128]{2,1,0:T(8,128)(2,1)}, u32[]{:S(2)}, u32[]{:S(2)}) async-start(bf16[8,304,128]{2,1,0:T(8,128)(2,1)} %pad_maximum_fusion), calls=%async_computation.2 | async-start | bytes 1245184 | tf_op jit(solution)/shard_map/all_to_all | solution.py:15
  61.0 2.1 %copy.27 = bf16[2,1024,153]{1,2,0:T(8,128)(2,1)} copy(bf16[2,1024,153]{1,0,2:T(2,128)(2,1)} %param.14) | data formatting | bytes 1253376 | tf_op args[6]
  63.1 8.6 %all-to-all-done.2.got = bf16[8,304,128]{2,1,0:T(8,128)(2,1)} async-done(((bf16[8,304,128]{2,1,0:T(8,128)(2,1)}), bf16[8,304,128]{2,1,0:T(8,128)(2,1)}, u32[]{:S(2)}, u32[]{:S(2)}) %all-to-all-start.2) | async-done | bytes 622624 | tf_op jit(solution)/shard_map/all_to_all | solution.py:15
  71.7 3.2 %shard_map.106 = (bf16[12,56,128]{2,1,0:T(8,128)(2,1)}, bf16[16,1024]{1,0:T(8,128)(2,1)}, f32[16,153]{1,0:T(8,128)}) custom-call(bf16[8,304,128]{2,1,0:T(8,128)(2,1)} %all-to-all-done.2.got, bf16[2,153,1024]{2,1,0:T(8,128)(2,1)} %bitcast.35), custom_call_target="tpu_custom_call" | custom-call | tf_op jit(solution)/shard_map/pallas_call | solution.py:297
  74.9 15.0 %all_to_all.36.got = bf16[12,56,128]{2,1,0:T(8,128)(2,1)S(1)} all-to-all(bf16[12,56,128]{2,1,0:T(8,128)(2,1)} %get-tuple-element.18), channel_id=1, replica_groups=mesh['x'=4,'z'=12,'c'=2,'node'=8] {'z'}, dimensions={0} | all-to-all | bytes 344064 | tf_op jit(solution)/shard_map/all_to_all | solution.py:15
  89.9 13.8 %all_to_all.37.got = f32[8,16,128]{2,1,0:T(8,128)S(1)} all-to-all(f32[8,16,128]{2,1,0:T(8,128)S(1)} %shard_map.107), channel_id=1, replica_groups=mesh['x'=4,'z'=12,'c'=2,'node'=8] {'node'}, dimensions={0} | all-to-all | bytes 131072 | tf_op jit(solution)/shard_map/all_to_all | solution.py:15
  103.8 0.6 shard_map.108
  104.4 4.1 %all-to-all-start.5 = ((bf16[12,16,128]{2,1,0:T(8,128)(2,1)}), bf16[12,16,128]{2,1,0:T(8,128)(2,1)S(1)}, u32[]{:S(2)}, u32[]{:S(2)}) async-start(bf16[12,16,128]{2,1,0:T(8,128)(2,1)} %shard_map.108), calls=%async_computation.5 | async-start | bytes 98304 | tf_op jit(solution)/shard_map/all_to_all | solution.py:15
  108.5 0.0 copy-start.3
  108.6 0.7 copy-done.3
  109.3 0.3 shard_map.109
  109.5 8.8 %all-to-all-done.5.grad = bf16[12,16,128]{2,1,0:T(8,128)(2,1)S(1)} async-done(((bf16[12,16,128]{2,1,0:T(8,128)(2,1)}), bf16[12,16,128]{2,1,0:T(8,128)(2,1)S(1)}, u32[]{:S(2)}, u32[]{:S(2)}) %all-to-all-start.5) | async-done | bytes 49184 | tf_op jit(solution)/shard_map/all_to_all | solution.py:15
  118.3 14.9 %all_to_all.38.got = bf16[8,192,128]{2,1,0:T(8,128)(2,1)S(1)} all-to-all(bf16[8,192,128]{2,1,0:T(8,128)(2,1)S(1)} %shard_map.110), channel_id=1, replica_groups=mesh['x'=4,'z'=12,'c'=2,'node'=8] {'x','c'}, dimensions={0} | all-to-all | bytes 786432 | tf_op jit(solution)/shard_map/all_to_all | solution.py:15
  133.2 0.9 shard_map.111
  (8 shorter events, 0.2 us)
Async XLA Ops:
  0.6 17.9 %copy-start = (bf16[12,8,128,128]{3,2,1,0:T(8,128)(2,1)S(1)}, bf16[12,8,128,128]{3,2,1,0:T(8,128)(2,1)}, u32[]{:S(2)}) copy-start(bf16[12,8,128,128]{3,2,1,0:T(8,128)(2,1)} %param.10) | copy-start | bytes 9437188
  2.2 19.7 %all-to-all-start = ((bf16[8,96,128]{2,1,0:T(8,128)(2,1)}), bf16[8,96,128]{2,1,0:T(8,128)(2,1)S(1)}, u32[]{:S(2)}, u32[]{:S(2)}) async-start(bf16[8,96,128]{2,1,0:T(8,128)(2,1)} %shard_map.103), calls=%async_computation | async-start | bytes 393216 | tf_op jit(solution)/shard_map/all_to_all | solution.py:15
  18.5 3.4 %copy-start.1 = (bf16[2,8,1024]{2,1,0:T(8,128)(2,1)S(1)}, bf16[2,8,1024]{2,1,0:T(8,128)(2,1)}, u32[]{:S(2)}) copy-start(bf16[2,8,1024]{2,1,0:T(8,128)(2,1)} %w.1) | copy-start | bytes 98308
  18.6 3.4 %copy-start.2 = (bf16[8,1536]{1,0:T(8,128)(2,1)S(1)}, bf16[8,1536]{1,0:T(8,128)(2,1)}, u32[]{:S(2)}) copy-start(bf16[8,1536]{1,0:T(8,128)(2,1)} %get-tuple-element.15.own) | copy-start | bytes 73732
  18.6 3.4 %copy-start.4 = (s32[12,4]{0,1:T(4,128)S(1)}, s32[12,4]{0,1:T(4,128)}, u32[]{:S(2)}) copy-start(s32[12,4]{0,1:T(4,128)} %param.13) | copy-start | bytes 580
  53.3 18.4 %all-to-all-start.2 = ((bf16[8,304,128]{2,1,0:T(8,128)(2,1)}), bf16[8,304,128]{2,1,0:T(8,128)(2,1)}, u32[]{:S(2)}, u32[]{:S(2)}) async-start(bf16[8,304,128]{2,1,0:T(8,128)(2,1)} %pad_maximum_fusion), calls=%async_computation.2 | async-start | bytes 1245184 | tf_op jit(solution)/shard_map/all_to_all | solution.py:15
  104.4 13.9 %all-to-all-start.5 = ((bf16[12,16,128]{2,1,0:T(8,128)(2,1)}), bf16[12,16,128]{2,1,0:T(8,128)(2,1)S(1)}, u32[]{:S(2)}, u32[]{:S(2)}) async-start(bf16[12,16,128]{2,1,0:T(8,128)(2,1)} %shard_map.108), calls=%async_computation.5 | async-start | bytes 98304 | tf_op jit(solution)/shard_map/all_to_all | solution.py:15
  108.5 0.7 copy-start.3

commit v15 on v14

--- a/solution.py
+++ b/solution.py
@@ -243,7 +243,6 @@
     strips = block // strip
     mids = blocks // xs
     limit = pltpu.CompilerParams(vmem_limit_bytes=16 * 2**20)
-    pick_limit = pltpu.CompilerParams(vmem_limit_bytes=64 * 2**20 - 3650 * 2**10)
     wide_limit = pltpu.CompilerParams(vmem_limit_bytes=60 * 2**20)
     away = pl.BlockSpec(memory_space=pltpu.HBM)
     whole = pl.BlockSpec(memory_space=pltpu.VMEM)
@@ -269,7 +268,7 @@
             jax.ShapeDtypeStruct((cols, blocks * block), BF16),
         ),
         scratch_shapes=[pltpu.VMEM((cols, sources), BF16), pltpu.SemaphoreType.DMA],
-        compiler_params=pick_limit,
+        compiler_params=limit,
     )(list_one.T, features)
     chosen = chosen.reshape(blocks, fanout, cols, block)
     agg = dot("hkfs,hkts->hft", chosen, adj_one).astype(BF16)

time: 135 us -> 135 us (level)
  local copies, waits for them, and re-layouts: 2.87 us -> 4.48 us
  Pallas kernels: 10.6 us -> 9.08 us
    unnamed x11 -> x13, local copies, waits for them, and re-layouts: 2.81 us -> 4.42 us
    pallas_call x1, Pallas kernels: 2.46 us -> 0.99 us  [per_device(): pl.pallas_call(pick_blocks, in_specs=[scalars, away], out_shape=(jax.Shap...]
  transfers between devices with their start and end apart: 3 -> 3, of which waited for: 3 -> 3; matrix products, arithmetic and copies ran while one was open for 3% -> 2% of each run, Pallas kernels for 2% -> 1%
where the time goes in v15:
time: 135 us; the launch traced here: 134 us
  blocking collectives  72.3 us (54%)
  starting transfers between devices  25.7 us (19%)
  waiting for transfers between devices  19.7 us (15%)
  Pallas kernels  9.08 us (7%)
  local copies, waits for them, and re-layouts  4.48 us (3%)
    all_to_all x4, blocking collectives, exchange(): return lax.all_to_all(parts, axis, 0, 0, tiled=True)  72.3 us
    all_to_all x3, starting transfers between devices, exchange(): return lax.all_to_all(parts, axis, 0, 0, tiled=True)  25.7 us
    all_to_all x3, waiting for transfers between devices, exchange(): return lax.all_to_all(parts, axis, 0, 0, tiled=True)  19.7 us
    unnamed x13, local copies, waits for them, and re-layouts  4.42 us
    pallas_call x1, Pallas kernels, per_device(): pl.pallas_call(middle, in_specs=[whole, away], scratch_shapes=[pltpu.VMEM...  3.2 us
  transfers between devices with their start and end apart: 3, of which 3 were waited for; matrix products, arithmetic and copies ran while one was open for 2% of the time, Pallas kernels for 1%

profile of v15, /device:TPU:1, one launch (start us, length us, event | category | flops | bytes accessed | tf_op | source)
XLA Modules:
  0.0 134.2 jit_solution(4325274658611175187)
XLA Ops:
  0.6 0.0 copy-start
  0.6 1.6 %shard_map.103 = bf16[8,96,128]{2,1,0:T(8,128)(2,1)} custom-call(bf16[64,128]{1,0:T(8,128)(2,1)} %bitcast.42, bf16[16,153]{1,0:T(8,128)(2,1)} %cot_in.1), custom_call_target="tpu_custom_call" | custom-call | tf_op jit(solution)/shard_map/pallas_call | solution.py:250
  2.2 13.8 %all-to-all-start = ((bf16[8,96,128]{2,1,0:T(8,128)(2,1)}), bf16[8,96,128]{2,1,0:T(8,128)(2,1)S(1)}, u32[]{:S(2)}, u32[]{:S(2)}) async-start(bf16[8,96,128]{2,1,0:T(8,128)(2,1)} %shard_map.103), calls=%async_computation | async-start | bytes 393216 | tf_op jit(solution)/shard_map/all_to_all | solution.py:15
  16.1 0.0 copy-start.1
  16.1 0.9 copy-done.1
  17.0 0.0 copy-start.4
  17.0 0.7 copy-done.4
  17.7 1.0 shard_map.104
  18.7 0.0 copy-done
  18.7 0.0 copy-start.2
  18.7 0.0 copy-start.5
  18.7 0.9 fusion.1.agg
  19.6 2.4 %all-to-all-done.got = bf16[8,96,128]{2,1,0:T(8,128)(2,1)S(1)} async-done(((bf16[8,96,128]{2,1,0:T(8,128)(2,1)}), bf16[8,96,128]{2,1,0:T(8,128)(2,1)S(1)}, u32[]{:S(2)}, u32[]{:S(2)}) %all-to-all-start) | async-done | bytes 196640 | tf_op jit(solution)/shard_map/all_to_all | solution.py:15
  22.0 0.0 copy-done.2
  22.0 0.0 copy-done.5
  22.0 1.4 %shard_map.105 = (bf16[12,168,128]{2,1,0:T(8,128)(2,1)S(1)}, bf16[128,384]{1,0:T(8,128)(2,1)S(1)}) custom-call(s32[4,12]{1,0:T(4,128)S(1)} %bitcast.36, bf16[8,96,128]{2,1,0:T(8,128)(2,1)S(1)} %all-to-all-done.got, bf16[12,8,128]{2,1,0:T(8,128)(2,1)S(1)} %fusion.1.agg, bf16[8,1536]{1,0:T(8,128)(2,1)S(1)} %get-tuple-element.15.own, ...), custom_call_target="tpu_custom_call" | custom-call | tf_op jit(solution)/shard_map/pallas_call | solution.py:276
  23.4 28.6 %all_to_all.35 = bf16[12,168,128]{2,1,0:T(8,128)(2,1)S(1)} all-to-all(bf16[12,168,128]{2,1,0:T(8,128)(2,1)S(1)} %get-tuple-element.16), channel_id=1, replica_groups=mesh['x'=4,'z'=12,'c'=2,'node'=8] {'z'}, dimensions={0} | all-to-all | bytes 1032192 | tf_op jit(solution)/shard_map/all_to_all | solution.py:15
  52.1 0.3 fusion
  52.4 0.9 pad_maximum_fusion
  53.3 7.7 %all-to-all-start.2 = ((bf16[8,304,128]{2,1,0:T(8,128)(2,1)}), bf16[8,304,128]{2,1,0:T(8,128)(2,1)}, u32[]{:S(2)}, u32[]{:S(2)}) async-start(bf16[8,304,128]{2,1,0:T(8,128)(2,1)} %pad_maximum_fusion), calls=%async_computation.2 | async-start | bytes 1245184 | tf_op jit(solution)/shard_map/all_to_all | solution.py:15
  61.0 2.1 %copy.27 = bf16[2,1024,153]{1,2,0:T(8,128)(2,1)} copy(bf16[2,1024,153]{1,0,2:T(2,128)(2,1)} %param.14) | data formatting | bytes 1253376 | tf_op args[6]
  63.1 8.6 %all-to-all-done.2.got = bf16[8,304,128]{2,1,0:T(8,128)(2,1)} async-done(((bf16[8,304,128]{2,1,0:T(8,128)(2,1)}), bf16[8,304,128]{2,1,0:T(8,128)(2,1)}, u32[]{:S(2)}, u32[]{:S(2)}) %all-to-all-start.2) | async-done | bytes 622624 | tf_op jit(solution)/shard_map/all_to_all | solution.py:15
  71.7 3.2 %shard_map.106 = (bf16[12,56,128]{2,1,0:T(8,128)(2,1)}, bf16[16,1024]{1,0:T(8,128)(2,1)}, f32[16,153]{1,0:T(8,128)}) custom-call(bf16[8,304,128]{2,1,0:T(8,128)(2,1)} %all-to-all-done.2.got, bf16[2,153,1024]{2,1,0:T(8,128)(2,1)} %bitcast.37), custom_call_target="tpu_custom_call" | custom-call | tf_op jit(solution)/shard_map/pallas_call | solution.py:296
  74.9 15.0 %all_to_all.36.got = bf16[12,56,128]{2,1,0:T(8,128)(2,1)S(1)} all-to-all(bf16[12,56,128]{2,1,0:T(8,128)(2,1)} %get-tuple-element.18), channel_id=1, replica_groups=mesh['x'=4,'z'=12,'c'=2,'node'=8] {'z'}, dimensions={0} | all-to-all | bytes 344064 | tf_op jit(solution)/shard_map/all_to_all | solution.py:15
  89.9 13.8 %all_to_all.37.got = f32[8,16,128]{2,1,0:T(8,128)S(1)} all-to-all(f32[8,16,128]{2,1,0:T(8,128)S(1)} %shard_map.107), channel_id=1, replica_groups=mesh['x'=4,'z'=12,'c'=2,'node'=8] {'node'}, dimensions={0} | all-to-all | bytes 131072 | tf_op jit(solution)/shard_map/all_to_all | solution.py:15
  103.8 0.6 shard_map.108
  104.4 4.1 %all-to-all-start.5 = ((bf16[12,16,128]{2,1,0:T(8,128)(2,1)}), bf16[12,16,128]{2,1,0:T(8,128)(2,1)S(1)}, u32[]{:S(2)}, u32[]{:S(2)}) async-start(bf16[12,16,128]{2,1,0:T(8,128)(2,1)} %shard_map.108), calls=%async_computation.5 | async-start | bytes 98304 | tf_op jit(solution)/shard_map/all_to_all | solution.py:15
  108.5 0.0 copy-start.3
  108.6 0.7 copy-done.3
  109.3 0.3 shard_map.109
  109.5 8.8 %all-to-all-done.5.grad = bf16[12,16,128]{2,1,0:T(8,128)(2,1)S(1)} async-done(((bf16[12,16,128]{2,1,0:T(8,128)(2,1)}), bf16[12,16,128]{2,1,0:T(8,128)(2,1)S(1)}, u32[]{:S(2)}, u32[]{:S(2)}) %all-to-all-start.5) | async-done | bytes 49184 | tf_op jit(solution)/shard_map/all_to_all | solution.py:15
  118.3 14.9 %all_to_all.38.got = bf16[8,192,128]{2,1,0:T(8,128)(2,1)S(1)} all-to-all(bf16[8,192,128]{2,1,0:T(8,128)(2,1)S(1)} %shard_map.110), channel_id=1, replica_groups=mesh['x'=4,'z'=12,'c'=2,'node'=8] {'x','c'}, dimensions={0} | all-to-all | bytes 786432 | tf_op jit(solution)/shard_map/all_to_all | solution.py:15
  133.2 0.9 shard_map.111
  (8 shorter events, 0.2 us)
Async XLA Ops:
  0.6 18.0 %copy-start = (bf16[12,8,128,128]{3,2,1,0:T(8,128)(2,1)S(1)}, bf16[12,8,128,128]{3,2,1,0:T(8,128)(2,1)}, u32[]{:S(2)}) copy-start(bf16[12,8,128,128]{3,2,1,0:T(8,128)(2,1)} %param.10) | copy-start | bytes 9437188
  2.2 19.7 %all-to-all-start = ((bf16[8,96,128]{2,1,0:T(8,128)(2,1)}), bf16[8,96,128]{2,1,0:T(8,128)(2,1)S(1)}, u32[]{:S(2)}, u32[]{:S(2)}) async-start(bf16[8,96,128]{2,1,0:T(8,128)(2,1)} %shard_map.103), calls=%async_computation | async-start | bytes 393216 | tf_op jit(solution)/shard_map/all_to_all | solution.py:15
  16.1 0.9 copy-start.1
  17.0 0.7 copy-start.4
  18.7 3.3 %copy-start.2 = (bf16[2,8,1024]{2,1,0:T(8,128)(2,1)S(1)}, bf16[2,8,1024]{2,1,0:T(8,128)(2,1)}, u32[]{:S(2)}) copy-start(bf16[2,8,1024]{2,1,0:T(8,128)(2,1)} %w.1) | copy-start | bytes 98308
  18.7 3.3 %copy-start.5 = (s32[12,4]{0,1:T(4,128)S(1)}, s32[12,4]{0,1:T(4,128)}, u32[]{:S(2)}) copy-start(s32[12,4]{0,1:T(4,128)} %param.13) | copy-start | bytes 580
  53.3 18.4 %all-to-all-start.2 = ((bf16[8,304,128]{2,1,0:T(8,128)(2,1)}), bf16[8,304,128]{2,1,0:T(8,128)(2,1)}, u32[]{:S(2)}, u32[]{:S(2)}) async-start(bf16[8,304,128]{2,1,0:T(8,128)(2,1)} %pad_maximum_fusion), calls=%async_computation.2 | async-start | bytes 1245184 | tf_op jit(solution)/shard_map/all_to_all | solution.py:15
  104.4 13.9 %all-to-all-start.5 = ((bf16[12,16,128]{2,1,0:T(8,128)(2,1)}), bf16[12,16,128]{2,1,0:T(8,128)(2,1)S(1)}, u32[]{:S(2)}, u32[]{:S(2)}) async-start(bf16[12,16,128]{2,1,0:T(8,128)(2,1)} %shard_map.108), calls=%async_computation.5 | async-start | bytes 98304 | tf_op jit(solution)/shard_map/all_to_all | solution.py:15
  108.5 0.7 copy-start.3
